TPU v7x, 32 devices: a whole 2x2x4 slice. The times are simulated.
32 devices in a mesh: group: 2 (over y), gx: 4 (over z), gz: 2 (over x), col: 2 (over core).
Axes of the slice: x: 2, y: 2, z: 4, core: 2. Of those that a mesh axis runs over, the one named last changes fastest.
Arguments:
- features: bfloat16 [32, 64, 16, 256], P(None, 'col', ('group', 'gx'), 'gz'), parts along dimension 2, may hold values from -6 to 6
- labels: int32 [64, 16, 256], P(None, ('group', 'gx'), 'gz'), parts along dimension 1, may hold values from 0 to 3
- grid_index: int32 [64], replicated, may hold values from 0 to 15
- stretch: float32 [16, 9], replicated, may hold values from 0.5 to 2
- tile_filter: float32 [32, 25], replicated, may hold values from -1.25 to 1.25
- wall_filter: float32 [32, 9], replicated, may hold values from -2 to 2
- class_weight: float32 [4, 32], replicated, may hold values from -1 to 1
Outputs:
- grad_features: bfloat16 [32, 64, 16, 256], P(None, 'col', ('group', 'gx'), 'gz'), parts along dimension 2
- grad_tile_filter: float32 [64, 25], P('group'), parts along dimension 0
- grad_wall_filter: float32 [64, 9], P('group'), parts along dimension 0
- grad_class_weight: float32 [8, 32], P('group'), parts along dimension 0
There are 2 independent parts, one for each index of `group`. A program takes and returns all parts, laid end to end along the dimension named above; an argument that names none is the same for every part. Nothing has to cross between parts.
All inputs are finite; a program needn't handle non-finite values.
Results may differ from a plain program's by a relative error of at most 0.0064.
Values may be sent and summed in bfloat16 or wider, within the bound.
No kernel may reach another device: no remote copies, remote signals or barrier semaphores. Data moves between devices by JAX's collectives and lax.ppermute only.
A program may use at most 64 MiB of HBM per device.

v0:
```python
import jax
import jax.numpy as jnp
from jax import lax
from jax.sharding import PartitionSpec as P


def with_halo(value, sides, width):
    for axis, dim in sides:
        size, length = (lax.axis_size(axis), value.shape[dim])
        up = [(i, (i + 1) % size) for i in range(size)]
        down = [(j, i) for i, j in up]
        last = lax.slice_in_dim(value, length - width, length, axis=dim)
        leading = lax.slice_in_dim(value, 0, width, axis=dim)
        before = lax.ppermute(last, axis, up)
        after = lax.ppermute(leading, axis, down)
        value = jnp.concatenate([before, value, after], axis=dim)
    return value


def rim_tiles(field):
    return with_halo(field, (("gx", 2), ("gz", 3)), 2)


def band_table(grid_index, stretch):
    levels = stretch.shape[0]
    onehot = (grid_index[:, None] == jnp.arange(levels, dtype=jnp.int32)[None, :]).astype(
        jnp.float32
    )
    return jnp.dot(onehot, stretch, precision=lax.Precision.HIGHEST)


def wall_forward(smooth_ext, wall_rows, band_rows):
    rows = band_rows.shape[0]
    total = jnp.zeros((smooth_ext.shape[0], rows) + smooth_ext.shape[2:], jnp.float32)
    for k in range(9):
        tap = wall_rows[:, k][:, None] * band_rows[:, k][None, :]
        total = total + tap[:, :, None, None] * smooth_ext[:, k : k + rows].astype(jnp.float32)
    return total


def wall_backward(grad_ext, wall_rows, band_ext, rows):
    total = jnp.zeros((grad_ext.shape[0], rows) + grad_ext.shape[2:], jnp.float32)
    for k in range(9):
        first = 8 - k
        tap = wall_rows[:, k][:, None] * band_ext[first : first + rows, k][None, :]
        total = total + tap[:, :, None, None] * grad_ext[:, first : first + rows].astype(
            jnp.float32
        )
    return total


def shards(features, labels, grid_index, stretch, tile_filter, wall_filter, class_weight):
    chans, half_rows, cells_x, cells_z = features.shape
    all_rows = labels.shape[0]
    classes = class_weight.shape[0]
    volume = all_rows * cells_x * lax.axis_size("gx") * cells_z * lax.axis_size("gz")
    widened = rim_tiles(features)
    smooth = jnp.zeros(features.shape, jnp.float32)
    for i in range(5):
        for j in range(5):
            weight = tile_filter[:, 5 * i + j][:, None, None, None]
            smooth = smooth + weight * widened[:, :, i : i + cells_x, j : j + cells_z].astype(
                jnp.float32
            )
    smoothed = smooth.astype(jnp.bfloat16)
    bands = band_table(grid_index, stretch)
    bands_pad = jnp.pad(bands, ((4, 4), (0, 0)))
    place = lax.axis_index("col")
    share = chans // lax.axis_size("col")
    first_chan = place * share
    pencil = lax.all_to_all(smoothed, "col", split_axis=0, concat_axis=1, tiled=True)
    smooth_ext = jnp.pad(pencil, ((0, 0), (4, 4), (0, 0), (0, 0)))
    wall_rows = lax.dynamic_slice_in_dim(wall_filter, first_chan, share, 0)
    class_rows = lax.dynamic_slice_in_dim(class_weight, first_chan, share, 1)
    wall_out = wall_forward(smooth_ext, wall_rows, bands)
    sig = jax.nn.sigmoid(wall_out)
    hidden = wall_out * sig
    partial_scores = jnp.einsum(
        "kc,cyxz->kyxz", class_rows, hidden, precision=lax.Precision.HIGHEST
    )
    scores = lax.psum(partial_scores, "col")
    targets = (labels[None] == jnp.arange(classes, dtype=jnp.int32)[:, None, None, None]).astype(
        jnp.float32
    )
    errors = scores - targets
    grad_hidden = jnp.einsum("kc,kyxz->cyxz", class_rows, errors, precision=lax.Precision.HIGHEST)
    grad_wall = (grad_hidden * sig * (1.0 + wall_out * (1.0 - sig))).astype(jnp.bfloat16)
    class_part = jnp.einsum("kyxz,cyxz->kc", errors, hidden, precision=lax.Precision.HIGHEST)
    grad_vals = grad_wall.astype(jnp.float32)
    wall_part = jnp.stack(
        [
            jnp.sum(
                grad_vals
                * bands[:, k][None, :, None, None]
                * smooth_ext[:, k : k + all_rows].astype(jnp.float32),
                axis=(1, 2, 3),
            )
            for k in range(9)
        ],
        axis=1,
    )
    grad_ext = jnp.pad(grad_wall, ((0, 0), (4, 4), (0, 0), (0, 0)))
    grad_smooth = wall_backward(grad_ext, wall_rows, bands_pad, all_rows).astype(jnp.bfloat16)
    grad_tile = lax.all_to_all(grad_smooth, "col", split_axis=1, concat_axis=0, tiled=True)
    wall_full = lax.dynamic_update_slice_in_dim(
        jnp.zeros((chans, 9), jnp.float32), wall_part, first_chan, 0
    )
    class_full = lax.dynamic_update_slice_in_dim(
        jnp.zeros((classes, chans), jnp.float32), class_part, first_chan, 1
    )
    grad_widened = rim_tiles(grad_tile)
    grad_tile_vals = grad_tile.astype(jnp.float32)
    grad_field = jnp.zeros(features.shape, jnp.float32)
    tile_terms = []
    for i in range(5):
        for j in range(5):
            weight = tile_filter[:, 5 * i + j][:, None, None, None]
            grad_field = grad_field + weight * grad_widened[
                :, :, 4 - i : 4 - i + cells_x, 4 - j : 4 - j + cells_z
            ].astype(jnp.float32)
            shifted = widened[:, :, i : i + cells_x, j : j + cells_z].astype(jnp.float32)
            tile_terms.append(jnp.sum(shifted * grad_tile_vals, axis=(1, 2, 3)))
    tile_part = jnp.stack(tile_terms, axis=1)
    totals = lax.psum((tile_part, wall_full, class_full), ("gx", "gz", "col"))
    return (
        grad_field.astype(jnp.bfloat16),
        totals[0] / volume,
        totals[1] / volume,
        totals[2] / volume,
    )


def solution(mesh):
    return jax.shard_map(
        shards,
        mesh=mesh,
        in_specs=(
            P(None, "col", ("group", "gx"), "gz"),
            P(None, ("group", "gx"), "gz"),
            P(),
            P(),
            P(),
            P(),
            P(),
        ),
        out_specs=(
            P(None, "col", ("group", "gx"), "gz"),
            P("group", None),
            P("group", None),
            P("group", None),
        ),
        check_vma=False,
    )
```

profile of v0, /device:TPU:0, one launch (start us, length us, event | category | flops | bytes accessed | tf_op | source)
XLA Modules:
  0.0 227.5 jit_solution(17064217156550470900)
XLA Ops:
  7.2 1.1 copy.53
  8.4 3.1 %collective-permute-start = (bf16[32,32,2,128]{3,1,2,0:T(8,128)(2,1)S(1)}, bf16[32,32,2,128]{3,1,2,0:T(8,128)(2,1)S(1)}, u32[]{:S(2)}, u32[]{:S(2)}) collective-permute-start(bf16[32,32,2,128]{3,1,2,0:T(8,128)(2,1)S(1)} %copy.53), channel_id=1, source_target_pairs={{0,4},{4,8},{8,12},{12,0},{1,5},{5,9},{9,13},{13,1},{2,6},{6,10},{... | collective-permute-start | bytes 1572872 | tf_op jit(solution)/shard_map/ppermute | solution.py:14
  11.5 2.1 collective-permute-start.1
  13.6 0.8 fusion.110
  14.6 1.1 dynamic-slice_bitcast_fusion.8
  15.7 0.7 broadcast_multiply_fusion.4
  16.4 0.7 broadcast_multiply_fusion.2
  17.1 0.7 broadcast_multiply_fusion
  18.1 2.5 %slice_reduce_fusion.24 = (f32[32]{0:T(128)S(1)}, f32[32]{0:T(128)S(1)}, f32[32]{0:T(128)S(1)}, f32[32]{0:T(128)S(1)}, f32[32]{0:T(128)S(1)}, /*index=5*/f32[32]...) fusion(f32[32,25]{1,0:T(8,128)} %param.11), kind=kLoop, calls=%fused_computation.296 | loop fusion | bytes 4864 | tf_op jit(solution)/shard_map/slice | solution.py:117
  20.6 5.7 %collective-permute-done = bf16[32,32,2,128]{3,1,2,0:T(8,128)(2,1)S(1)} collective-permute-done((bf16[32,32,2,128]{3,1,2,0:T(8,128)(2,1)S(1)}, bf16[32,32,2,128]{3,1,2,0:T(8,128)(2,1)S(1)}, u32[]{:S(2)}, u32[]{:S(2)}) %collective-permute-start) | collective-permute-done | bytes 524320 | tf_op jit(solution)/shard_map/ppermute | solution.py:14
  26.3 1.4 constant_dynamic-update-slice_fusion.1
  27.7 8.4 %collective-permute-done.1 = bf16[32,32,2,128]{3,1,2,0:T(8,128)(2,1)S(1)} collective-permute-done((bf16[32,32,2,128]{3,1,2,0:T(8,128)(2,1)S(1)}, bf16[32,32,2,128]{3,1,2,0:T(8,128)(2,1)S(1)}, u32[]{:S(2)}, u32[]{:S(2)}) %collective-permute-start.1) | collective-permute-done | bytes 524320 | tf_op jit(solution)/shard_map/ppermute | solution.py:15
  36.1 0.8 copy-done.9
  37.0 1.9 fusion.129
  38.9 3.1 %copy.56 = bf16[32,32,6,2]{1,0,3,2:T(8,128)(2,1)} copy(bf16[32,32,6,2]{3,1,2,0:T(8,128)(2,1)} %get-tuple-element.96) | data formatting | bytes 49152 | tf_op jit(solution)/shard_map/slice | solution.py:12
  42.0 1.5 collective-permute-start.2
  43.5 2.1 copy.58
  46.2 0.8 slice_reduce_fusion.23
  47.0 2.2 copy.57
  49.2 1.4 collective-permute-done.3
  50.6 3.0 %copy.59 = bf16[32,32,6,2]{3,1,2,0:T(8,128)(2,1)} copy(bf16[32,32,6,2]{1,0,3,2:T(8,128)(2,1)} %collective-permute-done.3) | data formatting | bytes 49152 | tf_op jit(solution)/shard_map/ppermute | solution.py:15
  53.5 11.2 %fusion.90 = (bf16[32,32,2,128]{3,1,2,0:T(8,128)(2,1)S(1)}, bf16[32,32,2,128]{3,1,2,0:T(8,128)(2,1)}, bf16[32,32,2,128]{3,1,2,0:T(8,128)(2,1)}) fusion(bf16[32,32,2,128]{3,1,2,0:T(8,128)(2,1)} %copy-done.9, bf16[32,32,2,128]{3,1,2,0:T(8,128)(2,1)} %copy-done.5, bf16[32,32,2,128]{3,1,2,0:T(8,128)(2,1)} %copy-done.7, f32[32]{0:T(128)} %get-tuple-element.81, ...), kind=kLoop, calls=%fused_computation.211 | loop fusion | flops 37486592 | bytes 4770944 | tf_op jit(solution)/shard_map/convert_element_type | solution.py:65
  64.8 4.2 %all_to_all.36 = bf16[32,32,2,128]{3,1,2,0:T(8,128)(2,1)S(1)} all-to-all(bf16[32,32,2,128]{3,1,2,0:T(8,128)(2,1)S(1)} %get-tuple-element.88), channel_id=1, replica_groups=mesh['group'=2,'gx'=4,'gz'=2,'col'=2] {'col'}, dimensions={0} | all-to-all | bytes 1048576 | tf_op jit(solution)/shard_map/all_to_all | solution.py:71
  69.2 2.7 %fusion.88 = (f32[16,64,2,128]{3,0,2,1:T(8,128)S(1)}, f32[16,64,2,128]{3,0,2,1:T(8,128)}) fusion(f32[16,64]{0,1:T(8,128)S(1)} %get-tuple-element.138, f32[16,64]{0,1:T(8,128)S(1)} %get-tuple-element.140, f32[16,64]{0,1:T(8,128)S(1)} %get-tuple-element.134, f32[16,64]{0,1:T(8,128)S(1)} %get-tuple-element.142, bf16[16,64,2,128]{3,0,2,1:T(8,128)(2,1)S(1)} %bitcast.143, ...), kind=kLoop, calls=%fused_computation.209 | loop fusion | flops 7864320 | bytes 2658304 | tf_op jit(solution)/shard_map/mul | solution.py:77
  72.0 1.3 fusion.113
  73.4 18.9 %all-reduce.6.cloned.1.call-done = f32[4,64,2,128]{3,0,2,1:T(4,128)} async-done(((f32[4,64,2,128]{3,0,2,1:T(4,128)}), f32[4,64,2,128]{3,0,2,1:T(4,128)}) %all-reduce.6.cloned.1.call-update) | async-done | bytes 262160 | tf_op jit(solution)/shard_map/psum | solution.py:81
  92.3 4.8 %fusion.42 = (f32[16]{0:T(128)S(1)}, f32[16]{0:T(128)S(1)}, f32[16]{0:T(128)S(1)}, f32[16]{0:T(128)S(1)}, f32[16]{0:T(128)S(1)}, /*index=5*/f32[16]{0:T(128)S(1)...) fusion(f32[64]{0:T(128)} %copy-done.40, ...), kind=kOutput, calls=%fused_computation.162 | convolution fusion | flops 24838000 | bytes 2952516 | tf_op jit(solution)/shard_map/kc,kyxz->cyxz/dot_general | solution.py:86
  97.2 1.7 fusion.48
  99.0 4.3 %all_to_all.37 = bf16[16,64,2,128]{3,0,2,1:T(8,128)(2,1)S(1)} all-to-all(bf16[16,64,2,128]{3,0,2,1:T(8,128)(2,1)S(1)} %fusion.48), channel_id=1, replica_groups=mesh['group'=2,'gx'=4,'gz'=2,'col'=2] {'col'}, dimensions={1} | all-to-all | bytes 1048576 | tf_op jit(solution)/shard_map/all_to_all | solution.py:104
  103.5 3.9 %fusion.85 = (f32[32]{0:T(128)S(1)}, f32[32]{0:T(128)S(1)}, f32[32]{0:T(128)S(1)}, f32[32]{0:T(128)S(1)}, f32[32]{0:T(128)S(1)}, /*index=5*/f32[32]{0:T(128)S(1)}, f32[32]{0:T(128)S(1)}, f32[32]{0:T(128)S(1)}, f32[32]{0:T(128)S(1)}) fusion(bf16[2,16,32,2,128]{4,2,3,1,0:T(8,128)(2,1)S(1)} %copy.64, bf16[32,32,6,2]{3,1,2,0:T(8,128)(2,1)S(1)} %copy-done.3, ...), kind=kLoop, calls=%fused_computation.205 | loop fusion | flops 14417632 | bytes 2122880 | tf_op jit(solution)/shard_map/reduce_sum | solution.py:122
  107.5 3.8 %fusion.82 = (f32[32]{0:T(128)S(1)}, f32[32]{0:T(128)S(1)}, f32[32]{0:T(128)S(1)}, f32[32]{0:T(128)S(1)}, f32[32]{0:T(128)S(1)}, /*index=5*/f32[32]{0:T(128)S(1)}, f32[32]{0:T(128)S(1)}, f32[32]{0:T(128)S(1)}, f32[32]{0:T(128)S(1)}) fusion(bf16[2,16,32,2,128]{4,2,3,1,0:T(8,128)(2,1)S(1)} %copy.64, ...), kind=kLoop, calls=%fused_computation.202 | loop fusion | flops 14417632 | bytes 2122880 | tf_op jit(solution)/shard_map/reduce_sum | solution.py:122
  111.2 1.8 collective-permute-start.4
  113.0 2.1 collective-permute-start.5
  115.1 1.1 fusion.84
  116.2 1.4 convolution_bitcast_fusion
  118.2 72.8 %all-reduce.3 = (f32[32,25]{0,1:T(8,128)S(1)}, f32[32,9]{0,1:T(8,128)S(1)}, f32[4,32]{1,0:T(4,128)S(1)}) all-reduce(f32[32,25]{0,1:T(8,128)S(1)} %stack.133, f32[32,9]{0,1:T(8,128)S(1)} %dynamic_update_slice.6, f32[4,32]{1,0:T(4,128)S(1)} %dynamic_update_slice.7), channel_id=1, replica_groups=mesh['group'=2,'gx'=4,'gz'=2,'col'=2] {'gx','gz','col'}, use_global_device_ids=true, to_apply=%region_26.27 | all-reduce | flops 1216 | bytes 9728 | tf_op jit(solution)/shard_map/psum | solution.py:124
  191.6 0.8 copy-done.12
  192.4 1.4 pad_maximum_fusion.1
  193.7 2.4 %fusion.128 = (bf16[32,32,6,2]{3,1,2,0:T(8,128)(2,1)}, bf16[32,32,6,2]{3,1,2,0:T(8,128)(2,1)}) fusion(bf16[32,32,6,128]{3,1,2,0:T(8,128)(2,1)S(1)} %pad_maximum_fusion.1), kind=kLoop, calls=%fused_computation.344 | loop fusion | bytes 98304 | tf_op jit(solution)/shard_map/slice | solution.py:13
  196.2 2.6 %copy.75 = bf16[32,32,6,2]{1,0,3,2:T(8,128)(2,1)S(1)} copy(bf16[32,32,6,2]{3,1,2,0:T(8,128)(2,1)} %get-tuple-element.93) | data formatting | bytes 49152
  198.8 2.5 %copy.76 = bf16[32,32,6,2]{1,0,3,2:T(8,128)(2,1)S(1)} copy(bf16[32,32,6,2]{3,1,2,0:T(8,128)(2,1)} %get-tuple-element.94) | data formatting | bytes 49152
  201.4 2.1 collective-permute-start.7
  204.0 0.7 copy.72
  204.7 1.4 copy.66
  206.1 2.2 copy.68
  208.5 4.3 %pad_maximum_fusion = (bf16[32,32,6,130]{3,1,2,0:T(8,128)(2,1)S(1)}, bf16[32,32,6,130]{3,1,2,0:T(8,128)(2,1)S(1)}) fusion(bf16[32,32,6,2]{3,1,2,0:T(8,128)(2,1)S(1)} %copy.66, bf16[32,32,2,128]{3,1,2,0:T(8,128)(2,1)} %collective-permute-done.5, bf16[32,32,2,128]{3,1,2,0:T(8,128)(2,1)S(1)} %bitcast.139, bf16[32,32,2,128]{3,1,2,0:T(8,128)(2,1)S(1)} %copy-done.13, ...), kind=kLoop, calls=%fused_computation.72 | loop fusion | flops 12779520 | bytes 4816896 | tf_op jit(solution)/shard_map/concatenate | solution.py:16
  212.9 6.4 %fusion.89 = bf16[32,32,2,128]{3,1,2,0:T(8,128)(2,1)S(1)} fusion(bf16[32,32,2,128]{3,1,2,0:T(8,128)(2,1)S(1)} %copy-done.13, bf16[32,32,2,128]{3,1,2,0:T(8,128)(2,1)S(1)} %bitcast.140, bf16[32,32,2,128]{3,1,2,0:T(8,128)(2,1)} %collective-permute-done.5, bf16[32,32,6,130]{3,1,2,0:T(8,128)(2,1)S(1)} %get-tuple-element.92, ...), kind=kLoop, calls=%fused_computation.210 | loop fusion | flops 20185088 | bytes 12586112 | tf_op jit(solution)/shard_map/convert_element_type | solution.py:126
  219.3 1.3 copy.71
  (121 shorter events, 3.5 us)
Async XLA Ops:
  7.2 6.4 %copy-start = (f32[16,9]{1,0:T(8,128)S(1)}, f32[16,9]{1,0:T(8,128)}, u32[]{:S(2)}) copy-start(f32[16,9]{1,0:T(8,128)} %param.10) | copy-start | bytes 1732
  7.2 85.1 %all-reduce.6.cloned.1.call-start = ((), (), s32[]{:S(2)}) async-start(), calls=%async_computation.2 | async-start | bytes 524288 | tf_op jit(solution)/shard_map/psum | solution.py:81
  8.4 27.7 %copy-start.5 = (bf16[32,32,2,128]{3,1,2,0:T(8,128)(2,1)}, bf16[32,32,2,128]{3,1,2,0:T(8,128)(2,1)S(1)}, u32[]{:S(2)}) copy-start(bf16[32,32,2,128]{3,1,2,0:T(8,128)(2,1)S(1)} %copy.53) | copy-start | bytes 1572868
  8.4 17.9 %collective-permute-start = (bf16[32,32,2,128]{3,1,2,0:T(8,128)(2,1)S(1)}, bf16[32,32,2,128]{3,1,2,0:T(8,128)(2,1)S(1)}, u32[]{:S(2)}, u32[]{:S(2)}) collective-permute-start(bf16[32,32,2,128]{3,1,2,0:T(8,128)(2,1)S(1)} %copy.53), channel_id=1, source_target_pairs={{0,4},{4,8},{8,12},{12,0},{1,5},{5,9},{9,13},{13,1},{2,6},{6,10},{... | collective-permute-start | bytes 1572872 | tf_op jit(solution)/shard_map/ppermute | solution.py:14
  11.5 24.6 %collective-permute-start.1 = (bf16[32,32,2,128]{3,1,2,0:T(8,128)(2,1)S(1)}, bf16[32,32,2,128]{3,1,2,0:T(8,128)(2,1)S(1)}, u32[]{:S(2)}, u32[]{:S(2)}) collective-permute-start(bf16[32,32,2,128]{3,1,2,0:T(8,128)(2,1)S(1)} %copy.53), channel_id=1, source_target_pairs={{4,0},{8,4},{12,8},{0,12},{5,1},{9,5},{13,9},{1,13},{6,2},{10,6},{... | collective-permute-start | bytes 1572872 | tf_op jit(solution)/shard_map/ppermute | solution.py:15
  14.6 6.0 %copy-start.48 = (f32[64]{0:T(128)}, f32[64]{0:T(128)S(1)}, u32[]{:S(2)}) copy-start(f32[64]{0:T(128)S(1)} %get-tuple-element.113) | copy-start | bytes 772
  26.3 9.8 %copy-start.7 = (bf16[32,32,2,128]{3,1,2,0:T(8,128)(2,1)}, bf16[32,32,2,128]{3,1,2,0:T(8,128)(2,1)S(1)}, u32[]{:S(2)}) copy-start(bf16[32,32,2,128]{3,1,2,0:T(8,128)(2,1)S(1)} %collective-permute-done) | copy-start | bytes 1572868
  38.9 7.3 %copy-start.4 = (f32[32,25]{1,0:T(8,128)S(1)}, f32[32,25]{1,0:T(8,128)}, u32[]{:S(2)}) copy-start(f32[32,25]{1,0:T(8,128)} %param.11) | copy-start | bytes 9604
  42.0 5.0 %collective-permute-start.2 = (bf16[32,32,6,2]{1,0,3,2:T(8,128)(2,1)}, bf16[32,32,6,2]{1,0,3,2:T(8,128)(2,1)}, u32[]{:S(2)}, u32[]{:S(2)}) collective-permute-start(bf16[32,32,6,2]{1,0,3,2:T(8,128)(2,1)} %copy.56), channel_id=1, source_target_pairs={{0,2},{2,0},{1,3},{3,1},{4,6},{6,4},{5,7},{7,5},{8,10},{10,8},{9,1... | collective-permute-start | bytes 73736 | tf_op jit(solution)/shard_map/ppermute | solution.py:14
  45.6 4.9 %collective-permute-start.3 = (bf16[32,32,6,2]{1,0,3,2:T(8,128)(2,1)}, bf16[32,32,6,2]{1,0,3,2:T(8,128)(2,1)}, u32[]{:S(2)}, u32[]{:S(2)}) collective-permute-start(bf16[32,32,6,2]{1,0,3,2:T(8,128)(2,1)} %copy.58), channel_id=1, source_target_pairs={{2,0},{0,2},{3,1},{1,3},{6,4},{4,6},{7,5},{5,7},{10,8},{8,10},{11,... | collective-permute-start | bytes 73736 | tf_op jit(solution)/shard_map/ppermute | solution.py:15
  49.2 15.6 %copy-start.1 = (bf16[32,32,6,2]{3,1,2,0:T(8,128)(2,1)}, bf16[32,32,6,2]{3,1,2,0:T(8,128)(2,1)S(1)}, u32[]{:S(2)}) copy-start(bf16[32,32,6,2]{3,1,2,0:T(8,128)(2,1)S(1)} %copy.57) | copy-start | bytes 73732
  64.7 7.2 %copy-start.39 = (f32[4,32]{1,0:T(4,128)S(1)}, f32[4,32]{1,0:T(4,128)}, u32[]{:S(2)}) copy-start(f32[4,32]{1,0:T(4,128)} %param.13) | copy-start | bytes 1540
  92.3 4.9 %copy-start.17 = (f32[16,64]{0,1:T(8,128)S(1)}, f32[16,64]{0,1:T(8,128)}, u32[]{:S(2)}) copy-start(f32[16,64]{0,1:T(8,128)} %get-tuple-element.129) | copy-start | bytes 12292
  92.3 4.9 %copy-start.18 = (f32[16,64]{0,1:T(8,128)S(1)}, f32[16,64]{0,1:T(8,128)}, u32[]{:S(2)}) copy-start(f32[16,64]{0,1:T(8,128)} %get-tuple-element.145) | copy-start | bytes 12292
  92.3 4.9 %copy-start.19 = (f32[16,64]{0,1:T(8,128)S(1)}, f32[16,64]{0,1:T(8,128)}, u32[]{:S(2)}) copy-start(f32[16,64]{0,1:T(8,128)} %get-tuple-element.133) | copy-start | bytes 12292
  92.3 4.9 %copy-start.20 = (f32[16,64]{0,1:T(8,128)S(1)}, f32[16,64]{0,1:T(8,128)}, u32[]{:S(2)}) copy-start(f32[16,64]{0,1:T(8,128)} %get-tuple-element.143) | copy-start | bytes 12292
  92.3 4.9 %copy-start.21 = (f32[16,64]{0,1:T(8,128)S(1)}, f32[16,64]{0,1:T(8,128)}, u32[]{:S(2)}) copy-start(f32[16,64]{0,1:T(8,128)} %get-tuple-element.137) | copy-start | bytes 12292
  92.3 4.9 %copy-start.22 = (f32[16,64]{0,1:T(8,128)S(1)}, f32[16,64]{0,1:T(8,128)}, u32[]{:S(2)}) copy-start(f32[16,64]{0,1:T(8,128)} %get-tuple-element.141) | copy-start | bytes 12292
  97.1 6.3 %copy-start.3 = (bf16[32,32,6,2]{3,1,2,0:T(8,128)(2,1)S(1)}, bf16[32,32,6,2]{3,1,2,0:T(8,128)(2,1)}, u32[]{:S(2)}) copy-start(bf16[32,32,6,2]{3,1,2,0:T(8,128)(2,1)} %copy.59) | copy-start | bytes 73732
  98.9 8.5 %copy-start.2 = (bf16[32,32,6,2]{3,1,2,0:T(8,128)(2,1)S(1)}, bf16[32,32,6,2]{3,1,2,0:T(8,128)(2,1)}, u32[]{:S(2)}) copy-start(bf16[32,32,6,2]{3,1,2,0:T(8,128)(2,1)} %copy-done.1) | copy-start | bytes 73732
  103.5 11.6 %copy-start.6 = (bf16[32,32,2,128]{3,1,2,0:T(8,128)(2,1)S(1)}, bf16[32,32,2,128]{3,1,2,0:T(8,128)(2,1)}, u32[]{:S(2)}) copy-start(bf16[32,32,2,128]{3,1,2,0:T(8,128)(2,1)} %copy-done.5) | copy-start | bytes 1572868
  103.5 11.6 %copy-start.8 = (bf16[32,32,2,128]{3,1,2,0:T(8,128)(2,1)S(1)}, bf16[32,32,2,128]{3,1,2,0:T(8,128)(2,1)}, u32[]{:S(2)}) copy-start(bf16[32,32,2,128]{3,1,2,0:T(8,128)(2,1)} %copy-done.7) | copy-start | bytes 1572868
  103.5 11.6 %copy-start.10 = (bf16[32,32,2,128]{3,1,2,0:T(8,128)(2,1)S(1)}, bf16[32,32,2,128]{3,1,2,0:T(8,128)(2,1)}, u32[]{:S(2)}) copy-start(bf16[32,32,2,128]{3,1,2,0:T(8,128)(2,1)} %copy-done.9) | copy-start | bytes 1572868
  103.5 11.6 %copy-start.11 = (bf16[32,32,2,128]{3,2,1,0:T(2,128)(2,1)S(1)}, bf16[32,32,2,128]{3,2,1,0:T(2,128)(2,1)}, u32[]{:S(2)}) copy-start(bf16[32,32,2,128]{3,2,1,0:T(2,128)(2,1)} %param.7) | copy-start | bytes 1572868
  103.5 11.6 %copy-start.14 = (bf16[32,32,2,128]{3,1,2,0:T(8,128)(2,1)S(1)}, bf16[32,32,2,128]{3,1,2,0:T(8,128)(2,1)}, u32[]{:S(2)}) copy-start(bf16[32,32,2,128]{3,1,2,0:T(8,128)(2,1)} %get-tuple-element.89) | copy-start | bytes 1572868
  103.5 11.6 %copy-start.15 = (bf16[32,32,2,128]{3,1,2,0:T(8,128)(2,1)S(1)}, bf16[32,32,2,128]{3,1,2,0:T(8,128)(2,1)}, u32[]{:S(2)}) copy-start(bf16[32,32,2,128]{3,1,2,0:T(8,128)(2,1)} %get-tuple-element.90) | copy-start | bytes 1572868
  107.4 8.8 %copy-start.16 = (f32[4,64,2,128]{3,0,2,1:T(4,128)S(1)}, f32[4,64,2,128]{3,0,2,1:T(4,128)}, u32[]{:S(2)}) copy-start(f32[4,64,2,128]{3,0,2,1:T(4,128)} %all-reduce.6.cloned.1.call-done) | copy-start | bytes 786436
  107.4 8.8 %copy-start.23 = (s32[64,2,128]{2,1,0:T(2,128)S(1)}, s32[64,2,128]{2,1,0:T(2,128)}, u32[]{:S(2)}) copy-start(s32[64,2,128]{2,1,0:T(2,128)} %param.8) | copy-start | bytes 196612
  111.2 80.3 %collective-permute-start.4 = (bf16[32,32,2,128]{3,1,2,0:T(8,128)(2,1)S(1)}, bf16[32,32,2,128]{3,1,2,0:T(8,128)(2,1)S(1)}, u32[]{:S(2)}, u32[]{:S(2)}) collective-permute-start(bf16[32,32,2,128]{3,1,2,0:T(8,128)(2,1)S(1)} %bitcast.136), channel_id=1, source_target_pairs={{0,4},{4,8},{8,12},{12,0},{1,5},{5,9},{9,13},{13,1},{2,6},{6,10},{... | collective-permute-start | bytes 1572872 | tf_op jit(solution)/shard_map/ppermute | solution.py:14
  113.0 79.4 %collective-permute-start.5 = (bf16[32,32,2,128]{3,1,2,0:T(8,128)(2,1)S(1)}, bf16[32,32,2,128]{3,1,2,0:T(8,128)(2,1)}, u32[]{:S(2)}, u32[]{:S(2)}) collective-permute-start(bf16[32,32,2,128]{3,1,2,0:T(8,128)(2,1)S(1)} %bitcast.137), channel_id=1, source_target_pairs={{4,0},{8,4},{12,8},{0,12},{5,1},{9,5},{13,9},{1,13},{6,2},{10,6},{... | collective-permute-start | bytes 1572872 | tf_op jit(solution)/shard_map/ppermute | solution.py:15
  196.2 12.2 %copy-start.13 = (bf16[32,32,2,128]{3,1,2,0:T(8,128)(2,1)S(1)}, bf16[32,32,2,128]{3,1,2,0:T(8,128)(2,1)}, u32[]{:S(2)}) copy-start(bf16[32,32,2,128]{3,1,2,0:T(8,128)(2,1)} %copy-done.12) | copy-start | bytes 1572868
  198.8 6.0 %collective-permute-start.6 = (bf16[32,32,6,2]{1,0,3,2:T(8,128)(2,1)S(1)}, bf16[32,32,6,2]{1,0,3,2:T(8,128)(2,1)S(1)}, u32[]{:S(2)}, u32[]{:S(2)}) collective-permute-start(bf16[32,32,6,2]{1,0,3,2:T(8,128)(2,1)S(1)} %copy.75), channel_id=1, source_target_pairs={{2,0},{0,2},{3,1},{1,3},{6,4},{4,6},{7,5},{5,7},{10,8},{8,10},{11,... | collective-permute-start | bytes 73736 | tf_op jit(solution)/shard_map/ppermute | solution.py:15
  201.4 4.7 %collective-permute-start.7 = (bf16[32,32,6,2]{1,0,3,2:T(8,128)(2,1)S(1)}, bf16[32,32,6,2]{1,0,3,2:T(8,128)(2,1)S(1)}, u32[]{:S(2)}, u32[]{:S(2)}) collective-permute-start(bf16[32,32,6,2]{1,0,3,2:T(8,128)(2,1)S(1)} %copy.76), channel_id=1, source_target_pairs={{0,2},{2,0},{1,3},{3,1},{4,6},{6,4},{5,7},{7,5},{8,10},{10,8},{9,1... | collective-permute-start | bytes 73736 | tf_op jit(solution)/shard_map/ppermute | solution.py:14
  208.3 4.4 %copy-start.24 = (f32[32]{0:T(128)S(1)}, f32[32]{0:T(128)}, u32[]{:S(2)}) copy-start(f32[32]{0:T(128)} %get-tuple-element.64) | copy-start | bytes 388
  208.3 4.4 %copy-start.25 = (f32[32]{0:T(128)S(1)}, f32[32]{0:T(128)}, u32[]{:S(2)}) copy-start(f32[32]{0:T(128)} %get-tuple-element.65) | copy-start | bytes 388
  208.3 4.4 %copy-start.26 = (f32[32]{0:T(128)S(1)}, f32[32]{0:T(128)}, u32[]{:S(2)}) copy-start(f32[32]{0:T(128)} %get-tuple-element.66) | copy-start | bytes 388
  208.3 4.4 %copy-start.27 = (f32[32]{0:T(128)S(1)}, f32[32]{0:T(128)}, u32[]{:S(2)}) copy-start(f32[32]{0:T(128)} %get-tuple-element.67) | copy-start | bytes 388
  208.4 4.4 %copy-start.28 = (f32[32]{0:T(128)S(1)}, f32[32]{0:T(128)}, u32[]{:S(2)}) copy-start(f32[32]{0:T(128)} %get-tuple-element.68) | copy-start | bytes 388
  208.4 4.4 %copy-start.29 = (f32[32]{0:T(128)S(1)}, f32[32]{0:T(128)}, u32[]{:S(2)}) copy-start(f32[32]{0:T(128)} %get-tuple-element.69) | copy-start | bytes 388
  208.4 4.4 %copy-start.30 = (f32[32]{0:T(128)S(1)}, f32[32]{0:T(128)}, u32[]{:S(2)}) copy-start(f32[32]{0:T(128)} %get-tuple-element.70) | copy-start | bytes 388
  208.4 4.4 %copy-start.31 = (f32[32]{0:T(128)S(1)}, f32[32]{0:T(128)}, u32[]{:S(2)}) copy-start(f32[32]{0:T(128)} %get-tuple-element.71) | copy-start | bytes 388
  208.4 4.4 %copy-start.32 = (f32[32]{0:T(128)S(1)}, f32[32]{0:T(128)}, u32[]{:S(2)}) copy-start(f32[32]{0:T(128)} %get-tuple-element.72) | copy-start | bytes 388
  208.4 4.4 %copy-start.33 = (f32[32]{0:T(128)S(1)}, f32[32]{0:T(128)}, u32[]{:S(2)}) copy-start(f32[32]{0:T(128)} %get-tuple-element.73) | copy-start | bytes 388
  208.4 4.4 %copy-start.34 = (f32[32]{0:T(128)S(1)}, f32[32]{0:T(128)}, u32[]{:S(2)}) copy-start(f32[32]{0:T(128)} %get-tuple-element.74) | copy-start | bytes 388
  208.4 4.4 %copy-start.35 = (f32[32]{0:T(128)S(1)}, f32[32]{0:T(128)}, u32[]{:S(2)}) copy-start(f32[32]{0:T(128)} %get-tuple-element.75) | copy-start | bytes 388
  208.4 4.4 %copy-start.36 = (f32[32]{0:T(128)S(1)}, f32[32]{0:T(128)}, u32[]{:S(2)}) copy-start(f32[32]{0:T(128)} %get-tuple-element.76) | copy-start | bytes 388
  208.4 4.4 %copy-start.37 = (f32[32]{0:T(128)S(1)}, f32[32]{0:T(128)}, u32[]{:S(2)}) copy-start(f32[32]{0:T(128)} %get-tuple-element.81) | copy-start | bytes 388
  208.5 4.4 %copy-start.38 = (f32[32]{0:T(128)S(1)}, f32[32]{0:T(128)}, u32[]{:S(2)}) copy-start(f32[32]{0:T(128)} %get-tuple-element.82) | copy-start | bytes 388
  (10 other events, 28.0 us)
Sparse Core Ops, SparseCore 0:
  73.5 18.7 all-reduce.5
where the time goes:
time: 228 us; the launch traced here: 227 us
  blocking collectives  81.2 us (36%)
  other arithmetic  39.9 us (18%)
  local copies, waits for them, and re-layouts  35.5 us (16%)
  waiting for transfers between devices  34.4 us (15%)
  between operations  14.8 us (6%)
  starting transfers between devices  13.2 us (6%)
  matrix products  8.43 us (4%)
    psum x1, blocking collectives, shards(): totals = lax.psum((tile_part, wall_full, class_full), ('gx', 'gz', 'col'))  72.8 us
    psum x1, waiting for transfers between devices, shards(): scores = lax.psum(partial_scores, 'col')  18.9 us
    unnamed x105, local copies, waits for them, and re-layouts  11.5 us
    convert_element_type x1, other arithmetic, shards(): smoothed = smooth.astype(jnp.bfloat16)  11.2 us
    ppermute x4, waiting for transfers between devices, with_halo(): after = lax.ppermute(leading, axis, down)  9.77 us
    reduce_sum x3, other arithmetic, shards(): tile_terms.append(jnp.sum(shifted * grad_tile_vals, axis=(1, 2, 3)))  8.73 us
    ppermute x4, starting transfers between devices, with_halo(): before = lax.ppermute(last, axis, up)  8.43 us
    slice x3, local copies, waits for them, and re-layouts, with_halo(): leading = lax.slice_in_dim(value, 0, width, axis=dim)  6.44 us
  transfers between devices with their start and end apart: 9, of which 4 were waited for; matrix products, arithmetic and copies ran while one was open for 10% of the time, Pallas kernels for 0%

commit v1 on v0

--- a/solution.py
+++ b/solution.py
@@ -1,7 +1,557 @@
+import functools
+
 import jax
 import jax.numpy as jnp
 from jax import lax
+from jax.experimental import pallas as pl
+from jax.experimental.pallas import tpu as pltpu
 from jax.sharding import PartitionSpec as P
+
+LANES = 128
+TAPS = 5
+REACH = 2
+EDGE = 4
+WALL = 9
+WALL_HALO = 8
+ROW_WALL = TAPS * TAPS
+ROW_CLASS = ROW_WALL + WALL
+CENTRE = ROW_WALL // 2
+F32, BF16 = jnp.float32, jnp.bfloat16
+
+
+class Plan:
+    def __init__(self, ring, chans, rows, cells_x, cells_z, classes):
+        self.ring, self.chans, self.rows, self.cells_x = ring, chans, rows, cells_x
+        self.classes = classes
+        self.window = cells_z // ring
+        self.block = self.window + 2 * EDGE
+        self.per = LANES // self.block
+        self.slots = chans + 1
+        self.groups = self.slots // self.per
+        self.xs = ring * cells_x
+        self.packs = chans // ring
+        self.reach_rows = rows + 2 * (WALL_HALO // 2)
+        self.edge_slots = LANES // (2 * EDGE)
+        self.edge_groups = -(-self.slots // self.edge_slots)
+        self.table_rows = -(-(ROW_CLASS + classes) // 8) * 8
+
+
+def fits(ring, gz, col, chans, rows, cells_x, cells_z, classes):
+    if cells_z != LANES or cells_x != 2 or col != 2 or ring < 2 or ring > 4 or LANES % ring:
+        return False
+    block = LANES // ring + 2 * EDGE
+    per = LANES // block
+    return (chans + 1) % per == 0 and chans % ring == 0 and rows % 16 == 0 and ring * cells_x >= TAPS
+
+
+def vmem(count):
+    return [pl.BlockSpec(memory_space=pltpu.VMEM)] * count
+
+
+def call(body, outs, args, scratch=()):
+    return pl.pallas_call(
+        body,
+        out_shape=outs,
+        in_specs=vmem(len(args)),
+        out_specs=vmem(len(outs)),
+        scratch_shapes=list(scratch),
+        compiler_params=pltpu.CompilerParams(vmem_limit_bytes=40 * 2**20),
+    )(*args)
+
+
+def lane_of(rows):
+    return lax.broadcasted_iota(jnp.int32, (rows, LANES), 1)
+
+
+def edge_body(p, field, labels, out):
+    core = lax.axis_index("col")
+    tall = p.rows * p.cells_x
+    lane = lane_of(tall)
+
+    def group(g, count, fetch):
+        total = jnp.zeros((tall, LANES), F32)
+        for e in range(count):
+            moved = pltpu.roll(fetch(g * p.edge_slots + e), (2 * EDGE * e + EDGE) % LANES, 1)
+            total = jnp.where(lane // (2 * EDGE) == e, moved, total)
+        out[g] = total.astype(BF16)
+
+    def step(g, carry):
+        group(g, p.edge_slots, lambda c: field[c].astype(F32))
+        return carry
+
+    full = p.chans // p.edge_slots
+    lax.fori_loop(0, full, step, 0)
+    own = labels[pl.ds(pl.multiple_of(core * tall, 8), tall), :].astype(F32)
+    group(full, p.slots - full * p.edge_slots, lambda c: own)
+
+
+def pack_body(p, cuts, field, labels, left, right, *refs):
+    outs, stage = refs[:-1], refs[-1]
+    ring = p.ring
+    me, core = lax.axis_index("gx"), lax.axis_index("col")
+    tall = p.rows * p.cells_x
+    lane = lane_of(tall)
+    takes = [lax.rem(me + d, ring) for d in range(ring)]
+    fixes = [
+        ((lane >= LANES - EDGE) & (k == 0)) | ((lane < EDGE) & (k == ring - 1)) for k in takes
+    ]
+    older = lane % (2 * EDGE) < EDGE
+
+    def edges(c):
+        g, e = c // p.edge_slots, c % p.edge_slots
+        both = jnp.where(older, left[g].astype(F32), right[g].astype(F32))
+        return pltpu.roll(both, LANES - EDGE - 2 * EDGE * e, 1)
+
+    def group(cg, fetch, chunk, first):
+        values = [fetch(cg * p.per + b) for b in range(p.per)]
+        rims = [edges(cg * p.per + b) for b in range(p.per)]
+        for d in range(ring):
+            total = jnp.zeros((tall, LANES), F32)
+            for b in range(p.per):
+                shift = lax.rem(2 * LANES + p.block * b + EDGE - p.window * takes[d], LANES)
+                moved = pltpu.roll(jnp.where(fixes[d], rims[b], values[b]), shift, 1)
+                total = jnp.where(lane // p.block == b, moved, total)
+            stage[d] = total
+            for xp in range(p.cells_x):
+                outs[chunk * ring + d][cg - first, xp] = stage[
+                    d, pl.ds(xp, p.rows, stride=p.cells_x), :
+                ].astype(BF16)
+
+    own = labels[pl.ds(pl.multiple_of(core * tall, 8), tall), :].astype(F32)
+    for chunk, (first, last) in enumerate(cuts):
+        tail = last == p.groups
+
+        def step(cg, carry, chunk=chunk, first=first):
+            group(cg, lambda c: field[c].astype(F32), chunk, first)
+            return carry
+
+        lax.fori_loop(first, last - 1 if tail else last, step, 0)
+        if tail:
+            group(last - 1, lambda c: field[c].astype(F32) if c < p.chans else own, chunk, first)
+
+
+def cell_of(p, d, xp):
+    return (xp - p.cells_x * d) % p.xs
+
+
+def conv_body(p, first, count, table, *refs):
+    pieces, smooth, rim = refs[: p.ring], refs[p.ring], refs[p.ring + 1]
+    core = lax.axis_index("col")
+
+    def step(g, carry):
+        weights = [table[first + g, pl.ds(t, 1), :] for t in range(ROW_WALL)]
+        tops, lows = {}, {}
+        for part in range(p.rows // 16):
+            cells = {}
+            for d in range(p.ring):
+                for xp in range(p.cells_x):
+                    cells[cell_of(p, d, xp)] = pieces[d][g, xp, pl.ds(16 * part, 16), :].astype(F32)
+            for x in range(p.xs):
+                total = None
+                for j in range(TAPS):
+                    line = None
+                    for i in range(TAPS):
+                        term = weights[TAPS * i + j] * cells[(x + i - REACH) % p.xs]
+                        line = term if line is None else line + term
+                    if j != REACH:
+                        line = pltpu.roll(line, (REACH - j) % LANES, 1)
+                    total = line if total is None else total + line
+                smooth[g, x, pl.ds(16 * part, 16), :] = total.astype(BF16)
+                if part == 0:
+                    tops[x] = total[:8]
+                if part == p.rows // 16 - 1:
+                    lows[x] = total[8:]
+        for pair in range(p.xs // 2):
+            top = jnp.concatenate([tops[2 * pair], tops[2 * pair + 1]], axis=0)
+            low = jnp.concatenate([lows[2 * pair], lows[2 * pair + 1]], axis=0)
+            rim[g, pair] = jnp.where(core == 0, low, top).astype(BF16)
+        return carry
+
+    lax.fori_loop(0, count, step, 0)
+
+
+def fill_column(p, core, smooth, rim, g, x, store):
+    store(WALL_HALO, p.rows, smooth[g, x].astype(F32))
+    near = rim[g, x // 2].astype(F32)[8 * (x % 2) : 8 * (x % 2) + 8]
+    store(0, WALL_HALO, jnp.where(core == 0, 0.0, near))
+    store(WALL_HALO + p.rows, WALL_HALO, jnp.where(core == 0, near, 0.0))
+
+
+def own_lanes(p, rows):
+    lane = lane_of(rows)
+    place = lane % p.block
+    return (place >= EDGE) & (place < EDGE + p.window) & (lane < p.per * p.block)
+
+
+def spread(p, value, lane):
+    total = value
+    for b in range(p.per - 1):
+        moved = pltpu.roll(value, LANES - p.block * (p.per - 1 - b), 1)
+        total = jnp.where(lane // p.block == b, moved, total)
+    return total
+
+
+def wall_body(p, cuts, table, bands, *refs):
+    count = len(cuts)
+    smooths, rims = refs[:count], refs[count : 2 * count]
+    refs = refs[2 * count :]
+    results = refs[: p.ring]
+    grad_smooth, grad_wall, hidden_out, errors_out = refs[p.ring : p.ring + 4]
+    column, hidden, slope, score, wall, field = refs[p.ring + 4 :]
+    core, me = lax.axis_index("col"), lax.axis_index("gx")
+    blocks = p.reach_rows // 8
+    lane = lane_of(8)
+    half = WALL // 2
+    all_rows = 2 * p.rows
+
+    for chunk, (first, last) in enumerate(cuts):
+
+        def fill(g, carry, chunk=chunk, first=first):
+            for x in range(p.xs):
+
+                def store(start, length, value, x=x):
+                    column[first + g, x, pl.ds(start, length), :] = value
+
+                fill_column(p, core, smooths[chunk], rims[chunk], g, x, store)
+            return carry
+
+        lax.fori_loop(0, last - first, fill, 0)
+
+    score[...] = jnp.zeros_like(score)
+
+    def forward(cg, carry):
+        taps = [table[cg, pl.ds(ROW_WALL + k, 1), :] for k in range(WALL)]
+        classes = [table[cg, pl.ds(ROW_CLASS + k, 1), :] for k in range(p.classes)]
+        for blk in range(blocks):
+            rows = pl.ds(8 * blk, 8)
+            sums = [None] * p.xs
+            for k in range(WALL):
+                tap = taps[k] * bands[k, rows, :]
+                for x in range(p.xs):
+                    term = tap * column[cg, x, pl.ds(8 * blk + k, 8), :]
+                    sums[x] = term if k == 0 else sums[x] + term
+            for x in range(p.xs):
+                value = sums[x]
+                sig = 0.5 * jnp.tanh(0.5 * value) + 0.5
+                act = value * sig
+                hidden[cg, x, rows, :] = act
+                slope[cg, x, rows, :] = sig + act * (1.0 - sig)
+                for k in range(p.classes):
+                    score[k, x, rows, :] += classes[k] * act
+        return carry
+
+    lax.fori_loop(0, p.groups, forward, 0)
+
+    def judge(blk, carry):
+        rows = pl.ds(pl.multiple_of(8 * blk, 8), 8)
+        place = core * p.rows - half + 8 * blk + lax.broadcasted_iota(jnp.int32, (8, LANES), 0)
+        inside = (place >= 0) & (place < all_rows)
+        for x in range(p.xs):
+            label = spread(p, column[p.groups - 1, x, pl.ds(8 * blk + half, 8), :], lane)
+            for k in range(p.classes):
+                value = score[k, x, rows, :]
+                total = value
+                for b in range(1, p.per):
+                    total = total + pltpu.roll(value, p.block * b, 1)
+                error = spread(p, total, lane) - jnp.where(label == k, 1.0, 0.0)
+                score[k, x, rows, :] = jnp.where(inside, error, 0.0)
+        return carry
+
+    lax.fori_loop(0, blocks, judge, 0)
+    own = own_lanes(p, p.rows)
+    for k in range(p.classes):
+        for x in range(p.xs):
+            errors_out[k, x] = jnp.where(own, score[k, x, pl.ds(half, p.rows), :], 0.0)
+
+    def backward(cg, carry):
+        taps = [table[cg, pl.ds(ROW_WALL + k, 1), :] for k in range(WALL)]
+        classes = [table[cg, pl.ds(ROW_CLASS + k, 1), :] for k in range(p.classes)]
+        for blk in range(blocks):
+            rows = pl.ds(8 * blk, 8)
+            for x in range(p.xs):
+                grad = classes[0] * score[0, x, rows, :]
+                for k in range(1, p.classes):
+                    grad = grad + classes[k] * score[k, x, rows, :]
+                wall[x, rows, :] = (grad * slope[cg, x, rows, :]).astype(BF16).astype(F32)
+        for x in range(p.xs):
+            grad_wall[cg, x] = jnp.where(own, wall[x, pl.ds(half, p.rows), :], 0.0).astype(BF16)
+            hidden_out[cg, x] = hidden[cg, x, pl.ds(half, p.rows), :].astype(BF16)
+        for part in range(p.rows // 16):
+            sums = [None] * p.xs
+            for k in range(WALL):
+                rows = pl.ds(16 * part + WALL - 1 - k, 16)
+                tap = taps[k] * bands[k, rows, :]
+                for x in range(p.xs):
+                    term = tap * wall[x, rows, :]
+                    sums[x] = term if k == 0 else sums[x] + term
+            for x in range(p.xs):
+                grad_smooth[cg, x, pl.ds(16 * part, 16), :] = sums[x].astype(BF16)
+        weights = [table[cg, pl.ds(t, 1), :] for t in range(ROW_WALL)]
+        for part in range(p.rows // 16):
+            rows = pl.ds(16 * part, 16)
+            cells = [grad_smooth[cg, x, rows, :].astype(F32) for x in range(p.xs)]
+            for x in range(p.xs):
+                total = None
+                for j in range(TAPS):
+                    line = None
+                    for i in range(TAPS):
+                        term = weights[TAPS * i + j] * cells[(x - i + REACH) % p.xs]
+                        line = term if line is None else line + term
+                    if j != REACH:
+                        line = pltpu.roll(line, (j - REACH) % LANES, 1)
+                    total = line if total is None else total + line
+                field[cg, x, rows, :] = total
+        return carry
+
+    lax.fori_loop(0, p.groups, backward, 0)
+
+    wide = lane_of(p.rows)
+
+    def ship(pack, carry):
+        for b in range(p.ring):
+            c = pack * p.ring + b
+            cg, at = c // p.per, c % p.per
+            spot = lax.rem(b + me, p.ring)
+            shift = lax.rem(2 * LANES + p.window * spot - p.block * at - EDGE, LANES)
+            for d in range(p.ring):
+                for xp in range(p.cells_x):
+                    moved = pltpu.roll(field[cg, cell_of(p, d, xp)], shift, 1)
+                    held = column[0, cell_of(p, d, xp), pl.ds(0, p.rows), :]
+                    column[0, cell_of(p, d, xp), pl.ds(0, p.rows), :] = jnp.where(
+                        wide // p.window == spot, moved, held
+                    )
+        for d in range(p.ring):
+            for xp in range(p.cells_x):
+                results[d][pack, xp] = column[0, cell_of(p, d, xp), pl.ds(0, p.rows), :].astype(
+                    BF16
+                )
+        return carry
+
+    lax.fori_loop(0, p.packs, ship, 0)
+
+
+def weight_body(p, cuts, bands, grad_smooth, grad_wall, hidden, errors, *refs):
+    count = len(cuts)
+    smooths, rims = refs[:count], refs[count : 2 * count]
+    refs = refs[2 * count :]
+    pieces = [refs[i * p.ring : (i + 1) * p.ring] for i in range(count)]
+    out, column, lines = refs[count * p.ring :]
+    core = lax.axis_index("col")
+    half = WALL // 2
+    own = own_lanes(p, 16)
+    out[...] = jnp.zeros_like(out)
+    lines[...] = jnp.zeros_like(lines)
+    lane = lane_of(LANES)
+    channel = lax.broadcasted_iota(jnp.int32, (LANES, LANES), 0)
+
+    def fold(value):
+        total = value[:8]
+        for r in range(8, value.shape[0], 8):
+            total = total + value[r : r + 8]
+        return jnp.sum(total, axis=0, keepdims=True)
+
+    for chunk, (first, last) in enumerate(cuts):
+
+        def step(g, carry, chunk=chunk, first=first):
+            cg = first + g
+            sums = [None] * ROW_WALL
+            for part in range(p.rows // 16):
+                rows = pl.ds(16 * part, 16)
+                cells = {}
+                for d in range(p.ring):
+                    for xp in range(p.cells_x):
+                        cells[cell_of(p, d, xp)] = pieces[chunk][d][g, xp, rows, :].astype(F32)
+                for x in range(p.xs):
+                    grad = jnp.where(own, grad_smooth[cg, x, rows, :].astype(F32), 0.0)
+                    for j in range(TAPS):
+                        moved = grad if j == REACH else pltpu.roll(grad, (j - REACH) % LANES, 1)
+                        for i in range(TAPS):
+                            t = TAPS * i + j
+                            term = cells[(x + i - REACH) % p.xs] * moved
+                            term = term[:8] + term[8:]
+                            sums[t] = term if sums[t] is None else sums[t] + term
+            for t in range(ROW_WALL):
+                lines[pl.ds(t, 1), :] = fold(sums[t])
+            for x in range(p.xs):
+
+                def store(start, length, value, x=x):
+                    column[x, pl.ds(start, length), :] = value
+
+                fill_column(p, core, smooths[chunk], rims[chunk], g, x, store)
+            grads = [grad_wall[cg, x].astype(F32) for x in range(p.xs)]
+            for k in range(WALL):
+                total = None
+                for x in range(p.xs):
+                    term = grads[x] * column[x, pl.ds(half + k, p.rows), :]
+                    total = term if total is None else total + term
+                lines[pl.ds(ROW_WALL + k, 1), :] = fold(total * bands[k, pl.ds(half, p.rows), :])
+            for k in range(p.classes):
+                total = None
+                for x in range(p.xs):
+                    term = errors[k, x] * hidden[cg, x].astype(F32)
+                    total = term if total is None else total + term
+                lines[pl.ds(ROW_CLASS + k, 1), :] = fold(total)
+            pick = (lane // p.block + cg * p.per == channel) & (lane < p.per * p.block)
+            out[...] += lax.dot_general(
+                lines[...],
+                jnp.where(pick, 1.0, 0.0),
+                (((1,), (1,)), ((), ())),
+                precision=lax.Precision.HIGHEST,
+                preferred_element_type=F32,
+            )
+            return carry
+
+        lax.fori_loop(0, last - first, step, 0)
+
+
+def unpack_body(p, *refs):
+    pieces, out, stage = refs[: p.ring], refs[p.ring], refs[p.ring + 1]
+    me = lax.axis_index("gx")
+    spot = lane_of(p.rows) // p.window
+
+    def step(pack, carry):
+        for xp in range(p.cells_x):
+            values = [pieces[d][pack, xp].astype(F32) for d in range(p.ring)]
+            for b in range(p.ring):
+                total = values[0]
+                for d in range(1, p.ring):
+                    total = jnp.where(spot == lax.rem(b + me + d, p.ring), values[d], total)
+                total = pltpu.roll(total, (LANES - p.window * b) % LANES, 1) if b else total
+                stage[b, pl.ds(xp, p.rows, stride=p.cells_x), :] = total
+        for b in range(p.ring):
+            out[pack * p.ring + b] = stage[b].astype(BF16)
+        return carry
+
+    lax.fori_loop(0, p.packs, step, 0)
+
+
+def rotation(size, by):
+    return [(i, (i + by) % size) for i in range(size)]
+
+
+def sum_over(value, axis):
+    size = lax.axis_size(axis)
+    return sum((lax.ppermute(value, axis, rotation(size, d)) for d in range(1, size)), value)
+
+
+def band_rows(grid_index, stretch):
+    levels = stretch.shape[0]
+    onehot = (grid_index[:, None] == jnp.arange(levels, dtype=jnp.int32)[None, :]).astype(F32)
+    return jnp.dot(onehot, stretch, precision=lax.Precision.HIGHEST)
+
+
+def by_windows(features, labels, grid_index, stretch, tile_filter, wall_filter, class_weight):
+    chans, rows, cells_x, cells_z = features.shape
+    classes = class_weight.shape[0]
+    ring, gz = lax.axis_size("gx"), lax.axis_size("gz")
+    p = Plan(ring, chans, rows, cells_x, cells_z, classes)
+    volume = labels.shape[0] * cells_x * ring * cells_z * gz
+    tall = rows * cells_x
+    middle = p.groups // 2
+    cuts = ((0, middle), (middle, p.groups))
+
+    field = features.reshape(chans, tall, cells_z)
+    marks = labels.reshape(labels.shape[0] * cells_x, cells_z)
+    (edge,) = call(
+        functools.partial(edge_body, p),
+        [jax.ShapeDtypeStruct((p.edge_groups, tall, LANES), BF16)],
+        (field, marks),
+    )
+    left = lax.ppermute(edge, "gz", rotation(gz, 1))
+    right = left if gz == 2 else lax.ppermute(edge, "gz", rotation(gz, -1))
+
+    windows = call(
+        functools.partial(pack_body, p, cuts),
+        [
+            jax.ShapeDtypeStruct((last - first, cells_x, rows, LANES), BF16)
+            for first, last in cuts
+            for d in range(ring)
+        ],
+        (field, marks, left, right),
+        [pltpu.VMEM((ring, tall, LANES), F32)],
+    )
+
+    bands = band_rows(grid_index, stretch)
+    half = WALL // 2
+    near = lax.dynamic_slice_in_dim(
+        jnp.pad(bands, ((half, half), (0, 0))), lax.axis_index("col") * rows, p.reach_rows, 0
+    )
+    near = jnp.broadcast_to(near.T[:, :, None], (WALL, p.reach_rows, LANES))
+    params = jnp.concatenate([tile_filter.T, wall_filter.T, class_weight], axis=0)
+    extra = (jnp.arange(params.shape[0]) == CENTRE).astype(F32)[:, None]
+    params = jnp.concatenate([params, extra], axis=1).reshape(-1, p.groups, p.per, 1)
+    table = jnp.broadcast_to(params, params.shape[:3] + (p.block,))
+    table = table.reshape(params.shape[0], p.groups, p.per * p.block)
+    table = jnp.pad(
+        table,
+        ((0, p.table_rows - table.shape[0]), (0, 0), (0, LANES - p.per * p.block)),
+    ).transpose(1, 0, 2)
+
+    smooths, rims, pieces = [], [], []
+    for chunk, (first, last) in enumerate(cuts):
+        sent = windows[chunk * ring : (chunk + 1) * ring]
+        got = [sent[0]] + [
+            lax.ppermute(sent[d], "gx", rotation(ring, d)) for d in range(1, ring)
+        ]
+        smooth, rim = call(
+            functools.partial(conv_body, p, first, last - first),
+            [
+                jax.ShapeDtypeStruct((last - first, p.xs, rows, LANES), BF16),
+                jax.ShapeDtypeStruct((last - first, p.xs // 2, 16, LANES), BF16),
+            ],
+            (table, *got),
+        )
+        smooths.append(smooth)
+        rims.append(lax.ppermute(rim, "col", rotation(2, 1)))
+        pieces += got
+
+    out_shapes = [jax.ShapeDtypeStruct((p.packs, cells_x, rows, LANES), BF16)] * ring + [
+        jax.ShapeDtypeStruct((p.groups, p.xs, rows, LANES), BF16),
+        jax.ShapeDtypeStruct((p.groups, p.xs, rows, LANES), BF16),
+        jax.ShapeDtypeStruct((p.groups, p.xs, rows, LANES), BF16),
+        jax.ShapeDtypeStruct((classes, p.xs, rows, LANES), F32),
+    ]
+    solved = call(
+        functools.partial(wall_body, p, cuts),
+        out_shapes,
+        (table, near, *smooths, *rims),
+        [
+            pltpu.VMEM((p.groups, p.xs, rows + 2 * WALL_HALO, LANES), F32),
+            pltpu.VMEM((p.groups, p.xs, p.reach_rows, LANES), F32),
+            pltpu.VMEM((p.groups, p.xs, p.reach_rows, LANES), F32),
+            pltpu.VMEM((classes, p.xs, p.reach_rows, LANES), F32),
+            pltpu.VMEM((p.xs, p.reach_rows, LANES), F32),
+            pltpu.VMEM((p.groups, p.xs, rows, LANES), F32),
+        ],
+    )
+    results, (grad_smooth, grad_wall, hidden, errors) = solved[:ring], solved[ring:]
+    back = [results[0]] + [
+        lax.ppermute(results[d], "gx", rotation(ring, -d)) for d in range(1, ring)
+    ]
+    (sums,) = call(
+        functools.partial(weight_body, p, cuts),
+        [jax.ShapeDtypeStruct((p.table_rows, LANES), F32)],
+        (near, grad_smooth, grad_wall, hidden, errors, *smooths, *rims, *pieces),
+        [
+            pltpu.VMEM((p.xs, rows + 2 * WALL_HALO, LANES), F32),
+            pltpu.VMEM((p.table_rows, LANES), F32),
+        ],
+    )
+    for axis in ("col", "gz", "gx"):
+        sums = sum_over(sums, axis)
+    sums = sums / volume
+    (grad_field,) = call(
+        functools.partial(unpack_body, p),
+        [jax.ShapeDtypeStruct((chans, tall, cells_z), BF16)],
+        back,
+        [pltpu.VMEM((ring, tall, LANES), F32)],
+    )
+    return (
+        grad_field.reshape(features.shape),
+        sums[:ROW_WALL, :chans].T,
+        sums[ROW_WALL:ROW_CLASS, :chans].T,
+        sums[ROW_CLASS : ROW_CLASS + classes, :chans],
+    )
 
 
 def with_halo(value, sides, width):
@@ -21,14 +571,6 @@
     return with_halo(field, (("gx", 2), ("gz", 3)), 2)
 
 
-def band_table(grid_index, stretch):
-    levels = stretch.shape[0]
-    onehot = (grid_index[:, None] == jnp.arange(levels, dtype=jnp.int32)[None, :]).astype(
-        jnp.float32
-    )
-    return jnp.dot(onehot, stretch, precision=lax.Precision.HIGHEST)
-
-
 def wall_forward(smooth_ext, wall_rows, band_rows):
     rows = band_rows.shape[0]
     total = jnp.zeros((smooth_ext.shape[0], rows) + smooth_ext.shape[2:], jnp.float32)
@@ -49,7 +591,7 @@
     return total
 
 
-def shards(features, labels, grid_index, stretch, tile_filter, wall_filter, class_weight):
+def by_halos(features, labels, grid_index, stretch, tile_filter, wall_filter, class_weight):
     chans, half_rows, cells_x, cells_z = features.shape
     all_rows = labels.shape[0]
     classes = class_weight.shape[0]
@@ -63,7 +605,7 @@
                 jnp.float32
             )
     smoothed = smooth.astype(jnp.bfloat16)
-    bands = band_table(grid_index, stretch)
+    bands = band_rows(grid_index, stretch)
     bands_pad = jnp.pad(bands, ((4, 4), (0, 0)))
     place = lax.axis_index("col")
     share = chans // lax.axis_size("col")
@@ -128,6 +670,12 @@
         totals[1] / volume,
         totals[2] / volume,
     )
+
+
+def shards(features, labels, grid_index, stretch, tile_filter, wall_filter, class_weight):
+    sizes = [lax.axis_size(axis) for axis in ("gx", "gz", "col")]
+    plan = by_windows if fits(*sizes, *features.shape, class_weight.shape[0]) else by_halos
+    return plan(features, labels, grid_index, stretch, tile_filter, wall_filter, class_weight)
 
 
 def solution(mesh):

time: 228 us -> 75.8 us (0.33)
  blocking collectives: 81.2 us -> 0 us
  other arithmetic: 39.9 us -> 0.11 us
  local copies, waits for them, and re-layouts: 35.5 us -> 6.5 us
  Pallas kernels: 0 us -> 25.2 us
  waiting for transfers between devices: 34.4 us -> 19.5 us
  between operations: 14.8 us -> 0.77 us
  starting transfers between devices: 13.2 us -> 23.3 us
  matrix products: 8.43 us -> 0.2 us
    psum x1 -> x0, blocking collectives: 72.8 us -> none  [shards(): totals = lax.psum((tile_part, wall_full, class_full), ('gx', 'gz', 'col'))]
    pallas_call x0 -> x7, Pallas kernels: none -> 25.2 us  [call(): pl.pallas_call(body, out_shape=outs, in_specs=vmem(len(args)), out_specs=...]
    convert_element_type x3 -> x1, other arithmetic: 19.4 us -> 0.02 us  [by_windows(): extra = (jnp.arange(params.shape[0]) == CENTRE).astype(F32)[:, None]]
    psum x1 -> x0, waiting for transfers between devices: 18.9 us -> none  [shards(): scores = lax.psum(partial_scores, 'col')]
    slice x7 -> x1, local copies, waits for them, and re-layouts: 14 us -> 0.58 us  [by_windows(): sums[ROW_CLASS:ROW_CLASS + classes, :chans]]
    ppermute x8 -> x17, starting transfers between devices: 13.2 us -> 23.3 us  [the longest x6 9.99 us: by_windows(): lax.ppermute(sent[d], 'gx', rotation(ring, d))]
    ppermute x4 -> x0, local copies, waits for them, and re-layouts: 8.78 us -> none  [the longest x2 4.41 us: with_halo(): before = lax.ppermute(last, axis, up)]
    reduce_sum x3 -> x0, other arithmetic: 8.73 us -> none  [shards(): tile_terms.append(jnp.sum(shifted * grad_tile_vals, axis=(1, 2, 3)))]
  transfers between devices with their start and end apart: 9 -> 17, of which waited for: 4 -> 10; matrix products, arithmetic and copies ran while one was open for 10% -> 5% of each run, Pallas kernels for 0% -> 4%
where the time goes in v1:
time: 75.8 us; the launch traced here: 75.6 us
  Pallas kernels  25.2 us (33%)
  starting transfers between devices  23.3 us (31%)
  waiting for transfers between devices  19.5 us (26%)
  local copies, waits for them, and re-layouts  6.5 us (9%)
  between operations  0.77 us (1%)
    pallas_call x7, Pallas kernels, call(): pl.pallas_call(body, out_shape=outs, in_specs=vmem(len(args)), out_specs=...  25.2 us
    ppermute x6, starting transfers between devices, by_windows(): lax.ppermute(sent[d], 'gx', rotation(ring, d))  9.99 us
    ppermute x3, waiting for transfers between devices, by_windows(): lax.ppermute(results[d], 'gx', rotation(ring, -d))  7.52 us
    ppermute x6, waiting for transfers between devices, by_windows(): lax.ppermute(sent[d], 'gx', rotation(ring, d))  6.06 us
    ppermute x5, starting transfers between devices, sum_over(): lax.ppermute(value, axis, rotation(size, d))  5.9 us
    ppermute x5, waiting for transfers between devices, sum_over(): lax.ppermute(value, axis, rotation(size, d))  4.34 us
    ppermute x3, starting transfers between devices, by_windows(): lax.ppermute(results[d], 'gx', rotation(ring, -d))  4.32 us
    unnamed x20, local copies, waits for them, and re-layouts  3.97 us
  transfers between devices with their start and end apart: 17, of which 10 were waited for; matrix products, arithmetic and copies ran while one was open for 5% of the time, Pallas kernels for 4%

profile of v1, /device:TPU:0, one launch (start us, length us, event | category | flops | bytes accessed | tf_op | source)
XLA Modules:
  0.0 75.6 jit_solution(11500085143838223654)
XLA Ops:
  0.7 1.0 %copy-done.1 = bf16[32,32,2,128]{3,2,1,0:T(2,128)(2,1)S(1)} copy-done((bf16[32,32,2,128]{3,2,1,0:T(2,128)(2,1)S(1)}, bf16[32,32,2,128]{3,2,1,0:T(2,128)(2,1)}, u32[]{:S(2)}) %copy-start.1) | copy-done | bytes 524312
  1.7 0.8 %copy-done.3 = s32[64,2,128]{2,1,0:T(2,128)S(1)} copy-done((s32[64,2,128]{2,1,0:T(2,128)S(1)}, s32[64,2,128]{2,1,0:T(2,128)}, u32[]{:S(2)}) %copy-start.3) | copy-done | bytes 65560
  2.5 0.3 shard_map.102
  2.9 3.0 %collective-permute-start = (bf16[3,64,128]{2,1,0:T(8,128)(2,1)S(1)}, bf16[3,64,128]{2,1,0:T(8,128)(2,1)S(1)}, u32[]{:S(2)}, u32[]{:S(2)}) collective-permute-start(bf16[3,64,128]{2,1,0:T(8,128)(2,1)S(1)} %shard_map.102), channel_id=1, source_target_pairs={{0,2},{2,0},{1,3},{3,1},{4,6},{6,4},{5,7},{7,5},{8,10},{10,8},{9,1... | collective-permute-start | bytes 147464 | tf_op jit(solution)/shard_map/ppermute | solution.py:460
  5.9 0.2 fusion
  6.1 0.7 copy-done.6
  6.8 0.1 copy.15
  6.9 0.6 copy-done.7
  7.5 0.1 copy.16
  7.6 0.4 collective-permute-done.left.right
  8.0 2.3 %shard_map.103 = (bf16[5,2,32,128]{3,2,1,0:T(8,128)(2,1)S(1)}, bf16[5,2,32,128]{3,2,1,0:T(8,128)(2,1)S(1)}, bf16[5,2,32,128]{3,2,1,0:T(8,128)(2,1)S(1)}, bf16[5,...) custom-call(bf16[32,64,128]{2,1,0:T(8,128)(2,1)S(1)} %bitcast.19, ...), custom_call_target="tpu_custom_call" | custom-call | tf_op jit(solution)/shard_map/pallas_call | solution.py:52
  10.3 2.2 %collective-permute-start.1 = (bf16[5,2,32,128]{3,2,1,0:T(8,128)(2,1)S(1)}, bf16[5,2,32,128]{3,2,1,0:T(8,128)(2,1)S(1)}, u32[]{:S(2)}, u32[]{:S(2)}) collective-permute-start(bf16[5,2,32,128]{3,2,1,0:T(8,128)(2,1)S(1)} %get-tuple-element.25), channel_id=1, source_target_pairs={{0,4},{4,8},{8,12},{12,0},{1,5},{5,9},{9,13},{13,1},{2,6},{6,10},{... | collective-permute-start | bytes 245768 | tf_op jit(solution)/shard_map/ppermute | solution.py:494
  12.5 0.1 pad_maximum_fusion
  12.6 0.2 copy.17
  12.7 0.5 broadcast_in_dim.7
  13.2 0.4 reshape.34
  13.6 2.7 %collective-permute-start.2 = (bf16[5,2,32,128]{3,2,1,0:T(8,128)(2,1)S(1)}, bf16[5,2,32,128]{3,2,1,0:T(8,128)(2,1)S(1)}, u32[]{:S(2)}, u32[]{:S(2)}) collective-permute-start(bf16[5,2,32,128]{3,2,1,0:T(8,128)(2,1)S(1)} %get-tuple-element.26), channel_id=1, source_target_pairs={{0,8},{4,12},{8,0},{12,4},{1,9},{5,13},{9,1},{13,5},{2,10},{6,14},... | collective-permute-start | bytes 245768 | tf_op jit(solution)/shard_map/ppermute | solution.py:494
  16.3 1.3 %collective-permute-start.3 = (bf16[5,2,32,128]{3,2,1,0:T(8,128)(2,1)S(1)}, bf16[5,2,32,128]{3,2,1,0:T(8,128)(2,1)S(1)}, u32[]{:S(2)}, u32[]{:S(2)}) collective-permute-start(bf16[5,2,32,128]{3,2,1,0:T(8,128)(2,1)S(1)} %get-tuple-element.27), channel_id=1, source_target_pairs={{0,12},{4,0},{8,4},{12,8},{1,13},{5,1},{9,5},{13,9},{2,14},{6,2},{... | collective-permute-start | bytes 245768 | tf_op jit(solution)/shard_map/ppermute | solution.py:494
  17.6 0.7 collective-permute-start.4
  18.3 0.3 collective-permute-start.5
  18.6 2.8 %collective-permute-start.6 = (bf16[6,2,32,128]{3,2,1,0:T(8,128)(2,1)S(1)}, bf16[6,2,32,128]{3,2,1,0:T(8,128)(2,1)S(1)}, u32[]{:S(2)}, u32[]{:S(2)}) collective-permute-start(bf16[6,2,32,128]{3,2,1,0:T(8,128)(2,1)S(1)} %get-tuple-element.32), channel_id=1, source_target_pairs={{0,12},{4,0},{8,4},{12,8},{1,13},{5,1},{9,5},{13,9},{2,14},{6,2},{... | collective-permute-start | bytes 294920 | tf_op jit(solution)/shard_map/ppermute | solution.py:494
  21.5 0.3 collective-permute-done.2.refs_2_.refs_6_
  21.8 1.0 %collective-permute-done.3.refs_3_.refs_7_ = bf16[5,2,32,128]{3,2,1,0:T(8,128)(2,1)S(1)} collective-permute-done((bf16[5,2,32,128]{3,2,1,0:T(8,128)(2,1)S(1)}, bf16[5,2,32,128]{3,2,1,0:T(8,128)(2,1)S(1)}, u32[]{:S(2)}, u32[]{:S(2)}) %collective-permute-start.3) | collective-permute-done | bytes 81952 | tf_op jit(solution)/shard_map/ppermute | solution.py:494
  22.8 1.3 %shard_map.104 = (bf16[5,8,32,128]{3,2,1,0:T(8,128)(2,1)S(1)}, bf16[5,4,16,128]{3,2,1,0:T(8,128)(2,1)S(1)}) custom-call(f32[11,40,128]{2,1,0:T(8,128)S(1)} %pad_bitcast_fusion.table, bf16[5,2,32,128]{3,2,1,0:T(8,128)(2,1)S(1)} %get-tuple-element.24.refs_0_.refs_4_, bf16[5,2,32,128]{3,2,1,0:T(8,128)(2,1)S(1)} %collective-permute-done.1.refs_1_.refs_5_, ...), custom_call_target="tpu_custom_call" | custom-call | tf_op jit(solution)/shard_map/pallas_call | solution.py:52
  24.1 0.1 collective-permute-start.7
  24.2 1.0 %collective-permute-done.4.refs_1_.refs_9_ = bf16[6,2,32,128]{3,2,1,0:T(8,128)(2,1)S(1)} collective-permute-done((bf16[6,2,32,128]{3,2,1,0:T(8,128)(2,1)S(1)}, bf16[6,2,32,128]{3,2,1,0:T(8,128)(2,1)S(1)}, u32[]{:S(2)}, u32[]{:S(2)}) %collective-permute-start.4) | collective-permute-done | bytes 98336 | tf_op jit(solution)/shard_map/ppermute | solution.py:494
  25.1 3.8 %collective-permute-done.5.refs_2_.refs_10_ = bf16[6,2,32,128]{3,2,1,0:T(8,128)(2,1)S(1)} collective-permute-done((bf16[6,2,32,128]{3,2,1,0:T(8,128)(2,1)S(1)}, bf16[6,2,32,128]{3,2,1,0:T(8,128)(2,1)S(1)}, u32[]{:S(2)}, u32[]{:S(2)}) %collective-permute-start.5) | collective-permute-done | bytes 98336 | tf_op jit(solution)/shard_map/ppermute | solution.py:494
  28.9 1.6 %shard_map.105 = (bf16[6,8,32,128]{3,2,1,0:T(8,128)(2,1)S(1)}, bf16[6,4,16,128]{3,2,1,0:T(8,128)(2,1)S(1)}) custom-call(f32[11,40,128]{2,1,0:T(8,128)S(1)} %pad_bitcast_fusion.table, bf16[6,2,32,128]{3,2,1,0:T(8,128)(2,1)S(1)} %get-tuple-element.29.refs_0_.refs_8_, bf16[6,2,32,128]{3,2,1,0:T(8,128)(2,1)S(1)} %collective-permute-done.4.refs_1_.refs_9_, ...), custom_call_target="tpu_custom_call" | custom-call | tf_op jit(solution)/shard_map/pallas_call | solution.py:52
  30.5 0.1 collective-permute-start.8
  30.5 0.1 dynamic-slice_bitcast_fusion
  30.6 1.2 %collective-permute-done.8.refs_3_ = bf16[6,4,16,128]{3,2,1,0:T(8,128)(2,1)S(1)} collective-permute-done((bf16[6,4,16,128]{3,2,1,0:T(8,128)(2,1)S(1)}, bf16[6,4,16,128]{3,2,1,0:T(8,128)(2,1)S(1)}, u32[]{:S(2)}, u32[]{:S(2)}) %collective-permute-start.8) | collective-permute-done | bytes 98336 | tf_op jit(solution)/shard_map/ppermute | solution.py:505
  31.8 0.1 broadcast_in_dim.8.bands
  31.9 10.9 %shard_map.106 = (bf16[8,2,32,128]{3,2,1,0:T(8,128)(2,1)S(1)}, bf16[8,2,32,128]{3,2,1,0:T(8,128)(2,1)S(1)}, bf16[8,2,32,128]{3,2,1,0:T(8,128)(2,1)S(1)}, bf16[8,...) custom-call(f32[11,40,128]{2,1,0:T(8,128)S(1)} %pad_bitcast_fusion.t, ...), custom_call_target="tpu_custom_call" | custom-call | tf_op jit(solution)/shard_map/pallas_call | solution.py:52
  42.8 7.1 %shard_map.108 = f32[40,128]{1,0:T(8,128)S(1)} custom-call(f32[9,40,128]{2,1,0:T(8,128)S(1)} %broadcast_in_dim.8.bands, bf16[11,8,32,128]{3,2,1,0:T(8,128)(2,1)S(1)} %get-tuple-element.40.grad_smooth, bf16[11,8,32,128]{3,2,1,0:T(8,128)(2,1)S(1)} %get-tuple-element.41.grad_wall, bf16[11,8,32,128]{3,2,1,0:T(8,128)(2,1)S(1)} %get-tuple-element.42.hidden, ...), custom_call_target="tpu_custom_call" | custom-call | tf_op jit(solution)/shard_map/pallas_call | solution.py:52
  50.0 0.2 collective-permute-start.12
  50.2 1.0 %collective-permute-done.12 = f32[40,128]{1,0:T(8,128)S(1)} collective-permute-done((f32[40,128]{1,0:T(8,128)S(1)}, f32[40,128]{1,0:T(8,128)S(1)}, u32[]{:S(2)}, u32[]{:S(2)}) %collective-permute-start.12) | collective-permute-done | bytes 20512 | tf_op jit(solution)/shard_map/ppermute | solution.py:434
  51.2 1.5 %collective-permute-start.13 = (f32[40,128]{1,0:T(8,128)S(1)}, f32[40,128]{1,0:T(8,128)S(1)}, u32[]{:S(2)}, u32[]{:S(2)}) collective-permute-start(f32[40,128]{1,0:T(8,128)S(1)} %add.23), channel_id=1, source_target_pairs={{0,2},{2,0},{1,3},{3,1},{4,6},{6,4},{5,7},{7,5},{8,10},{10,8},{9,1... | collective-permute-start | bytes 61448 | tf_op jit(solution)/shard_map/ppermute | solution.py:434
  52.7 2.3 %collective-permute-done.13 = f32[40,128]{1,0:T(8,128)S(1)} collective-permute-done((f32[40,128]{1,0:T(8,128)S(1)}, f32[40,128]{1,0:T(8,128)S(1)}, u32[]{:S(2)}, u32[]{:S(2)}) %collective-permute-start.13) | collective-permute-done | bytes 20512 | tf_op jit(solution)/shard_map/ppermute | solution.py:434
  55.0 3.6 %collective-permute-start.16 = (f32[40,128]{1,0:T(8,128)S(1)}, f32[40,128]{1,0:T(8,128)S(1)}, u32[]{:S(2)}, u32[]{:S(2)}) collective-permute-start(f32[40,128]{1,0:T(8,128)S(1)} %add.24), channel_id=1, source_target_pairs={{0,12},{4,0},{8,4},{12,8},{1,13},{5,1},{9,5},{13,9},{2,14},{6,2},{... | collective-permute-start | bytes 61448 | tf_op jit(solution)/shard_map/ppermute | solution.py:434
  58.6 0.6 collective-permute-start.14
  59.2 3.2 %collective-permute-start.9 = (bf16[8,2,32,128]{3,2,1,0:T(8,128)(2,1)S(1)}, bf16[8,2,32,128]{3,2,1,0:T(8,128)(2,1)S(1)}, u32[]{:S(2)}, u32[]{:S(2)}) collective-permute-start(bf16[8,2,32,128]{3,2,1,0:T(8,128)(2,1)S(1)} %get-tuple-element.37), channel_id=1, source_target_pairs={{0,12},{4,0},{8,4},{12,8},{1,13},{5,1},{9,5},{13,9},{2,14},{6,2},{... | collective-permute-start | bytes 393224 | tf_op jit(solution)/shard_map/ppermute | solution.py:529
  62.4 1.1 %collective-permute-start.10 = (bf16[8,2,32,128]{3,2,1,0:T(8,128)(2,1)S(1)}, bf16[8,2,32,128]{3,2,1,0:T(8,128)(2,1)S(1)}, u32[]{:S(2)}, u32[]{:S(2)}) collective-permute-start(bf16[8,2,32,128]{3,2,1,0:T(8,128)(2,1)S(1)} %get-tuple-element.38), channel_id=1, source_target_pairs={{0,8},{4,12},{8,0},{12,4},{1,9},{5,13},{9,1},{13,5},{2,10},{6,14},... | collective-permute-start | bytes 393224 | tf_op jit(solution)/shard_map/ppermute | solution.py:529
  63.5 1.0 %collective-permute-done.14 = f32[40,128]{1,0:T(8,128)S(1)} collective-permute-done((f32[40,128]{1,0:T(8,128)S(1)}, f32[40,128]{1,0:T(8,128)S(1)}, u32[]{:S(2)}, u32[]{:S(2)}) %collective-permute-start.14) | collective-permute-done | bytes 20512 | tf_op jit(solution)/shard_map/ppermute | solution.py:434
  64.5 0.6 slice.14
  65.1 0.7 copy.18
  65.8 0.6 slice_bitcast_fusion.1
  66.4 7.5 %collective-permute-done.10.refs_2_ = bf16[8,2,32,128]{3,2,1,0:T(8,128)(2,1)S(1)} collective-permute-done((bf16[8,2,32,128]{3,2,1,0:T(8,128)(2,1)S(1)}, bf16[8,2,32,128]{3,2,1,0:T(8,128)(2,1)S(1)}, u32[]{:S(2)}, u32[]{:S(2)}) %collective-permute-start.10) | collective-permute-done | bytes 131104 | tf_op jit(solution)/shard_map/ppermute | solution.py:529
  73.9 1.6 %shard_map.107 = bf16[32,64,128]{2,1,0:T(8,128)(2,1)} custom-call(bf16[8,2,32,128]{3,2,1,0:T(8,128)(2,1)S(1)} %get-tuple-element.36.refs_0_, bf16[8,2,32,128]{3,2,1,0:T(8,128)(2,1)S(1)} %collective-permute-done.9.refs_1_, bf16[8,2,32,128]{3,2,1,0:T(8,128)(2,1)S(1)} %collective-permute-done.10.refs_2_, bf16[8,2,32,128]{3,2,1,0:T(8,128)(2,1)S(1)} %collective-permute-done.11.refs_3_), custom_call_target="tpu_custom_call" | custom-call | tf_op jit(solution)/shard_map/pallas_call | solution.py:52
  (30 shorter events, 0.1 us)
Async XLA Ops:
  0.6 5.2 %copy-start = (f32[16,9]{1,0:T(8,128)S(1)}, f32[16,9]{1,0:T(8,128)}, u32[]{:S(2)}) copy-start(f32[16,9]{1,0:T(8,128)} %param.10) | copy-start | bytes 1732
  0.6 1.0 %copy-start.1 = (bf16[32,32,2,128]{3,2,1,0:T(2,128)(2,1)S(1)}, bf16[32,32,2,128]{3,2,1,0:T(2,128)(2,1)}, u32[]{:S(2)}) copy-start(bf16[32,32,2,128]{3,2,1,0:T(2,128)(2,1)} %param.7) | copy-start | bytes 1572868
  1.7 0.8 %copy-start.3 = (s32[64,2,128]{2,1,0:T(2,128)S(1)}, s32[64,2,128]{2,1,0:T(2,128)}, u32[]{:S(2)}) copy-start(s32[64,2,128]{2,1,0:T(2,128)} %param.8) | copy-start | bytes 196612
  2.5 3.3 %copy-start.8 = (s32[64]{0:T(128)S(1)}, s32[64]{0:T(128)}, u32[]{:S(2)}) copy-start(s32[64]{0:T(128)} %param.9) | copy-start | bytes 772
  2.5 5.4 %copy-start.2 = (bf16[32,32,2,128]{3,2,1,0:T(2,128)(2,1)S(1)}, bf16[32,32,2,128]{3,2,1,0:T(2,128)(2,1)}, u32[]{:S(2)}) copy-start(bf16[32,32,2,128]{3,2,1,0:T(2,128)(2,1)} %param.7) | copy-start | bytes 1572868
  2.9 5.1 %copy-start.4 = (s32[64,2,128]{2,1,0:T(2,128)S(1)}, s32[64,2,128]{2,1,0:T(2,128)}, u32[]{:S(2)}) copy-start(s32[64,2,128]{2,1,0:T(2,128)} %param.8) | copy-start | bytes 196612
  2.9 5.1 %collective-permute-start = (bf16[3,64,128]{2,1,0:T(8,128)(2,1)S(1)}, bf16[3,64,128]{2,1,0:T(8,128)(2,1)S(1)}, u32[]{:S(2)}, u32[]{:S(2)}) collective-permute-start(bf16[3,64,128]{2,1,0:T(8,128)(2,1)S(1)} %shard_map.102), channel_id=1, source_target_pairs={{0,2},{2,0},{1,3},{3,1},{4,6},{6,4},{5,7},{7,5},{8,10},{10,8},{9,1... | collective-permute-start | bytes 147464 | tf_op jit(solution)/shard_map/ppermute | solution.py:460
  6.1 0.7 copy-start.6
  6.8 0.7 copy-start.7
  7.6 4.9 %copy-start.5 = (f32[32,25]{1,0:T(8,128)S(1)}, f32[32,25]{1,0:T(8,128)}, u32[]{:S(2)}) copy-start(f32[32,25]{1,0:T(8,128)} %param.11) | copy-start | bytes 9604
  10.3 8.3 %collective-permute-start.1 = (bf16[5,2,32,128]{3,2,1,0:T(8,128)(2,1)S(1)}, bf16[5,2,32,128]{3,2,1,0:T(8,128)(2,1)S(1)}, u32[]{:S(2)}, u32[]{:S(2)}) collective-permute-start(bf16[5,2,32,128]{3,2,1,0:T(8,128)(2,1)S(1)} %get-tuple-element.25), channel_id=1, source_target_pairs={{0,4},{4,8},{8,12},{12,0},{1,5},{5,9},{9,13},{13,1},{2,6},{6,10},{... | collective-permute-start | bytes 245768 | tf_op jit(solution)/shard_map/ppermute | solution.py:494
  13.6 8.2 %collective-permute-start.2 = (bf16[5,2,32,128]{3,2,1,0:T(8,128)(2,1)S(1)}, bf16[5,2,32,128]{3,2,1,0:T(8,128)(2,1)S(1)}, u32[]{:S(2)}, u32[]{:S(2)}) collective-permute-start(bf16[5,2,32,128]{3,2,1,0:T(8,128)(2,1)S(1)} %get-tuple-element.26), channel_id=1, source_target_pairs={{0,8},{4,12},{8,0},{12,4},{1,9},{5,13},{9,1},{13,5},{2,10},{6,14},... | collective-permute-start | bytes 245768 | tf_op jit(solution)/shard_map/ppermute | solution.py:494
  16.3 6.5 %collective-permute-start.3 = (bf16[5,2,32,128]{3,2,1,0:T(8,128)(2,1)S(1)}, bf16[5,2,32,128]{3,2,1,0:T(8,128)(2,1)S(1)}, u32[]{:S(2)}, u32[]{:S(2)}) collective-permute-start(bf16[5,2,32,128]{3,2,1,0:T(8,128)(2,1)S(1)} %get-tuple-element.27), channel_id=1, source_target_pairs={{0,12},{4,0},{8,4},{12,8},{1,13},{5,1},{9,5},{13,9},{2,14},{6,2},{... | collective-permute-start | bytes 245768 | tf_op jit(solution)/shard_map/ppermute | solution.py:494
  17.6 7.5 %collective-permute-start.4 = (bf16[6,2,32,128]{3,2,1,0:T(8,128)(2,1)S(1)}, bf16[6,2,32,128]{3,2,1,0:T(8,128)(2,1)S(1)}, u32[]{:S(2)}, u32[]{:S(2)}) collective-permute-start(bf16[6,2,32,128]{3,2,1,0:T(8,128)(2,1)S(1)} %get-tuple-element.30), channel_id=1, source_target_pairs={{0,4},{4,8},{8,12},{12,0},{1,5},{5,9},{9,13},{13,1},{2,6},{6,10},{... | collective-permute-start | bytes 294920 | tf_op jit(solution)/shard_map/ppermute | solution.py:494
  18.3 10.6 %collective-permute-start.5 = (bf16[6,2,32,128]{3,2,1,0:T(8,128)(2,1)S(1)}, bf16[6,2,32,128]{3,2,1,0:T(8,128)(2,1)S(1)}, u32[]{:S(2)}, u32[]{:S(2)}) collective-permute-start(bf16[6,2,32,128]{3,2,1,0:T(8,128)(2,1)S(1)} %get-tuple-element.31), channel_id=1, source_target_pairs={{0,8},{4,12},{8,0},{12,4},{1,9},{5,13},{9,1},{13,5},{2,10},{6,14},... | collective-permute-start | bytes 294920 | tf_op jit(solution)/shard_map/ppermute | solution.py:494
  18.6 10.3 %collective-permute-start.6 = (bf16[6,2,32,128]{3,2,1,0:T(8,128)(2,1)S(1)}, bf16[6,2,32,128]{3,2,1,0:T(8,128)(2,1)S(1)}, u32[]{:S(2)}, u32[]{:S(2)}) collective-permute-start(bf16[6,2,32,128]{3,2,1,0:T(8,128)(2,1)S(1)} %get-tuple-element.32), channel_id=1, source_target_pairs={{0,12},{4,0},{8,4},{12,8},{1,13},{5,1},{9,5},{13,9},{2,14},{6,2},{... | collective-permute-start | bytes 294920 | tf_op jit(solution)/shard_map/ppermute | solution.py:494
  24.1 6.5 %collective-permute-start.7 = (bf16[5,4,16,128]{3,2,1,0:T(8,128)(2,1)S(1)}, bf16[5,4,16,128]{3,2,1,0:T(8,128)(2,1)S(1)}, u32[]{:S(2)}, u32[]{:S(2)}) collective-permute-start(bf16[5,4,16,128]{3,2,1,0:T(8,128)(2,1)S(1)} %get-tuple-element.34), channel_id=1, source_target_pairs={{0,1},{1,0},{2,3},{3,2},{4,5},{5,4},{6,7},{7,6},{8,9},{9,8},{10,11... | collective-permute-start | bytes 245768 | tf_op jit(solution)/shard_map/ppermute | solution.py:505
  30.5 1.4 %collective-permute-start.8 = (bf16[6,4,16,128]{3,2,1,0:T(8,128)(2,1)S(1)}, bf16[6,4,16,128]{3,2,1,0:T(8,128)(2,1)S(1)}, u32[]{:S(2)}, u32[]{:S(2)}) collective-permute-start(bf16[6,4,16,128]{3,2,1,0:T(8,128)(2,1)S(1)} %get-tuple-element.35), channel_id=1, source_target_pairs={{0,1},{1,0},{2,3},{3,2},{4,5},{5,4},{6,7},{7,6},{8,9},{9,8},{10,11... | collective-permute-start | bytes 294920 | tf_op jit(solution)/shard_map/ppermute | solution.py:505
  50.0 1.3 %collective-permute-start.12 = (f32[40,128]{1,0:T(8,128)S(1)}, f32[40,128]{1,0:T(8,128)S(1)}, u32[]{:S(2)}, u32[]{:S(2)}) collective-permute-start(f32[40,128]{1,0:T(8,128)S(1)} %shard_map.108), channel_id=1, source_target_pairs={{0,1},{1,0},{2,3},{3,2},{4,5},{5,4},{6,7},{7,6},{8,9},{9,8},{10,11... | collective-permute-start | bytes 61448 | tf_op jit(solution)/shard_map/ppermute | solution.py:434
  51.2 3.8 %collective-permute-start.13 = (f32[40,128]{1,0:T(8,128)S(1)}, f32[40,128]{1,0:T(8,128)S(1)}, u32[]{:S(2)}, u32[]{:S(2)}) collective-permute-start(f32[40,128]{1,0:T(8,128)S(1)} %add.23), channel_id=1, source_target_pairs={{0,2},{2,0},{1,3},{3,1},{4,6},{6,4},{5,7},{7,5},{8,10},{10,8},{9,1... | collective-permute-start | bytes 61448 | tf_op jit(solution)/shard_map/ppermute | solution.py:434
  55.0 8.5 %collective-permute-start.16 = (f32[40,128]{1,0:T(8,128)S(1)}, f32[40,128]{1,0:T(8,128)S(1)}, u32[]{:S(2)}, u32[]{:S(2)}) collective-permute-start(f32[40,128]{1,0:T(8,128)S(1)} %add.24), channel_id=1, source_target_pairs={{0,12},{4,0},{8,4},{12,8},{1,13},{5,1},{9,5},{13,9},{2,14},{6,2},{... | collective-permute-start | bytes 61448 | tf_op jit(solution)/shard_map/ppermute | solution.py:434
  58.6 5.0 %collective-permute-start.15 = (f32[40,128]{1,0:T(8,128)S(1)}, f32[40,128]{1,0:T(8,128)S(1)}, u32[]{:S(2)}, u32[]{:S(2)}) collective-permute-start(f32[40,128]{1,0:T(8,128)S(1)} %add.24), channel_id=1, source_target_pairs={{0,8},{4,12},{8,0},{12,4},{1,9},{5,13},{9,1},{13,5},{2,10},{6,14},... | collective-permute-start | bytes 61448 | tf_op jit(solution)/shard_map/ppermute | solution.py:434
  58.6 6.0 %collective-permute-start.14 = (f32[40,128]{1,0:T(8,128)S(1)}, f32[40,128]{1,0:T(8,128)S(1)}, u32[]{:S(2)}, u32[]{:S(2)}) collective-permute-start(f32[40,128]{1,0:T(8,128)S(1)} %add.24), channel_id=1, source_target_pairs={{0,4},{4,8},{8,12},{12,0},{1,5},{5,9},{9,13},{13,1},{2,6},{6,10},{... | collective-permute-start | bytes 61448 | tf_op jit(solution)/shard_map/ppermute | solution.py:434
  59.2 7.2 %collective-permute-start.9 = (bf16[8,2,32,128]{3,2,1,0:T(8,128)(2,1)S(1)}, bf16[8,2,32,128]{3,2,1,0:T(8,128)(2,1)S(1)}, u32[]{:S(2)}, u32[]{:S(2)}) collective-permute-start(bf16[8,2,32,128]{3,2,1,0:T(8,128)(2,1)S(1)} %get-tuple-element.37), channel_id=1, source_target_pairs={{0,12},{4,0},{8,4},{12,8},{1,13},{5,1},{9,5},{13,9},{2,14},{6,2},{... | collective-permute-start | bytes 393224 | tf_op jit(solution)/shard_map/ppermute | solution.py:529
  62.4 11.5 %collective-permute-start.10 = (bf16[8,2,32,128]{3,2,1,0:T(8,128)(2,1)S(1)}, bf16[8,2,32,128]{3,2,1,0:T(8,128)(2,1)S(1)}, u32[]{:S(2)}, u32[]{:S(2)}) collective-permute-start(bf16[8,2,32,128]{3,2,1,0:T(8,128)(2,1)S(1)} %get-tuple-element.38), channel_id=1, source_target_pairs={{0,8},{4,12},{8,0},{12,4},{1,9},{5,13},{9,1},{13,5},{2,10},{6,14},... | collective-permute-start | bytes 393224 | tf_op jit(solution)/shard_map/ppermute | solution.py:529
  63.5 10.4 %collective-permute-start.11 = (bf16[8,2,32,128]{3,2,1,0:T(8,128)(2,1)S(1)}, bf16[8,2,32,128]{3,2,1,0:T(8,128)(2,1)S(1)}, u32[]{:S(2)}, u32[]{:S(2)}) collective-permute-start(bf16[8,2,32,128]{3,2,1,0:T(8,128)(2,1)S(1)} %get-tuple-element.39), channel_id=1, source_target_pairs={{0,4},{4,8},{8,12},{12,0},{1,5},{5,9},{9,13},{13,1},{2,6},{6,10},{... | collective-permute-start | bytes 393224 | tf_op jit(solution)/shard_map/ppermute | solution.py:529

commit v2 on v1

--- a/solution.py
+++ b/solution.py
@@ -1,4 +1,5 @@
 import functools
+import math
 
 import jax
 import jax.numpy as jnp
@@ -36,6 +37,17 @@
         self.table_rows = -(-(ROW_CLASS + classes) // 8) * 8
 
 
+    def cuts(self):
+        unit = math.lcm(self.per, self.ring)
+        step = unit // self.per
+        firsts = list(range(0, self.groups, step))
+        if len(firsts) > 3:
+            firsts = [firsts[0], firsts[len(firsts) // 3], firsts[len(firsts) * 2 // 3]]
+        cuts = tuple(zip(firsts, firsts[1:] + [self.groups]))
+        early = cuts[-1][0] * self.per // self.ring
+        return cuts, (early, self.packs - early)
+
+
 def fits(ring, gz, col, chans, rows, cells_x, cells_z, classes):
     if cells_z != LANES or cells_x != 2 or col != 2 or ring < 2 or ring > 4 or LANES % ring:
         return False
@@ -48,11 +60,14 @@
     return [pl.BlockSpec(memory_space=pltpu.VMEM)] * count
 
 
-def call(body, outs, args, scratch=()):
+def call(body, outs, args, scratch=(), micros=1.0, unread=0):
     return pl.pallas_call(
         body,
         out_shape=outs,
-        in_specs=vmem(len(args)),
+        in_specs=vmem(len(args) - unread) + [pl.BlockSpec(memory_space=pl.ANY)] * unread,
+        cost_estimate=pl.CostEstimate(
+            flops=0, bytes_accessed=int(3.0e6 * micros), transcendentals=0
+        ),
         out_specs=vmem(len(outs)),
         scratch_shapes=list(scratch),
         compiler_params=pltpu.CompilerParams(vmem_limit_bytes=40 * 2**20),
@@ -134,92 +149,70 @@
     return (xp - p.cells_x * d) % p.xs
 
 
-def conv_body(p, first, count, table, *refs):
-    pieces, smooth, rim = refs[: p.ring], refs[p.ring], refs[p.ring + 1]
+def smooth_group(p, table, cg, pieces, g, store):
+    weights = [table[cg, pl.ds(t, 1), :] for t in range(ROW_WALL)]
+    for part in range(p.rows // 16):
+        cells = {}
+        for d in range(p.ring):
+            for xp in range(p.cells_x):
+                cells[cell_of(p, d, xp)] = pieces[d][g, xp, pl.ds(16 * part, 16), :].astype(F32)
+        for x in range(p.xs):
+            total = None
+            for j in range(TAPS):
+                line = None
+                for i in range(TAPS):
+                    term = weights[TAPS * i + j] * cells[(x + i - REACH) % p.xs]
+                    line = term if line is None else line + term
+                if j != REACH:
+                    line = pltpu.roll(line, (REACH - j) % LANES, 1)
+                total = line if total is None else total + line
+            store(x, 16 * part, total.astype(BF16))
+
+
+def activate(value):
+    sig = 0.5 * jnp.tanh(0.5 * value) + 0.5
+    act = value * sig
+    return act, sig + act * (1.0 - sig)
+
+
+def forward_body(p, first, count, last, table, bands, *refs):
+    refs = list(refs)
+
+    def take(number):
+        taken = refs[:number]
+        del refs[:number]
+        return taken
+
+    pieces = take(p.ring)
+    before = take(1 if first else 0)
+    rims = take(len(refs) - 6 if last else 0)
+    smooth, hidden, slope, score, rim, column = refs
     core = lax.axis_index("col")
+    blocks = p.reach_rows // 8
+    score[...] = before[0][...] if first else jnp.zeros_like(score)
+    for x in range(p.xs):
+        column[x, pl.ds(0, WALL_HALO), :] = jnp.zeros((WALL_HALO, LANES), F32)
+        column[x, pl.ds(WALL_HALO + p.rows, WALL_HALO), :] = jnp.zeros((WALL_HALO, LANES), F32)
+    base = 0
+    for other in rims:
+        rim[pl.ds(base, other.shape[0])] = other[...]
+        base += other.shape[0]
 
     def step(g, carry):
-        weights = [table[first + g, pl.ds(t, 1), :] for t in range(ROW_WALL)]
-        tops, lows = {}, {}
-        for part in range(p.rows // 16):
-            cells = {}
-            for d in range(p.ring):
-                for xp in range(p.cells_x):
-                    cells[cell_of(p, d, xp)] = pieces[d][g, xp, pl.ds(16 * part, 16), :].astype(F32)
-            for x in range(p.xs):
-                total = None
-                for j in range(TAPS):
-                    line = None
-                    for i in range(TAPS):
-                        term = weights[TAPS * i + j] * cells[(x + i - REACH) % p.xs]
-                        line = term if line is None else line + term
-                    if j != REACH:
-                        line = pltpu.roll(line, (REACH - j) % LANES, 1)
-                    total = line if total is None else total + line
-                smooth[g, x, pl.ds(16 * part, 16), :] = total.astype(BF16)
-                if part == 0:
-                    tops[x] = total[:8]
-                if part == p.rows // 16 - 1:
-                    lows[x] = total[8:]
+        cg = first + g
+
+        def store(x, row, value):
+            smooth[g, x, pl.ds(row, 16), :] = value
+            column[x, pl.ds(WALL_HALO + row, 16), :] = value.astype(F32)
+
+        smooth_group(p, table, cg, pieces, g, store)
         for pair in range(p.xs // 2):
-            top = jnp.concatenate([tops[2 * pair], tops[2 * pair + 1]], axis=0)
-            low = jnp.concatenate([lows[2 * pair], lows[2 * pair + 1]], axis=0)
-            rim[g, pair] = jnp.where(core == 0, low, top).astype(BF16)
-        return carry
-
-    lax.fori_loop(0, count, step, 0)
-
-
-def fill_column(p, core, smooth, rim, g, x, store):
-    store(WALL_HALO, p.rows, smooth[g, x].astype(F32))
-    near = rim[g, x // 2].astype(F32)[8 * (x % 2) : 8 * (x % 2) + 8]
-    store(0, WALL_HALO, jnp.where(core == 0, 0.0, near))
-    store(WALL_HALO + p.rows, WALL_HALO, jnp.where(core == 0, near, 0.0))
-
-
-def own_lanes(p, rows):
-    lane = lane_of(rows)
-    place = lane % p.block
-    return (place >= EDGE) & (place < EDGE + p.window) & (lane < p.per * p.block)
-
-
-def spread(p, value, lane):
-    total = value
-    for b in range(p.per - 1):
-        moved = pltpu.roll(value, LANES - p.block * (p.per - 1 - b), 1)
-        total = jnp.where(lane // p.block == b, moved, total)
-    return total
-
-
-def wall_body(p, cuts, table, bands, *refs):
-    count = len(cuts)
-    smooths, rims = refs[:count], refs[count : 2 * count]
-    refs = refs[2 * count :]
-    results = refs[: p.ring]
-    grad_smooth, grad_wall, hidden_out, errors_out = refs[p.ring : p.ring + 4]
-    column, hidden, slope, score, wall, field = refs[p.ring + 4 :]
-    core, me = lax.axis_index("col"), lax.axis_index("gx")
-    blocks = p.reach_rows // 8
-    lane = lane_of(8)
-    half = WALL // 2
-    all_rows = 2 * p.rows
-
-    for chunk, (first, last) in enumerate(cuts):
-
-        def fill(g, carry, chunk=chunk, first=first):
-            for x in range(p.xs):
-
-                def store(start, length, value, x=x):
-                    column[first + g, x, pl.ds(start, length), :] = value
-
-                fill_column(p, core, smooths[chunk], rims[chunk], g, x, store)
-            return carry
-
-        lax.fori_loop(0, last - first, fill, 0)
-
-    score[...] = jnp.zeros_like(score)
-
-    def forward(cg, carry):
+            cells = (2 * pair, 2 * pair + 1)
+            tops = [column[x, pl.ds(WALL_HALO, 8), :] for x in cells]
+            lows = [column[x, pl.ds(p.rows, 8), :] for x in cells]
+            rim[base + g, pair] = jnp.where(
+                core == 0, jnp.concatenate(lows, axis=0), jnp.concatenate(tops, axis=0)
+            ).astype(BF16)
         taps = [table[cg, pl.ds(ROW_WALL + k, 1), :] for k in range(WALL)]
         classes = [table[cg, pl.ds(ROW_CLASS + k, 1), :] for k in range(p.classes)]
         for blk in range(blocks):
@@ -228,26 +221,96 @@
             for k in range(WALL):
                 tap = taps[k] * bands[k, rows, :]
                 for x in range(p.xs):
-                    term = tap * column[cg, x, pl.ds(8 * blk + k, 8), :]
+                    term = tap * column[x, pl.ds(8 * blk + k, 8), :]
                     sums[x] = term if k == 0 else sums[x] + term
             for x in range(p.xs):
-                value = sums[x]
-                sig = 0.5 * jnp.tanh(0.5 * value) + 0.5
-                act = value * sig
-                hidden[cg, x, rows, :] = act
-                slope[cg, x, rows, :] = sig + act * (1.0 - sig)
+                hidden[g, x, rows, :], slope[g, x, rows, :] = act, _ = activate(sums[x])
                 for k in range(p.classes):
                     score[k, x, rows, :] += classes[k] * act
         return carry
 
-    lax.fori_loop(0, p.groups, forward, 0)
-
-    def judge(blk, carry):
+    lax.fori_loop(0, count, step, 0)
+
+
+def fill_column(p, core, smooth, rim, g, cg, x, store):
+    store(WALL_HALO, p.rows, smooth[g, x].astype(F32))
+    near = rim[cg, x // 2].astype(F32)[8 * (x % 2) : 8 * (x % 2) + 8]
+    store(0, WALL_HALO, jnp.where(core == 0, 0.0, near))
+    store(WALL_HALO + p.rows, WALL_HALO, jnp.where(core == 0, near, 0.0))
+
+
+def own_lanes(p, rows):
+    lane = lane_of(rows)
+    place = lane % p.block
+    return (place >= EDGE) & (place < EDGE + p.window) & (lane < p.per * p.block)
+
+
+def spread(p, value, lane):
+    total = value
+    for b in range(p.per - 1):
+        moved = pltpu.roll(value, LANES - p.block * (p.per - 1 - b), 1)
+        total = jnp.where(lane // p.block == b, moved, total)
+    return total
+
+
+def near_block(p, core):
+    return pl.multiple_of(jnp.where(core == 0, p.reach_rows - 8, 0), 8)
+
+
+def edge_rows(p, core, cuts, table, bands, smooths, rim, score, hidden_near, slope_near):
+    base = near_block(p, core)
+    rows = pl.ds(base, 8)
+    for k in range(p.classes):
+        for x in range(p.xs):
+            score[k, x, rows, :] = jnp.zeros((8, LANES), F32)
+
+    for chunk, (first, last) in enumerate(cuts):
+
+        def step(g, carry, chunk=chunk, first=first):
+            cg = first + g
+            taps = [
+                table[cg, pl.ds(ROW_WALL + k, 1), :] * bands[k, rows, :] for k in range(WALL)
+            ]
+            classes = [table[cg, pl.ds(ROW_CLASS + k, 1), :] for k in range(p.classes)]
+            for x in range(p.xs):
+                near = rim[cg, x // 2].astype(F32)[8 * (x % 2) : 8 * (x % 2) + 8]
+                low = smooths[chunk][g, x, pl.ds(p.rows - 16, 16), :].astype(F32)[8:]
+                top = smooths[chunk][g, x, pl.ds(0, 16), :].astype(F32)[:8]
+                hidden_near[cg, x] = jnp.where(core == 0, low, near)
+                slope_near[cg, x] = jnp.where(core == 0, near, top)
+            sums = []
+            for x in range(p.xs):
+                both = jnp.concatenate([hidden_near[cg, x], slope_near[cg, x]], axis=0)
+                total = taps[0] * both[:8]
+                for k in range(1, WALL):
+                    total = total + taps[k] * both[k : k + 8]
+                sums.append(total)
+            for x in range(p.xs):
+                act, bend = activate(sums[x])
+                hidden_near[cg, x], slope_near[cg, x] = act, bend
+                for k in range(p.classes):
+                    score[k, x, rows, :] += classes[k] * act
+            return carry
+
+        lax.fori_loop(0, last - first, step, 0)
+
+
+def judge(p, core, smooth, rim, score, errors, column):
+    lane = lane_of(8)
+    half = WALL // 2
+    for x in range(p.xs):
+
+        def store(start, length, value, x=x):
+            column[x, pl.ds(start, length), :] = value
+
+        fill_column(p, core, smooth, rim, smooth.shape[0] - 1, p.groups - 1, x, store)
+
+    def step(blk, carry):
         rows = pl.ds(pl.multiple_of(8 * blk, 8), 8)
         place = core * p.rows - half + 8 * blk + lax.broadcasted_iota(jnp.int32, (8, LANES), 0)
-        inside = (place >= 0) & (place < all_rows)
+        inside = (place >= 0) & (place < 2 * p.rows)
         for x in range(p.xs):
-            label = spread(p, column[p.groups - 1, x, pl.ds(8 * blk + half, 8), :], lane)
+            label = spread(p, column[x, pl.ds(8 * blk + half, 8), :], lane)
             for k in range(p.classes):
                 value = score[k, x, rows, :]
                 total = value
@@ -257,25 +320,42 @@
                 score[k, x, rows, :] = jnp.where(inside, error, 0.0)
         return carry
 
-    lax.fori_loop(0, blocks, judge, 0)
+    lax.fori_loop(0, p.reach_rows // 8, step, 0)
     own = own_lanes(p, p.rows)
     for k in range(p.classes):
         for x in range(p.xs):
-            errors_out[k, x] = jnp.where(own, score[k, x, pl.ds(half, p.rows), :], 0.0)
-
-    def backward(cg, carry):
+            errors[k, x] = jnp.where(own, score[k, x, pl.ds(half, p.rows), :], 0.0)
+
+
+def with_near(p, core, blk, value, near):
+    if blk == 0:
+        return jnp.where(core == 0, value, near)
+    if blk == p.reach_rows // 8 - 1:
+        return jnp.where(core == 0, near, value)
+    return value
+
+
+def backward_groups(
+    p, first, count, table, bands, score, slope, slope_near, grad_smooth, grad_wall, wall, field
+):
+    core = lax.axis_index("col")
+    half = WALL // 2
+    own = own_lanes(p, p.rows)
+
+    def step(g, carry):
+        cg = first + g
         taps = [table[cg, pl.ds(ROW_WALL + k, 1), :] for k in range(WALL)]
         classes = [table[cg, pl.ds(ROW_CLASS + k, 1), :] for k in range(p.classes)]
-        for blk in range(blocks):
+        for blk in range(p.reach_rows // 8):
             rows = pl.ds(8 * blk, 8)
             for x in range(p.xs):
                 grad = classes[0] * score[0, x, rows, :]
                 for k in range(1, p.classes):
                     grad = grad + classes[k] * score[k, x, rows, :]
-                wall[x, rows, :] = (grad * slope[cg, x, rows, :]).astype(BF16).astype(F32)
+                bend = with_near(p, core, blk, slope[g, x, rows, :], slope_near[cg, x])
+                wall[x, rows, :] = (grad * bend).astype(BF16).astype(F32)
         for x in range(p.xs):
-            grad_wall[cg, x] = jnp.where(own, wall[x, pl.ds(half, p.rows), :], 0.0).astype(BF16)
-            hidden_out[cg, x] = hidden[cg, x, pl.ds(half, p.rows), :].astype(BF16)
+            grad_wall[g, x] = jnp.where(own, wall[x, pl.ds(half, p.rows), :], 0.0).astype(BF16)
         for part in range(p.rows // 16):
             sums = [None] * p.xs
             for k in range(WALL):
@@ -285,11 +365,11 @@
                     term = tap * wall[x, rows, :]
                     sums[x] = term if k == 0 else sums[x] + term
             for x in range(p.xs):
-                grad_smooth[cg, x, pl.ds(16 * part, 16), :] = sums[x].astype(BF16)
+                grad_smooth[g, x, pl.ds(16 * part, 16), :] = sums[x].astype(BF16)
         weights = [table[cg, pl.ds(t, 1), :] for t in range(ROW_WALL)]
         for part in range(p.rows // 16):
             rows = pl.ds(16 * part, 16)
-            cells = [grad_smooth[cg, x, rows, :].astype(F32) for x in range(p.xs)]
+            cells = [grad_smooth[g, x, rows, :].astype(F32) for x in range(p.xs)]
             for x in range(p.xs):
                 total = None
                 for j in range(TAPS):
@@ -300,49 +380,80 @@
                     if j != REACH:
                         line = pltpu.roll(line, (j - REACH) % LANES, 1)
                     total = line if total is None else total + line
-                field[cg, x, rows, :] = total
+                field[g, x, rows, :] = total
         return carry
 
-    lax.fori_loop(0, p.groups, backward, 0)
-
-    wide = lane_of(p.rows)
-
-    def ship(pack, carry):
+    lax.fori_loop(0, count, step, 0)
+
+
+def ship(p, packs, field, results):
+    me = lax.axis_index("gx")
+    wide = lane_of(p.rows) // p.window
+
+    def step(pack, carry):
+        totals = [jnp.zeros((p.rows, LANES), F32)] * p.xs
         for b in range(p.ring):
             c = pack * p.ring + b
-            cg, at = c // p.per, c % p.per
             spot = lax.rem(b + me, p.ring)
-            shift = lax.rem(2 * LANES + p.window * spot - p.block * at - EDGE, LANES)
-            for d in range(p.ring):
-                for xp in range(p.cells_x):
-                    moved = pltpu.roll(field[cg, cell_of(p, d, xp)], shift, 1)
-                    held = column[0, cell_of(p, d, xp), pl.ds(0, p.rows), :]
-                    column[0, cell_of(p, d, xp), pl.ds(0, p.rows), :] = jnp.where(
-                        wide // p.window == spot, moved, held
-                    )
+            shift = lax.rem(2 * LANES + p.window * spot - p.block * (c % p.per) - EDGE, LANES)
+            for x in range(p.xs):
+                moved = pltpu.roll(field[c // p.per, x], shift, 1)
+                totals[x] = jnp.where(wide == spot, moved, totals[x])
         for d in range(p.ring):
             for xp in range(p.cells_x):
-                results[d][pack, xp] = column[0, cell_of(p, d, xp), pl.ds(0, p.rows), :].astype(
-                    BF16
-                )
+                results[d][pack, xp] = totals[cell_of(p, d, xp)].astype(BF16)
         return carry
 
-    lax.fori_loop(0, p.packs, ship, 0)
-
-
-def weight_body(p, cuts, bands, grad_smooth, grad_wall, hidden, errors, *refs):
+    lax.fori_loop(0, packs, step, 0)
+
+
+def backward_body(p, cuts, packs, table, bands, score_in, rim, *refs):
     count = len(cuts)
-    smooths, rims = refs[:count], refs[count : 2 * count]
-    refs = refs[2 * count :]
-    pieces = [refs[i * p.ring : (i + 1) * p.ring] for i in range(count)]
-    out, column, lines = refs[count * p.ring :]
+    smooths, slopes, refs = refs[:count], refs[count : 2 * count - 1], refs[2 * count - 1 :]
+    results, refs = refs[: p.ring], refs[p.ring :]
+    score, errors, hidden_near, slope_near = refs[:4]
+    grads = refs[4:-3]
+    wall, field, column = refs[-3:]
+    core = lax.axis_index("col")
+    score[...] = score_in[...]
+    edge_rows(p, core, cuts, table, bands, smooths, rim, score, hidden_near, slope_near)
+    judge(p, core, smooths[-1], rim, score, errors, column)
+    for i, (first, last) in enumerate(cuts[:-1]):
+        backward_groups(
+            p, first, last - first, table, bands, score, slopes[i], slope_near,
+            grads[i], grads[count - 1 + i], wall, field.at[pl.ds(first, last - first)],
+        )
+    ship(p, packs, field, results)
+
+
+def finish_body(
+    p, cuts, packs, table, bands, score, errors, hidden_near, slope_near, rim, slope, *refs
+):
+    count = len(cuts)
+    refs = list(refs)
+
+    def take(number):
+        taken = refs[:number]
+        del refs[:number]
+        return taken
+
+    hiddens, smooths = take(count), take(count)
+    pieces = [take(p.ring) for i in range(count)]
+    grad_smooths, grad_walls = take(count - 1), take(count - 1)
+    results = take(p.ring)
+    out, wall, field, last_smooth, last_wall, column, lines = refs
+    first, last = cuts[-1]
+    backward_groups(
+        p, first, last - first, table, bands, score, slope, slope_near, last_smooth, last_wall,
+        wall, field,
+    )
+    ship(p, packs, field, results)
+    grad_smooths, grad_walls = grad_smooths + [last_smooth], grad_walls + [last_wall]
+
     core = lax.axis_index("col")
     half = WALL // 2
     own = own_lanes(p, 16)
-    out[...] = jnp.zeros_like(out)
     lines[...] = jnp.zeros_like(lines)
-    lane = lane_of(LANES)
-    channel = lax.broadcasted_iota(jnp.int32, (LANES, LANES), 0)
 
     def fold(value):
         total = value[:8]
@@ -362,7 +473,7 @@
                     for xp in range(p.cells_x):
                         cells[cell_of(p, d, xp)] = pieces[chunk][d][g, xp, rows, :].astype(F32)
                 for x in range(p.xs):
-                    grad = jnp.where(own, grad_smooth[cg, x, rows, :].astype(F32), 0.0)
+                    grad = jnp.where(own, grad_smooths[chunk][g, x, rows, :].astype(F32), 0.0)
                     for j in range(TAPS):
                         moved = grad if j == REACH else pltpu.roll(grad, (j - REACH) % LANES, 1)
                         for i in range(TAPS):
@@ -371,45 +482,63 @@
                             term = term[:8] + term[8:]
                             sums[t] = term if sums[t] is None else sums[t] + term
             for t in range(ROW_WALL):
-                lines[pl.ds(t, 1), :] = fold(sums[t])
+                lines[cg, pl.ds(t, 1), :] = fold(sums[t])
             for x in range(p.xs):
 
                 def store(start, length, value, x=x):
                     column[x, pl.ds(start, length), :] = value
 
-                fill_column(p, core, smooths[chunk], rims[chunk], g, x, store)
-            grads = [grad_wall[cg, x].astype(F32) for x in range(p.xs)]
+                fill_column(p, core, smooths[chunk], rim, g, cg, x, store)
+            grads = [grad_walls[chunk][g, x].astype(F32) for x in range(p.xs)]
             for k in range(WALL):
                 total = None
                 for x in range(p.xs):
                     term = grads[x] * column[x, pl.ds(half + k, p.rows), :]
                     total = term if total is None else total + term
-                lines[pl.ds(ROW_WALL + k, 1), :] = fold(total * bands[k, pl.ds(half, p.rows), :])
+                lines[cg, pl.ds(ROW_WALL + k, 1), :] = fold(
+                    total * bands[k, pl.ds(half, p.rows), :]
+                )
+            for x in range(p.xs):
+                for blk in range(p.reach_rows // 8):
+                    rows = pl.ds(8 * blk, 8)
+                    wall[x, rows, :] = with_near(
+                        p, core, blk, hiddens[chunk][g, x, rows, :], hidden_near[cg, x]
+                    )
             for k in range(p.classes):
                 total = None
                 for x in range(p.xs):
-                    term = errors[k, x] * hidden[cg, x].astype(F32)
+                    term = errors[k, x] * wall[x, pl.ds(half, p.rows), :]
                     total = term if total is None else total + term
-                lines[pl.ds(ROW_CLASS + k, 1), :] = fold(total)
-            pick = (lane // p.block + cg * p.per == channel) & (lane < p.per * p.block)
-            out[...] += lax.dot_general(
-                lines[...],
-                jnp.where(pick, 1.0, 0.0),
-                (((1,), (1,)), ((), ())),
-                precision=lax.Precision.HIGHEST,
-                preferred_element_type=F32,
-            )
+                lines[cg, pl.ds(ROW_CLASS + k, 1), :] = fold(total)
             return carry
 
         lax.fori_loop(0, last - first, step, 0)
 
+    lane = lane_of(LANES)
+    channel = lax.broadcasted_iota(jnp.int32, (LANES, LANES), 0)
+    total = jnp.zeros((p.table_rows, LANES), F32)
+    for cg in range(p.groups):
+        pick = (lane // p.block + cg * p.per == channel) & (lane < p.per * p.block)
+        total = total + lax.dot_general(
+            lines[cg],
+            jnp.where(pick, 1.0, 0.0),
+            (((1,), (1,)), ((), ())),
+            precision=lax.Precision.HIGHEST,
+            preferred_element_type=F32,
+        )
+    out[...] = total
+
+
+def pass_body(value, *refs):
+    refs[-1][...] = value[...]
+
 
 def unpack_body(p, *refs):
-    pieces, out, stage = refs[: p.ring], refs[p.ring], refs[p.ring + 1]
+    out, stage = refs[-2:]
     me = lax.axis_index("gx")
     spot = lane_of(p.rows) // p.window
 
-    def step(pack, carry):
+    def step(pack, carry, pieces, base):
         for xp in range(p.cells_x):
             values = [pieces[d][pack, xp].astype(F32) for d in range(p.ring)]
             for b in range(p.ring):
@@ -419,10 +548,15 @@
                 total = pltpu.roll(total, (LANES - p.window * b) % LANES, 1) if b else total
                 stage[b, pl.ds(xp, p.rows, stride=p.cells_x), :] = total
         for b in range(p.ring):
-            out[pack * p.ring + b] = stage[b].astype(BF16)
+            out[(base + pack) * p.ring + b] = stage[b].astype(BF16)
         return carry
 
-    lax.fori_loop(0, p.packs, step, 0)
+    base = 0
+    for i in range(0, len(refs) - 2, p.ring):
+        pieces = refs[i : i + p.ring]
+        size = pieces[0].shape[0]
+        lax.fori_loop(0, size, functools.partial(step, pieces=pieces, base=base), 0)
+        base += size
 
 
 def rotation(size, by):
@@ -432,6 +566,19 @@
 def sum_over(value, axis):
     size = lax.axis_size(axis)
     return sum((lax.ppermute(value, axis, rotation(size, d)) for d in range(1, size)), value)
+
+
+def sum_near(value):
+    col, gz = lax.axis_size("col"), lax.axis_size("gz")
+    total = value
+    for d in range(1, col * gz):
+        pairs = [
+            (i * col + j, (i + d // col) % gz * col + (j + d) % col)
+            for i in range(gz)
+            for j in range(col)
+        ]
+        total = total + lax.ppermute(value, ("gz", "col"), pairs)
+    return total
 
 
 def band_rows(grid_index, stretch):
@@ -447,8 +594,7 @@
     p = Plan(ring, chans, rows, cells_x, cells_z, classes)
     volume = labels.shape[0] * cells_x * ring * cells_z * gz
     tall = rows * cells_x
-    middle = p.groups // 2
-    cuts = ((0, middle), (middle, p.groups))
+    cuts, packs = p.cuts()
 
     field = features.reshape(chans, tall, cells_z)
     marks = labels.reshape(labels.shape[0] * cells_x, cells_z)
@@ -487,58 +633,95 @@
         ((0, p.table_rows - table.shape[0]), (0, 0), (0, LANES - p.per * p.block)),
     ).transpose(1, 0, 2)
 
-    smooths, rims, pieces = [], [], []
+    def shape(*sizes, kind=BF16):
+        return jax.ShapeDtypeStruct(sizes, kind)
+
+    column = pltpu.VMEM((p.xs, rows + 2 * WALL_HALO, LANES), F32)
+    wall = pltpu.VMEM((p.xs, p.reach_rows, LANES), F32)
+    smooths, rims, pieces, hiddens, slopes, score = [], [], [], [], [], ()
     for chunk, (first, last) in enumerate(cuts):
+        size = last - first
         sent = windows[chunk * ring : (chunk + 1) * ring]
         got = [sent[0]] + [
             lax.ppermute(sent[d], "gx", rotation(ring, d)) for d in range(1, ring)
         ]
-        smooth, rim = call(
-            functools.partial(conv_body, p, first, last - first),
+        final = last == p.groups
+        smooth, hidden, slope, *score = call(
+            functools.partial(forward_body, p, first, size, final),
             [
-                jax.ShapeDtypeStruct((last - first, p.xs, rows, LANES), BF16),
-                jax.ShapeDtypeStruct((last - first, p.xs // 2, 16, LANES), BF16),
+                shape(size, p.xs, rows, LANES),
+                shape(size, p.xs, p.reach_rows, LANES, kind=F32),
+                shape(size, p.xs, p.reach_rows, LANES, kind=F32),
+                shape(classes, p.xs, p.reach_rows, LANES, kind=F32),
+                shape(p.groups if final else size, p.xs // 2, 16, LANES),
             ],
-            (table, *got),
+            (table, near, *got, *score[:1], *(rims if final else [])),
+            [column],
+            micros=0.001,
         )
-        smooths.append(smooth)
-        rims.append(lax.ppermute(rim, "col", rotation(2, 1)))
-        pieces += got
-
-    out_shapes = [jax.ShapeDtypeStruct((p.packs, cells_x, rows, LANES), BF16)] * ring + [
-        jax.ShapeDtypeStruct((p.groups, p.xs, rows, LANES), BF16),
-        jax.ShapeDtypeStruct((p.groups, p.xs, rows, LANES), BF16),
-        jax.ShapeDtypeStruct((p.groups, p.xs, rows, LANES), BF16),
-        jax.ShapeDtypeStruct((classes, p.xs, rows, LANES), F32),
+        rims.append(score[1])
+        smooths, pieces = smooths + [smooth], pieces + got
+        hiddens, slopes = hiddens + [hidden], slopes + [slope]
+    score = score[0]
+    rim = lax.ppermute(rims[-1], "col", rotation(2, 1))
+
+    sizes = [last - first for first, last in cuts]
+    early = sizes[:-1]
+    solved = call(
+        functools.partial(backward_body, p, cuts, packs[0]),
+        [shape(packs[0], cells_x, rows, LANES)] * ring
+        + [
+            shape(classes, p.xs, p.reach_rows, LANES, kind=F32),
+            shape(classes, p.xs, rows, LANES, kind=F32),
+            shape(p.groups, p.xs, 8, LANES, kind=F32),
+            shape(p.groups, p.xs, 8, LANES, kind=F32),
+        ]
+        + [shape(size, p.xs, rows, LANES) for size in early] * 2,
+        (table, near, score, rim, *smooths, *slopes[:-1]),
+        [wall, pltpu.VMEM((sum(early), p.xs, rows, LANES), F32), column],
+        micros=5,
+    )
+    sent, solved = solved[:ring], solved[ring:]
+    score, errors, hidden_near, slope_near, *grads = solved
+    back = [sent[0]] + [
+        lax.ppermute(sent[d], "gx", rotation(ring, -d)) for d in range(1, ring)
     ]
-    solved = call(
-        functools.partial(wall_body, p, cuts),
-        out_shapes,
-        (table, near, *smooths, *rims),
+    *sent, sums = call(
+        functools.partial(finish_body, p, cuts, packs[1]),
+        [shape(packs[1], cells_x, rows, LANES)] * ring + [shape(p.table_rows, LANES, kind=F32)],
+        (
+            *(table, near, score, errors, hidden_near, slope_near, rim, slopes[-1]),
+            *hiddens, *smooths, *pieces, *grads,
+        ),
         [
-            pltpu.VMEM((p.groups, p.xs, rows + 2 * WALL_HALO, LANES), F32),
-            pltpu.VMEM((p.groups, p.xs, p.reach_rows, LANES), F32),
-            pltpu.VMEM((p.groups, p.xs, p.reach_rows, LANES), F32),
-            pltpu.VMEM((classes, p.xs, p.reach_rows, LANES), F32),
-            pltpu.VMEM((p.xs, p.reach_rows, LANES), F32),
-            pltpu.VMEM((p.groups, p.xs, rows, LANES), F32),
+            wall,
+            pltpu.VMEM((sizes[-1], p.xs, rows, LANES), F32),
+            pltpu.VMEM((sizes[-1], p.xs, rows, LANES), BF16),
+            pltpu.VMEM((sizes[-1], p.xs, rows, LANES), BF16),
+            column,
+            pltpu.VMEM((p.groups, p.table_rows, LANES), F32),
         ],
-    )
-    results, (grad_smooth, grad_wall, hidden, errors) = solved[:ring], solved[ring:]
-    back = [results[0]] + [
-        lax.ppermute(results[d], "gx", rotation(ring, -d)) for d in range(1, ring)
+        micros=0.01,
+    )
+    (sums,) = call(
+        pass_body,
+        [shape(p.table_rows, LANES, kind=F32)],
+        (sums, *back[1:]),
+        micros=0.1,
+        unread=ring - 1,
+    )
+    back += [sent[0]] + [
+        lax.ppermute(sent[d], "gx", rotation(ring, -d)) for d in range(1, ring)
     ]
+    sums = sum_over(sums, "gx")
     (sums,) = call(
-        functools.partial(weight_body, p, cuts),
-        [jax.ShapeDtypeStruct((p.table_rows, LANES), F32)],
-        (near, grad_smooth, grad_wall, hidden, errors, *smooths, *rims, *pieces),
-        [
-            pltpu.VMEM((p.xs, rows + 2 * WALL_HALO, LANES), F32),
-            pltpu.VMEM((p.table_rows, LANES), F32),
-        ],
-    )
-    for axis in ("col", "gz", "gx"):
-        sums = sum_over(sums, axis)
+        pass_body,
+        [shape(p.table_rows, LANES, kind=F32)],
+        (sums, *back[ring + 1 :]),
+        micros=0.1,
+        unread=ring - 1,
+    )
+    sums = sum_near(sums)
     sums = sums / volume
     (grad_field,) = call(
         functools.partial(unpack_body, p),

time: 75.8 us -> 76.6 us (1.011)
  starting transfers between devices: 23.3 us -> 34.2 us
  waiting for transfers between devices: 19.5 us -> 8.77 us
  local copies, waits for them, and re-layouts: 6.5 us -> 7.54 us
    ppermute x6 -> x9, starting transfers between devices: 9.99 us -> 17.4 us  [by_windows(): lax.ppermute(sent[d], 'gx', rotation(ring, d))]
    ppermute x5 -> x10, starting transfers between devices: 4.46 us -> 10 us  [the longest x6 8.11 us: by_windows(): lax.ppermute(sent[d], 'gx', rotation(ring, -d))]
    ppermute x6 -> x9, waiting for transfers between devices: 6.06 us -> 0.95 us  [by_windows(): lax.ppermute(sent[d], 'gx', rotation(ring, d))]
    ppermute x5 -> x3, waiting for transfers between devices: 4.34 us -> 1.19 us  [sum_over(): lax.ppermute(value, axis, rotation(size, d))]
    ppermute x5 -> x10, waiting for transfers between devices: 8.72 us -> 6.62 us  [the longest x6 4.9 us: by_windows(): lax.ppermute(sent[d], 'gx', rotation(ring, -d))]
    ppermute x5 -> x3, starting transfers between devices: 5.9 us -> 3.9 us  [sum_over(): lax.ppermute(value, axis, rotation(size, d))]
    unnamed x20, local copies, waits for them, and re-layouts: 3.97 us -> 5.02 us
    pallas_call x7 -> x10, Pallas kernels: 25.2 us -> 24.7 us  [call(): pl.pallas_call(body, out_shape=outs, in_specs=vmem(len(args) - unread) +...]
  transfers between devices with their start and end apart: 17 -> 23, of which waited for: 10 -> 8; matrix products, arithmetic and copies ran while one was open for 5% -> 2% of each run, Pallas kernels for 4% -> 18%
where the time goes in v2:
time: 76.6 us; the launch traced here: 76.3 us
  starting transfers between devices  34.2 us (45%)
  Pallas kernels  24.7 us (32%)
  waiting for transfers between devices  8.77 us (11%)
  local copies, waits for them, and re-layouts  7.54 us (10%)
  between operations  0.84 us (1%)
    pallas_call x10, Pallas kernels, call(): pl.pallas_call(body, out_shape=outs, in_specs=vmem(len(args) - unread) +...  24.7 us
    ppermute x9, starting transfers between devices, by_windows(): lax.ppermute(sent[d], 'gx', rotation(ring, d))  17.4 us
    ppermute x6, starting transfers between devices, by_windows(): lax.ppermute(sent[d], 'gx', rotation(ring, -d))  8.11 us
    unnamed x20, local copies, waits for them, and re-layouts  5.02 us
    ppermute x6, waiting for transfers between devices, by_windows(): lax.ppermute(sent[d], 'gx', rotation(ring, -d))  4.9 us
    ppermute x3, starting transfers between devices, sum_over(): lax.ppermute(value, axis, rotation(size, d))  3.9 us
    ppermute x1, starting transfers between devices, by_windows(): left = lax.ppermute(edge, 'gz', rotation(gz, 1))  2.95 us
    ppermute x3, starting transfers between devices, sum_near(): total = total + lax.ppermute(value, ('gz', 'col'), pairs)  1.85 us
  transfers between devices with their start and end apart: 23, of which 8 were waited for; matrix products, arithmetic and copies ran while one was open for 2% of the time, Pallas kernels for 18%

profile of v2, /device:TPU:0, one launch (start us, length us, event | category | flops | bytes accessed | tf_op | source)
XLA Modules:
  0.0 76.3 jit_solution(4625675960043161602)
XLA Ops:
  0.7 1.0 %copy-done.1 = bf16[32,32,2,128]{3,2,1,0:T(2,128)(2,1)S(1)} copy-done((bf16[32,32,2,128]{3,2,1,0:T(2,128)(2,1)S(1)}, bf16[32,32,2,128]{3,2,1,0:T(2,128)(2,1)}, u32[]{:S(2)}) %copy-start.1) | copy-done | bytes 524312
  1.7 0.8 %copy-done.3 = s32[64,2,128]{2,1,0:T(2,128)S(1)} copy-done((s32[64,2,128]{2,1,0:T(2,128)S(1)}, s32[64,2,128]{2,1,0:T(2,128)}, u32[]{:S(2)}) %copy-start.3) | copy-done | bytes 65560
  2.5 0.3 shard_map.102
  2.9 3.0 %collective-permute-start = (bf16[3,64,128]{2,1,0:T(8,128)(2,1)S(1)}, bf16[3,64,128]{2,1,0:T(8,128)(2,1)S(1)}, u32[]{:S(2)}, u32[]{:S(2)}) collective-permute-start(bf16[3,64,128]{2,1,0:T(8,128)(2,1)S(1)} %shard_map.102), channel_id=1, source_target_pairs={{0,2},{2,0},{1,3},{3,1},{4,6},{6,4},{5,7},{7,5},{8,10},{10,8},{9,1... | collective-permute-start | bytes 147464 | tf_op jit(solution)/shard_map/ppermute | solution.py:606
  5.9 0.6 copy-done.7
  6.6 0.6 copy-done.8
  7.2 0.2 fusion
  7.4 0.5 copy-done.5
  8.0 0.2 copy.17
  8.2 0.5 broadcast_in_dim.7
  8.7 0.4 reshape.34
  9.1 0.7 copy-done.2
  9.7 2.3 %shard_map.103 = (bf16[4,2,32,128]{3,2,1,0:T(8,128)(2,1)S(1)}, bf16[4,2,32,128]{3,2,1,0:T(8,128)(2,1)S(1)}, bf16[4,2,32,128]{3,2,1,0:T(8,128)(2,1)S(1)}, bf16[4,...) custom-call(bf16[32,64,128]{2,1,0:T(8,128)(2,1)S(1)} %bitcast.19, ...), custom_call_target="tpu_custom_call" | custom-call | bytes 3000000 | tf_op jit(solution)/shard_map/pallas_call | solution.py:64
  12.1 1.6 %collective-permute-start.4 = (bf16[4,2,32,128]{3,2,1,0:T(8,128)(2,1)S(1)}, bf16[4,2,32,128]{3,2,1,0:T(8,128)(2,1)S(1)}, u32[]{:S(2)}, u32[]{:S(2)}) collective-permute-start(bf16[4,2,32,128]{3,2,1,0:T(8,128)(2,1)S(1)} %get-tuple-element.53), channel_id=1, source_target_pairs={{0,4},{4,8},{8,12},{12,0},{1,5},{5,9},{9,13},{13,1},{2,6},{6,10},{... | collective-permute-start | bytes 196616 | tf_op jit(solution)/shard_map/ppermute | solution.py:646
  13.7 1.6 %collective-permute-start.7 = (bf16[4,2,32,128]{3,2,1,0:T(8,128)(2,1)S(1)}, bf16[4,2,32,128]{3,2,1,0:T(8,128)(2,1)S(1)}, u32[]{:S(2)}, u32[]{:S(2)}) collective-permute-start(bf16[4,2,32,128]{3,2,1,0:T(8,128)(2,1)S(1)} %get-tuple-element.57), channel_id=1, source_target_pairs={{0,4},{4,8},{8,12},{12,0},{1,5},{5,9},{9,13},{13,1},{2,6},{6,10},{... | collective-permute-start | bytes 196616 | tf_op jit(solution)/shard_map/ppermute | solution.py:646
  15.3 1.2 %collective-permute-start.8 = (bf16[4,2,32,128]{3,2,1,0:T(8,128)(2,1)S(1)}, bf16[4,2,32,128]{3,2,1,0:T(8,128)(2,1)S(1)}, u32[]{:S(2)}, u32[]{:S(2)}) collective-permute-start(bf16[4,2,32,128]{3,2,1,0:T(8,128)(2,1)S(1)} %get-tuple-element.58), channel_id=1, source_target_pairs={{0,8},{4,12},{8,0},{12,4},{1,9},{5,13},{9,1},{13,5},{2,10},{6,14},... | collective-permute-start | bytes 196616 | tf_op jit(solution)/shard_map/ppermute | solution.py:646
  16.5 2.7 %collective-permute-start.9 = (bf16[4,2,32,128]{3,2,1,0:T(8,128)(2,1)S(1)}, bf16[4,2,32,128]{3,2,1,0:T(8,128)(2,1)S(1)}, u32[]{:S(2)}, u32[]{:S(2)}) collective-permute-start(bf16[4,2,32,128]{3,2,1,0:T(8,128)(2,1)S(1)} %get-tuple-element.59), channel_id=1, source_target_pairs={{0,12},{4,0},{8,4},{12,8},{1,13},{5,1},{9,5},{13,9},{2,14},{6,2},{... | collective-permute-start | bytes 196616 | tf_op jit(solution)/shard_map/ppermute | solution.py:646
  19.3 1.0 %collective-permute-start.2 = (bf16[3,2,32,128]{3,2,1,0:T(8,128)(2,1)S(1)}, bf16[3,2,32,128]{3,2,1,0:T(8,128)(2,1)S(1)}, u32[]{:S(2)}, u32[]{:S(2)}) collective-permute-start(bf16[3,2,32,128]{3,2,1,0:T(8,128)(2,1)S(1)} %get-tuple-element.50), channel_id=1, source_target_pairs={{0,8},{4,12},{8,0},{12,4},{1,9},{5,13},{9,1},{13,5},{2,10},{6,14},... | collective-permute-start | bytes 147464 | tf_op jit(solution)/shard_map/ppermute | solution.py:646
  20.3 0.2 collective-permute-done.7.refs_1_.refs_7_
  20.5 2.6 %collective-permute-start.3 = (bf16[3,2,32,128]{3,2,1,0:T(8,128)(2,1)S(1)}, bf16[3,2,32,128]{3,2,1,0:T(8,128)(2,1)S(1)}, u32[]{:S(2)}, u32[]{:S(2)}) collective-permute-start(bf16[3,2,32,128]{3,2,1,0:T(8,128)(2,1)S(1)} %get-tuple-element.51), channel_id=1, source_target_pairs={{0,12},{4,0},{8,4},{12,8},{1,13},{5,1},{9,5},{13,9},{2,14},{6,2},{... | collective-permute-start | bytes 147464 | tf_op jit(solution)/shard_map/ppermute | solution.py:646
  23.2 2.0 %collective-permute-start.5 = (bf16[4,2,32,128]{3,2,1,0:T(8,128)(2,1)S(1)}, bf16[4,2,32,128]{3,2,1,0:T(8,128)(2,1)S(1)}, u32[]{:S(2)}, u32[]{:S(2)}) collective-permute-start(bf16[4,2,32,128]{3,2,1,0:T(8,128)(2,1)S(1)} %get-tuple-element.54), channel_id=1, source_target_pairs={{0,8},{4,12},{8,0},{12,4},{1,9},{5,13},{9,1},{13,5},{2,10},{6,14},... | collective-permute-start | bytes 196616 | tf_op jit(solution)/shard_map/ppermute | solution.py:646
  25.1 4.6 %collective-permute-start.6 = (bf16[4,2,32,128]{3,2,1,0:T(8,128)(2,1)S(1)}, bf16[4,2,32,128]{3,2,1,0:T(8,128)(2,1)S(1)}, u32[]{:S(2)}, u32[]{:S(2)}) collective-permute-start(bf16[4,2,32,128]{3,2,1,0:T(8,128)(2,1)S(1)} %get-tuple-element.55), channel_id=1, source_target_pairs={{0,12},{4,0},{8,4},{12,8},{1,13},{5,1},{9,5},{13,9},{2,14},{6,2},{... | collective-permute-start | bytes 196616 | tf_op jit(solution)/shard_map/ppermute | solution.py:646
  29.9 1.9 %shard_map.104 = (bf16[4,8,32,128]{3,2,1,0:T(8,128)(2,1)S(1)}, f32[4,8,40,128]{3,2,1,0:T(8,128)S(1)}, f32[4,8,40,128]{3,2,1,0:T(8,128)S(1)}, f32[4,8,40,128]{3,2,1,0:T(8,128)S(1)}, bf16[4,4,16,128]{3,2,1,0:T(8,128)(2,1)S(1)}) custom-call(f32[11,40,128]{2,1,0:T(8,128)S(1)} %pad_bitcast_fusion.table, f32[9,40,128]{2,1,0:T(8,128)S(1)} %broadcast_in_dim.8.bands, ...), custom_call_target="tpu_custom_call" | custom-call | bytes 3000 | tf_op jit(solution)/shard_map/pallas_call | solution.py:64
  31.8 0.7 collective-permute-done.6.refs_3_.refs_13_
  32.5 1.9 %shard_map.105 = (bf16[4,8,32,128]{3,2,1,0:T(8,128)(2,1)S(1)}, f32[4,8,40,128]{3,2,1,0:T(8,128)S(1)}, f32[4,8,40,128]{3,2,1,0:T(8,128)S(1)}, f32[4,8,40,128]{3,2,1,0:T(8,128)S(1)}, bf16[4,4,16,128]{3,2,1,0:T(8,128)(2,1)S(1)}) custom-call(f32[11,40,128]{2,1,0:T(8,128)S(1)} %pad_bitcast_fusion.table, f32[9,40,128]{2,1,0:T(8,128)S(1)} %broadcast_in_dim.8.bands, ...), custom_call_target="tpu_custom_call" | custom-call | bytes 3000 | tf_op jit(solution)/shard_map/pallas_call | solution.py:64
  34.4 1.5 %shard_map.106 = (bf16[3,8,32,128]{3,2,1,0:T(8,128)(2,1)S(1)}, f32[3,8,40,128]{3,2,1,0:T(8,128)S(1)}, f32[3,8,40,128]{3,2,1,0:T(8,128)S(1)}, f32[4,8,40,128]{3,2,1,0:T(8,128)S(1)}, bf16[11,4,16,128]{3,2,1,0:T(8,128)(2,1)S(1)}) custom-call(f32[11,40,128]{2,1,0:T(8,128)S(1)} %pad_bitcast_fusion.table, f32[9,40,128]{2,1,0:T(8,128)S(1)} %broadcast_in_dim.8.bands, ...), custom_call_target="tpu_custom_call" | custom-call | bytes 3000 | tf_op jit(solution)/shard_map/pallas_call | solution.py:64
  36.0 1.4 %collective-permute-done.10.rim = bf16[11,4,16,128]{3,2,1,0:T(8,128)(2,1)S(1)} collective-permute-done((bf16[11,4,16,128]{3,2,1,0:T(8,128)(2,1)S(1)}, bf16[11,4,16,128]{3,2,1,0:T(8,128)(2,1)S(1)}, u32[]{:S(2)}, u32[]{:S(2)}) %collective-permute-start.10) | collective-permute-done | bytes 180256 | tf_op jit(solution)/shard_map/ppermute | solution.py:666
  37.4 7.1 %shard_map.107 = (bf16[6,2,32,128]{3,2,1,0:T(8,128)(2,1)S(1)}, bf16[6,2,32,128]{3,2,1,0:T(8,128)(2,1)S(1)}, bf16[6,2,32,128]{3,2,1,0:T(8,128)(2,1)S(1)}, bf16[6,...) custom-call(f32[11,40,128]{2,1,0:T(8,128)S(1)} %pad_bitcast_fusion.t, ...), custom_call_target="tpu_custom_call" | custom-call | bytes 15000000 | tf_op jit(solution)/shard_map/pallas_call | solution.py:64
  44.5 3.3 %collective-permute-start.11 = (bf16[6,2,32,128]{3,2,1,0:T(8,128)(2,1)S(1)}, bf16[6,2,32,128]{3,2,1,0:T(8,128)(2,1)S(1)}, u32[]{:S(2)}, u32[]{:S(2)}) collective-permute-start(bf16[6,2,32,128]{3,2,1,0:T(8,128)(2,1)S(1)} %get-tuple-element.72), channel_id=1, source_target_pairs={{0,12},{4,0},{8,4},{12,8},{1,13},{5,1},{9,5},{13,9},{2,14},{6,2},{... | collective-permute-start | bytes 294920 | tf_op jit(solution)/shard_map/ppermute | solution.py:687
  47.8 0.2 collective-permute-start.12
  48.1 0.4 collective-permute-start.13
  48.5 8.0 %shard_map.108 = (bf16[2,2,32,128]{3,2,1,0:T(8,128)(2,1)S(1)}, bf16[2,2,32,128]{3,2,1,0:T(8,128)(2,1)S(1)}, bf16[2,2,32,128]{3,2,1,0:T(8,128)(2,1)S(1)}, bf16[2,...) custom-call(f32[11,40,128]{2,1,0:T(8,128)S(1)} %pad_bitcast_fusion.table, f32[9,40,128]{2,1,0:T(8,128)S(1)} %broadcast_in_dim.8.bands, ...), custom_call_target="tpu_custom_call" | custom-call | bytes 30000 | tf_op jit(solution)/shard_map/pallas_call | solution.py:64
  56.5 0.7 collective-permute-done.12.refs_2_.refs_1_
  57.2 2.8 %collective-permute-start.19 = (f32[40,128]{1,0:T(8,128)S(1)}, f32[40,128]{1,0:T(8,128)S(1)}, u32[]{:S(2)}, u32[]{:S(2)}) collective-permute-start(f32[40,128]{1,0:T(8,128)S(1)} %shard_map.110), channel_id=1, source_target_pairs={{0,12},{4,0},{8,4},{12,8},{1,13},{5,1},{9,5},{13,9},{2,14},{6,2},{... | collective-permute-start | bytes 61448 | tf_op jit(solution)/shard_map/ppermute | solution.py:568
  60.0 0.9 %collective-permute-start.18 = (f32[40,128]{1,0:T(8,128)S(1)}, f32[40,128]{1,0:T(8,128)S(1)}, u32[]{:S(2)}, u32[]{:S(2)}) collective-permute-start(f32[40,128]{1,0:T(8,128)S(1)} %shard_map.110), channel_id=1, source_target_pairs={{0,8},{4,12},{8,0},{12,4},{1,9},{5,13},{9,1},{13,5},{2,10},{6,14},... | collective-permute-start | bytes 61448 | tf_op jit(solution)/shard_map/ppermute | solution.py:568
  60.9 0.2 collective-permute-start.17
  61.1 3.6 %collective-permute-start.14 = (bf16[2,2,32,128]{3,2,1,0:T(8,128)(2,1)S(1)}, bf16[2,2,32,128]{3,2,1,0:T(8,128)(2,1)S(1)}, u32[]{:S(2)}, u32[]{:S(2)}) collective-permute-start(bf16[2,2,32,128]{3,2,1,0:T(8,128)(2,1)S(1)} %get-tuple-element.88), channel_id=1, source_target_pairs={{0,12},{4,0},{8,4},{12,8},{1,13},{5,1},{9,5},{13,9},{2,14},{6,2},{... | collective-permute-start | bytes 98312 | tf_op jit(solution)/shard_map/ppermute | solution.py:714
  64.7 0.2 collective-permute-start.15
  64.9 0.3 collective-permute-start.16
  65.3 1.2 %collective-permute-done.17 = f32[40,128]{1,0:T(8,128)S(1)} collective-permute-done((f32[40,128]{1,0:T(8,128)S(1)}, f32[40,128]{1,0:T(8,128)S(1)}, u32[]{:S(2)}, u32[]{:S(2)}) %collective-permute-start.17) | collective-permute-done | bytes 20512 | tf_op jit(solution)/shard_map/ppermute | solution.py:568
  66.5 3.0 %collective-permute-done.15.refs_6_.refs_1_ = bf16[2,2,32,128]{3,2,1,0:T(8,128)(2,1)S(1)} collective-permute-done((bf16[2,2,32,128]{3,2,1,0:T(8,128)(2,1)S(1)}, bf16[2,2,32,128]{3,2,1,0:T(8,128)(2,1)S(1)}, u32[]{:S(2)}, u32[]{:S(2)}) %collective-permute-start.15) | collective-permute-done | bytes 32800 | tf_op jit(solution)/shard_map/ppermute | solution.py:714
  69.5 1.1 %collective-permute-done.16.refs_7_.refs_2_ = bf16[2,2,32,128]{3,2,1,0:T(8,128)(2,1)S(1)} collective-permute-done((bf16[2,2,32,128]{3,2,1,0:T(8,128)(2,1)S(1)}, bf16[2,2,32,128]{3,2,1,0:T(8,128)(2,1)S(1)}, u32[]{:S(2)}, u32[]{:S(2)}) %collective-permute-start.16) | collective-permute-done | bytes 32800 | tf_op jit(solution)/shard_map/ppermute | solution.py:714
  70.6 1.8 %collective-permute-start.20 = (f32[40,128]{1,0:T(8,128)S(1)}, f32[40,128]{1,0:T(8,128)S(1)}, u32[]{:S(2)}, u32[]{:S(2)}) collective-permute-start(f32[40,128]{1,0:T(8,128)S(1)} %shard_map.111), channel_id=1, source_target_pairs={{0,1},{1,0},{2,3},{3,2},{4,5},{5,4},{6,7},{7,6},{8,9},{9,8},{10,11... | collective-permute-start | bytes 61448 | tf_op jit(solution)/shard_map/ppermute | solution.py:580
  72.5 1.6 %shard_map.109 = bf16[32,64,128]{2,1,0:T(8,128)(2,1)} custom-call(bf16[6,2,32,128]{3,2,1,0:T(8,128)(2,1)S(1)} %get-tuple-element.71.refs_0_, bf16[6,2,32,128]{3,2,1,0:T(8,128)(2,1)S(1)} %collective-permute-done.11.refs_1_.refs_0_, bf16[6,2,32,128]{3,2,1,0:T(8,128)(2,1)S(1)} %collective-permute-done.12.refs_2_.refs_1_, ...), custom_call_target="tpu_custom_call" | custom-call | bytes 3000000 | tf_op jit(solution)/shard_map/pallas_call | solution.py:64
  74.1 0.3 collective-permute-done.21
  74.5 0.6 slice.14
  75.0 0.6 slice_bitcast_fusion.1
  75.7 0.7 copy.18
  (44 shorter events, 0.7 us)
Async XLA Ops:
  0.6 6.0 %copy-start = (f32[16,9]{1,0:T(8,128)S(1)}, f32[16,9]{1,0:T(8,128)}, u32[]{:S(2)}) copy-start(f32[16,9]{1,0:T(8,128)} %param.10) | copy-start | bytes 1732
  0.6 1.0 %copy-start.1 = (bf16[32,32,2,128]{3,2,1,0:T(2,128)(2,1)S(1)}, bf16[32,32,2,128]{3,2,1,0:T(2,128)(2,1)}, u32[]{:S(2)}) copy-start(bf16[32,32,2,128]{3,2,1,0:T(2,128)(2,1)} %param.7) | copy-start | bytes 1572868
  1.7 0.8 %copy-start.3 = (s32[64,2,128]{2,1,0:T(2,128)S(1)}, s32[64,2,128]{2,1,0:T(2,128)}, u32[]{:S(2)}) copy-start(s32[64,2,128]{2,1,0:T(2,128)} %param.8) | copy-start | bytes 196612
  2.5 3.3 %copy-start.6 = (f32[32,9]{0,1:T(8,128)S(1)}, f32[32,9]{0,1:T(8,128)}, u32[]{:S(2)}) copy-start(f32[32,9]{0,1:T(8,128)} %param.12) | copy-start | bytes 3460
  2.9 6.2 %collective-permute-start = (bf16[3,64,128]{2,1,0:T(8,128)(2,1)S(1)}, bf16[3,64,128]{2,1,0:T(8,128)(2,1)S(1)}, u32[]{:S(2)}, u32[]{:S(2)}) collective-permute-start(bf16[3,64,128]{2,1,0:T(8,128)(2,1)S(1)} %shard_map.102), channel_id=1, source_target_pairs={{0,2},{2,0},{1,3},{3,1},{4,6},{6,4},{5,7},{7,5},{8,10},{10,8},{9,1... | collective-permute-start | bytes 147464 | tf_op jit(solution)/shard_map/ppermute | solution.py:606
  5.8 0.7 copy-start.7
  6.5 0.7 copy-start.8
  7.2 0.7 copy-start.5
  8.7 1.0 %copy-start.2 = (bf16[32,32,2,128]{3,2,1,0:T(2,128)(2,1)S(1)}, bf16[32,32,2,128]{3,2,1,0:T(2,128)(2,1)}, u32[]{:S(2)}) copy-start(bf16[32,32,2,128]{3,2,1,0:T(2,128)(2,1)} %param.7) | copy-start | bytes 1572868
  8.7 1.0 %copy-start.4 = (s32[64,2,128]{2,1,0:T(2,128)S(1)}, s32[64,2,128]{2,1,0:T(2,128)}, u32[]{:S(2)}) copy-start(s32[64,2,128]{2,1,0:T(2,128)} %param.8) | copy-start | bytes 196612
  12.1 7.2 %collective-permute-start.4 = (bf16[4,2,32,128]{3,2,1,0:T(8,128)(2,1)S(1)}, bf16[4,2,32,128]{3,2,1,0:T(8,128)(2,1)S(1)}, u32[]{:S(2)}, u32[]{:S(2)}) collective-permute-start(bf16[4,2,32,128]{3,2,1,0:T(8,128)(2,1)S(1)} %get-tuple-element.53), channel_id=1, source_target_pairs={{0,4},{4,8},{8,12},{12,0},{1,5},{5,9},{9,13},{13,1},{2,6},{6,10},{... | collective-permute-start | bytes 196616 | tf_op jit(solution)/shard_map/ppermute | solution.py:646
  13.7 6.8 %collective-permute-start.7 = (bf16[4,2,32,128]{3,2,1,0:T(8,128)(2,1)S(1)}, bf16[4,2,32,128]{3,2,1,0:T(8,128)(2,1)S(1)}, u32[]{:S(2)}, u32[]{:S(2)}) collective-permute-start(bf16[4,2,32,128]{3,2,1,0:T(8,128)(2,1)S(1)} %get-tuple-element.57), channel_id=1, source_target_pairs={{0,4},{4,8},{8,12},{12,0},{1,5},{5,9},{9,13},{13,1},{2,6},{6,10},{... | collective-permute-start | bytes 196616 | tf_op jit(solution)/shard_map/ppermute | solution.py:646
  15.3 7.9 %collective-permute-start.8 = (bf16[4,2,32,128]{3,2,1,0:T(8,128)(2,1)S(1)}, bf16[4,2,32,128]{3,2,1,0:T(8,128)(2,1)S(1)}, u32[]{:S(2)}, u32[]{:S(2)}) collective-permute-start(bf16[4,2,32,128]{3,2,1,0:T(8,128)(2,1)S(1)} %get-tuple-element.58), channel_id=1, source_target_pairs={{0,8},{4,12},{8,0},{12,4},{1,9},{5,13},{9,1},{13,5},{2,10},{6,14},... | collective-permute-start | bytes 196616 | tf_op jit(solution)/shard_map/ppermute | solution.py:646
  16.5 8.6 %collective-permute-start.9 = (bf16[4,2,32,128]{3,2,1,0:T(8,128)(2,1)S(1)}, bf16[4,2,32,128]{3,2,1,0:T(8,128)(2,1)S(1)}, u32[]{:S(2)}, u32[]{:S(2)}) collective-permute-start(bf16[4,2,32,128]{3,2,1,0:T(8,128)(2,1)S(1)} %get-tuple-element.59), channel_id=1, source_target_pairs={{0,12},{4,0},{8,4},{12,8},{1,13},{5,1},{9,5},{13,9},{2,14},{6,2},{... | collective-permute-start | bytes 196616 | tf_op jit(solution)/shard_map/ppermute | solution.py:646
  19.2 15.2 %collective-permute-start.1 = (bf16[3,2,32,128]{3,2,1,0:T(8,128)(2,1)S(1)}, bf16[3,2,32,128]{3,2,1,0:T(8,128)(2,1)S(1)}, u32[]{:S(2)}, u32[]{:S(2)}) collective-permute-start(bf16[3,2,32,128]{3,2,1,0:T(8,128)(2,1)S(1)} %get-tuple-element.49), channel_id=1, source_target_pairs={{0,4},{4,8},{8,12},{12,0},{1,5},{5,9},{9,13},{13,1},{2,6},{6,10},{... | collective-permute-start | bytes 147464 | tf_op jit(solution)/shard_map/ppermute | solution.py:646
  19.3 15.1 %collective-permute-start.2 = (bf16[3,2,32,128]{3,2,1,0:T(8,128)(2,1)S(1)}, bf16[3,2,32,128]{3,2,1,0:T(8,128)(2,1)S(1)}, u32[]{:S(2)}, u32[]{:S(2)}) collective-permute-start(bf16[3,2,32,128]{3,2,1,0:T(8,128)(2,1)S(1)} %get-tuple-element.50), channel_id=1, source_target_pairs={{0,8},{4,12},{8,0},{12,4},{1,9},{5,13},{9,1},{13,5},{2,10},{6,14},... | collective-permute-start | bytes 147464 | tf_op jit(solution)/shard_map/ppermute | solution.py:646
  20.5 13.9 %collective-permute-start.3 = (bf16[3,2,32,128]{3,2,1,0:T(8,128)(2,1)S(1)}, bf16[3,2,32,128]{3,2,1,0:T(8,128)(2,1)S(1)}, u32[]{:S(2)}, u32[]{:S(2)}) collective-permute-start(bf16[3,2,32,128]{3,2,1,0:T(8,128)(2,1)S(1)} %get-tuple-element.51), channel_id=1, source_target_pairs={{0,12},{4,0},{8,4},{12,8},{1,13},{5,1},{9,5},{13,9},{2,14},{6,2},{... | collective-permute-start | bytes 147464 | tf_op jit(solution)/shard_map/ppermute | solution.py:646
  23.2 8.6 %collective-permute-start.5 = (bf16[4,2,32,128]{3,2,1,0:T(8,128)(2,1)S(1)}, bf16[4,2,32,128]{3,2,1,0:T(8,128)(2,1)S(1)}, u32[]{:S(2)}, u32[]{:S(2)}) collective-permute-start(bf16[4,2,32,128]{3,2,1,0:T(8,128)(2,1)S(1)} %get-tuple-element.54), channel_id=1, source_target_pairs={{0,8},{4,12},{8,0},{12,4},{1,9},{5,13},{9,1},{13,5},{2,10},{6,14},... | collective-permute-start | bytes 196616 | tf_op jit(solution)/shard_map/ppermute | solution.py:646
  25.1 7.4 %collective-permute-start.6 = (bf16[4,2,32,128]{3,2,1,0:T(8,128)(2,1)S(1)}, bf16[4,2,32,128]{3,2,1,0:T(8,128)(2,1)S(1)}, u32[]{:S(2)}, u32[]{:S(2)}) collective-permute-start(bf16[4,2,32,128]{3,2,1,0:T(8,128)(2,1)S(1)} %get-tuple-element.55), channel_id=1, source_target_pairs={{0,12},{4,0},{8,4},{12,8},{1,13},{5,1},{9,5},{13,9},{2,14},{6,2},{... | collective-permute-start | bytes 196616 | tf_op jit(solution)/shard_map/ppermute | solution.py:646
  35.9 1.5 %collective-permute-start.10 = (bf16[11,4,16,128]{3,2,1,0:T(8,128)(2,1)S(1)}, bf16[11,4,16,128]{3,2,1,0:T(8,128)(2,1)S(1)}, u32[]{:S(2)}, u32[]{:S(2)}) collective-permute-start(bf16[11,4,16,128]{3,2,1,0:T(8,128)(2,1)S(1)} %get-tuple-element.65), channel_id=1, source_target_pairs={{0,1},{1,0},{2,3},{3,2},{4,5},{5,4},{6,7},{7,6},{8,9},{9,8},{10,11... | collective-permute-start | bytes 540680 | tf_op jit(solution)/shard_map/ppermute | solution.py:666
  44.5 11.9 %collective-permute-start.11 = (bf16[6,2,32,128]{3,2,1,0:T(8,128)(2,1)S(1)}, bf16[6,2,32,128]{3,2,1,0:T(8,128)(2,1)S(1)}, u32[]{:S(2)}, u32[]{:S(2)}) collective-permute-start(bf16[6,2,32,128]{3,2,1,0:T(8,128)(2,1)S(1)} %get-tuple-element.72), channel_id=1, source_target_pairs={{0,12},{4,0},{8,4},{12,8},{1,13},{5,1},{9,5},{13,9},{2,14},{6,2},{... | collective-permute-start | bytes 294920 | tf_op jit(solution)/shard_map/ppermute | solution.py:687
  47.8 9.4 %collective-permute-start.12 = (bf16[6,2,32,128]{3,2,1,0:T(8,128)(2,1)S(1)}, bf16[6,2,32,128]{3,2,1,0:T(8,128)(2,1)S(1)}, u32[]{:S(2)}, u32[]{:S(2)}) collective-permute-start(bf16[6,2,32,128]{3,2,1,0:T(8,128)(2,1)S(1)} %get-tuple-element.73), channel_id=1, source_target_pairs={{0,8},{4,12},{8,0},{12,4},{1,9},{5,13},{9,1},{13,5},{2,10},{6,14},... | collective-permute-start | bytes 294920 | tf_op jit(solution)/shard_map/ppermute | solution.py:687
  48.1 9.1 %collective-permute-start.13 = (bf16[6,2,32,128]{3,2,1,0:T(8,128)(2,1)S(1)}, bf16[6,2,32,128]{3,2,1,0:T(8,128)(2,1)S(1)}, u32[]{:S(2)}, u32[]{:S(2)}) collective-permute-start(bf16[6,2,32,128]{3,2,1,0:T(8,128)(2,1)S(1)} %get-tuple-element.74), channel_id=1, source_target_pairs={{0,4},{4,8},{8,12},{12,0},{1,5},{5,9},{9,13},{13,1},{2,6},{6,10},{... | collective-permute-start | bytes 294920 | tf_op jit(solution)/shard_map/ppermute | solution.py:687
  57.2 7.7 %collective-permute-start.19 = (f32[40,128]{1,0:T(8,128)S(1)}, f32[40,128]{1,0:T(8,128)S(1)}, u32[]{:S(2)}, u32[]{:S(2)}) collective-permute-start(f32[40,128]{1,0:T(8,128)S(1)} %shard_map.110), channel_id=1, source_target_pairs={{0,12},{4,0},{8,4},{12,8},{1,13},{5,1},{9,5},{13,9},{2,14},{6,2},{... | collective-permute-start | bytes 61448 | tf_op jit(solution)/shard_map/ppermute | solution.py:568
  60.0 5.3 %collective-permute-start.18 = (f32[40,128]{1,0:T(8,128)S(1)}, f32[40,128]{1,0:T(8,128)S(1)}, u32[]{:S(2)}, u32[]{:S(2)}) collective-permute-start(f32[40,128]{1,0:T(8,128)S(1)} %shard_map.110), channel_id=1, source_target_pairs={{0,8},{4,12},{8,0},{12,4},{1,9},{5,13},{9,1},{13,5},{2,10},{6,14},... | collective-permute-start | bytes 61448 | tf_op jit(solution)/shard_map/ppermute | solution.py:568
  60.9 5.6 %collective-permute-start.17 = (f32[40,128]{1,0:T(8,128)S(1)}, f32[40,128]{1,0:T(8,128)S(1)}, u32[]{:S(2)}, u32[]{:S(2)}) collective-permute-start(f32[40,128]{1,0:T(8,128)S(1)} %shard_map.110), channel_id=1, source_target_pairs={{0,4},{4,8},{8,12},{12,0},{1,5},{5,9},{9,13},{13,1},{2,6},{6,10},{... | collective-permute-start | bytes 61448 | tf_op jit(solution)/shard_map/ppermute | solution.py:568
  61.1 5.4 %collective-permute-start.14 = (bf16[2,2,32,128]{3,2,1,0:T(8,128)(2,1)S(1)}, bf16[2,2,32,128]{3,2,1,0:T(8,128)(2,1)S(1)}, u32[]{:S(2)}, u32[]{:S(2)}) collective-permute-start(bf16[2,2,32,128]{3,2,1,0:T(8,128)(2,1)S(1)} %get-tuple-element.88), channel_id=1, source_target_pairs={{0,12},{4,0},{8,4},{12,8},{1,13},{5,1},{9,5},{13,9},{2,14},{6,2},{... | collective-permute-start | bytes 98312 | tf_op jit(solution)/shard_map/ppermute | solution.py:714
  64.7 4.8 %collective-permute-start.15 = (bf16[2,2,32,128]{3,2,1,0:T(8,128)(2,1)S(1)}, bf16[2,2,32,128]{3,2,1,0:T(8,128)(2,1)S(1)}, u32[]{:S(2)}, u32[]{:S(2)}) collective-permute-start(bf16[2,2,32,128]{3,2,1,0:T(8,128)(2,1)S(1)} %get-tuple-element.89), channel_id=1, source_target_pairs={{0,8},{4,12},{8,0},{12,4},{1,9},{5,13},{9,1},{13,5},{2,10},{6,14},... | collective-permute-start | bytes 98312 | tf_op jit(solution)/shard_map/ppermute | solution.py:714
  64.9 5.7 %collective-permute-start.16 = (bf16[2,2,32,128]{3,2,1,0:T(8,128)(2,1)S(1)}, bf16[2,2,32,128]{3,2,1,0:T(8,128)(2,1)S(1)}, u32[]{:S(2)}, u32[]{:S(2)}) collective-permute-start(bf16[2,2,32,128]{3,2,1,0:T(8,128)(2,1)S(1)} %get-tuple-element.90), channel_id=1, source_target_pairs={{0,4},{4,8},{8,12},{12,0},{1,5},{5,9},{9,13},{13,1},{2,6},{6,10},{... | collective-permute-start | bytes 98312 | tf_op jit(solution)/shard_map/ppermute | solution.py:714
  70.6 3.5 %collective-permute-start.22 = (f32[40,128]{1,0:T(8,128)S(1)}, f32[40,128]{1,0:T(8,128)S(1)}, u32[]{:S(2)}, u32[]{:S(2)}) collective-permute-start(f32[40,128]{1,0:T(8,128)S(1)} %shard_map.111), channel_id=1, source_target_pairs={{0,3},{1,2},{2,1},{3,0},{4,7},{5,6},{6,5},{7,4},{8,11},{9,10},{10,... | collective-permute-start | bytes 61448 | tf_op jit(solution)/shard_map/ppermute | solution.py:580
  70.6 3.8 %collective-permute-start.21 = (f32[40,128]{1,0:T(8,128)S(1)}, f32[40,128]{1,0:T(8,128)S(1)}, u32[]{:S(2)}, u32[]{:S(2)}) collective-permute-start(f32[40,128]{1,0:T(8,128)S(1)} %shard_map.111), channel_id=1, source_target_pairs={{0,2},{1,3},{2,0},{3,1},{4,6},{5,7},{6,4},{7,5},{8,10},{9,11},{10,... | collective-permute-start | bytes 61448 | tf_op jit(solution)/shard_map/ppermute | solution.py:580
  70.6 3.8 %collective-permute-start.20 = (f32[40,128]{1,0:T(8,128)S(1)}, f32[40,128]{1,0:T(8,128)S(1)}, u32[]{:S(2)}, u32[]{:S(2)}) collective-permute-start(f32[40,128]{1,0:T(8,128)S(1)} %shard_map.111), channel_id=1, source_target_pairs={{0,1},{1,0},{2,3},{3,2},{4,5},{5,4},{6,7},{7,6},{8,9},{9,8},{10,11... | collective-permute-start | bytes 61448 | tf_op jit(solution)/shard_map/ppermute | solution.py:580

commit v3 on v2

--- a/solution.py
+++ b/solution.py
@@ -1,5 +1,4 @@
 import functools
-import math
 
 import jax
 import jax.numpy as jnp
@@ -38,14 +37,8 @@
 
 
     def cuts(self):
-        unit = math.lcm(self.per, self.ring)
-        step = unit // self.per
-        firsts = list(range(0, self.groups, step))
-        if len(firsts) > 3:
-            firsts = [firsts[0], firsts[len(firsts) // 3], firsts[len(firsts) * 2 // 3]]
-        cuts = tuple(zip(firsts, firsts[1:] + [self.groups]))
-        early = cuts[-1][0] * self.per // self.ring
-        return cuts, (early, self.packs - early)
+        tail = -(-self.groups // 4)
+        return ((0, self.groups - tail), (self.groups - tail, self.groups))
 
 
 def fits(ring, gz, col, chans, rows, cells_x, cells_z, classes):
@@ -60,11 +53,14 @@
     return [pl.BlockSpec(memory_space=pltpu.VMEM)] * count
 
 
-def call(body, outs, args, scratch=(), micros=1.0, unread=0):
+def call(body, outs, args, scratch=(), micros=1.0, unread=0, scalars={}):
     return pl.pallas_call(
         body,
         out_shape=outs,
-        in_specs=vmem(len(args) - unread) + [pl.BlockSpec(memory_space=pl.ANY)] * unread,
+        in_specs=[
+            *(scalars.get(i, spec) for i, spec in enumerate(vmem(len(args) - unread))),
+            *[pl.BlockSpec(memory_space=pl.ANY)] * unread,
+        ],
         cost_estimate=pl.CostEstimate(
             flops=0, bytes_accessed=int(3.0e6 * micros), transcendentals=0
         ),
@@ -407,27 +403,27 @@
     lax.fori_loop(0, packs, step, 0)
 
 
-def backward_body(p, cuts, packs, table, bands, score_in, rim, *refs):
+def backward_body(p, cuts, table, bands, score_in, rim, *refs):
     count = len(cuts)
-    smooths, slopes, refs = refs[:count], refs[count : 2 * count - 1], refs[2 * count - 1 :]
+    smooths, slopes, refs = refs[:count], refs[count : 2 * count], refs[2 * count :]
     results, refs = refs[: p.ring], refs[p.ring :]
-    score, errors, hidden_near, slope_near = refs[:4]
-    grads = refs[4:-3]
-    wall, field, column = refs[-3:]
+    errors, hidden_near, grad_smooth, grad_wall = refs[:4]
+    score, slope_near, wall, field, column = refs[4:]
     core = lax.axis_index("col")
     score[...] = score_in[...]
     edge_rows(p, core, cuts, table, bands, smooths, rim, score, hidden_near, slope_near)
     judge(p, core, smooths[-1], rim, score, errors, column)
-    for i, (first, last) in enumerate(cuts[:-1]):
+    for (first, last), slope in zip(cuts, slopes):
+        own = pl.ds(first, last - first)
         backward_groups(
-            p, first, last - first, table, bands, score, slopes[i], slope_near,
-            grads[i], grads[count - 1 + i], wall, field.at[pl.ds(first, last - first)],
+            p, first, last - first, table, bands, score, slope, slope_near,
+            grad_smooth.at[own], grad_wall.at[own], wall, field.at[own],
         )
-    ship(p, packs, field, results)
-
-
-def finish_body(
-    p, cuts, packs, table, bands, score, errors, hidden_near, slope_near, rim, slope, *refs
+    ship(p, p.packs, field, results)
+
+
+def weight_body(
+    p, cuts, bands, errors, hidden_near, rim, grad_smooth, grad_wall, *refs
 ):
     count = len(cuts)
     refs = list(refs)
@@ -439,17 +435,7 @@
 
     hiddens, smooths = take(count), take(count)
     pieces = [take(p.ring) for i in range(count)]
-    grad_smooths, grad_walls = take(count - 1), take(count - 1)
-    results = take(p.ring)
-    out, wall, field, last_smooth, last_wall, column, lines = refs
-    first, last = cuts[-1]
-    backward_groups(
-        p, first, last - first, table, bands, score, slope, slope_near, last_smooth, last_wall,
-        wall, field,
-    )
-    ship(p, packs, field, results)
-    grad_smooths, grad_walls = grad_smooths + [last_smooth], grad_walls + [last_wall]
-
+    out, wall, column, lines = refs
     core = lax.axis_index("col")
     half = WALL // 2
     own = own_lanes(p, 16)
@@ -473,7 +459,7 @@
                     for xp in range(p.cells_x):
                         cells[cell_of(p, d, xp)] = pieces[chunk][d][g, xp, rows, :].astype(F32)
                 for x in range(p.xs):
-                    grad = jnp.where(own, grad_smooths[chunk][g, x, rows, :].astype(F32), 0.0)
+                    grad = jnp.where(own, grad_smooth[cg, x, rows, :].astype(F32), 0.0)
                     for j in range(TAPS):
                         moved = grad if j == REACH else pltpu.roll(grad, (j - REACH) % LANES, 1)
                         for i in range(TAPS):
@@ -489,7 +475,7 @@
                     column[x, pl.ds(start, length), :] = value
 
                 fill_column(p, core, smooths[chunk], rim, g, cg, x, store)
-            grads = [grad_walls[chunk][g, x].astype(F32) for x in range(p.xs)]
+            grads = [grad_wall[cg, x].astype(F32) for x in range(p.xs)]
             for k in range(WALL):
                 total = None
                 for x in range(p.xs):
@@ -568,17 +554,63 @@
     return sum((lax.ppermute(value, axis, rotation(size, d)) for d in range(1, size)), value)
 
 
-def sum_near(value):
+def near_parts(value):
     col, gz = lax.axis_size("col"), lax.axis_size("gz")
-    total = value
+    parts = [value]
     for d in range(1, col * gz):
         pairs = [
             (i * col + j, (i + d // col) % gz * col + (j + d) % col)
             for i in range(gz)
             for j in range(col)
         ]
-        total = total + lax.ppermute(value, ("gz", "col"), pairs)
-    return total
+        parts.append(lax.ppermute(value, ("gz", "col"), pairs))
+    return parts
+
+
+def table_body(p, tile, wall, classes, levels, stretch, *refs):
+    table, near = refs[-2:]
+    core = lax.axis_index("col")
+    lane = lax.broadcasted_iota(jnp.int32, (p.chans, LANES), 1)
+    channel = lax.broadcasted_iota(jnp.int32, (p.chans, LANES), 0)
+
+    def spread_rows(value, pick, dim):
+        return lax.dot_general(
+            value, pick, (((dim,), (0,)), ((), ())),
+            precision=lax.Precision.HIGHEST, preferred_element_type=F32,
+        )
+
+    for cg in range(p.groups):
+        pick = (lane // p.block + cg * p.per == channel) & (lane < p.per * p.block)
+        pick = jnp.where(pick, 1.0, 0.0)
+        table[cg, pl.ds(0, ROW_WALL), :] = spread_rows(tile[...], pick, 0)
+        table[cg, pl.ds(ROW_WALL, WALL), :] = spread_rows(wall[...], pick, 1)
+        table[cg, pl.ds(ROW_CLASS, p.classes), :] = spread_rows(classes[...], pick, 1)
+    marks = lane_of(1)
+    marks = (marks // p.block == p.per - 1) & (marks < p.per * p.block)
+    last = table[p.groups - 1, pl.ds(CENTRE, 1), :]
+    table[p.groups - 1, pl.ds(CENTRE, 1), :] = jnp.where(marks, 1.0, last)
+
+    def step(q, carry):
+        y = jnp.clip(core * p.rows - WALL // 2 + q, 0, 2 * p.rows - 1)
+        level = levels[y]
+        for k in range(WALL):
+            near[k, pl.ds(q, 1), :] = jnp.full((1, LANES), stretch[level, k], F32)
+        return carry
+
+    lax.fori_loop(0, p.reach_rows, step, 0)
+
+
+def sums_body(p, volume, *refs):
+    tile, wall, classes = refs[-3:]
+    total = refs[0][...]
+    for ref in refs[1:-3]:
+        total = total + ref[...]
+    total = total * (1.0 / volume)
+    rows = jnp.zeros((LANES - p.table_rows, LANES), F32)
+    turned = jnp.concatenate([total, rows], axis=0).T
+    tile[...] = turned[: p.chans, :ROW_WALL]
+    wall[...] = total[ROW_WALL:ROW_CLASS, : p.chans]
+    classes[...] = total[ROW_CLASS : ROW_CLASS + p.classes, : p.chans]
 
 
 def band_rows(grid_index, stretch):
@@ -594,7 +626,7 @@
     p = Plan(ring, chans, rows, cells_x, cells_z, classes)
     volume = labels.shape[0] * cells_x * ring * cells_z * gz
     tall = rows * cells_x
-    cuts, packs = p.cuts()
+    cuts = p.cuts()
 
     field = features.reshape(chans, tall, cells_z)
     marks = labels.reshape(labels.shape[0] * cells_x, cells_z)
@@ -617,25 +649,21 @@
         [pltpu.VMEM((ring, tall, LANES), F32)],
     )
 
-    bands = band_rows(grid_index, stretch)
-    half = WALL // 2
-    near = lax.dynamic_slice_in_dim(
-        jnp.pad(bands, ((half, half), (0, 0))), lax.axis_index("col") * rows, p.reach_rows, 0
-    )
-    near = jnp.broadcast_to(near.T[:, :, None], (WALL, p.reach_rows, LANES))
-    params = jnp.concatenate([tile_filter.T, wall_filter.T, class_weight], axis=0)
-    extra = (jnp.arange(params.shape[0]) == CENTRE).astype(F32)[:, None]
-    params = jnp.concatenate([params, extra], axis=1).reshape(-1, p.groups, p.per, 1)
-    table = jnp.broadcast_to(params, params.shape[:3] + (p.block,))
-    table = table.reshape(params.shape[0], p.groups, p.per * p.block)
-    table = jnp.pad(
-        table,
-        ((0, p.table_rows - table.shape[0]), (0, 0), (0, LANES - p.per * p.block)),
-    ).transpose(1, 0, 2)
-
     def shape(*sizes, kind=BF16):
         return jax.ShapeDtypeStruct(sizes, kind)
 
+    smem = pl.BlockSpec(memory_space=pltpu.SMEM)
+    table, near = call(
+        functools.partial(table_body, p),
+        [
+            shape(p.groups, p.table_rows, LANES, kind=F32),
+            shape(WALL, p.reach_rows, LANES, kind=F32),
+        ],
+        (tile_filter, wall_filter.T, class_weight, grid_index, stretch, windows[0]),
+        micros=0.1,
+        unread=1,
+        scalars={3: smem, 4: smem},
+    )
     column = pltpu.VMEM((p.xs, rows + 2 * WALL_HALO, LANES), F32)
     wall = pltpu.VMEM((p.xs, p.reach_rows, LANES), F32)
     smooths, rims, pieces, hiddens, slopes, score = [], [], [], [], [], ()
@@ -665,42 +693,37 @@
     score = score[0]
     rim = lax.ppermute(rims[-1], "col", rotation(2, 1))
 
-    sizes = [last - first for first, last in cuts]
-    early = sizes[:-1]
-    solved = call(
-        functools.partial(backward_body, p, cuts, packs[0]),
-        [shape(packs[0], cells_x, rows, LANES)] * ring
+    near_shape = (p.groups, p.xs, 8, LANES)
+    *sent, errors, hidden_near, grad_smooth, grad_wall = call(
+        functools.partial(backward_body, p, cuts),
+        [shape(p.packs, cells_x, rows, LANES)] * ring
         + [
-            shape(classes, p.xs, p.reach_rows, LANES, kind=F32),
             shape(classes, p.xs, rows, LANES, kind=F32),
-            shape(p.groups, p.xs, 8, LANES, kind=F32),
-            shape(p.groups, p.xs, 8, LANES, kind=F32),
-        ]
-        + [shape(size, p.xs, rows, LANES) for size in early] * 2,
-        (table, near, score, rim, *smooths, *slopes[:-1]),
-        [wall, pltpu.VMEM((sum(early), p.xs, rows, LANES), F32), column],
+            shape(*near_shape, kind=F32),
+            shape(p.groups, p.xs, rows, LANES),
+            shape(p.groups, p.xs, rows, LANES),
+        ],
+        (table, near, score, rim, *smooths, *slopes),
+        [
+            pltpu.VMEM((classes, p.xs, p.reach_rows, LANES), F32),
+            pltpu.VMEM(near_shape, F32),
+            wall,
+            pltpu.VMEM((p.groups, p.xs, rows, LANES), F32),
+            column,
+        ],
         micros=5,
     )
-    sent, solved = solved[:ring], solved[ring:]
-    score, errors, hidden_near, slope_near, *grads = solved
     back = [sent[0]] + [
         lax.ppermute(sent[d], "gx", rotation(ring, -d)) for d in range(1, ring)
     ]
-    *sent, sums = call(
-        functools.partial(finish_body, p, cuts, packs[1]),
-        [shape(packs[1], cells_x, rows, LANES)] * ring + [shape(p.table_rows, LANES, kind=F32)],
+    (sums,) = call(
+        functools.partial(weight_body, p, cuts),
+        [shape(p.table_rows, LANES, kind=F32)],
         (
-            *(table, near, score, errors, hidden_near, slope_near, rim, slopes[-1]),
-            *hiddens, *smooths, *pieces, *grads,
+            *(near, errors, hidden_near, rim, grad_smooth, grad_wall),
+            *hiddens, *smooths, *pieces,
         ),
-        [
-            wall,
-            pltpu.VMEM((sizes[-1], p.xs, rows, LANES), F32),
-            pltpu.VMEM((sizes[-1], p.xs, rows, LANES), BF16),
-            pltpu.VMEM((sizes[-1], p.xs, rows, LANES), BF16),
-            column,
-            pltpu.VMEM((p.groups, p.table_rows, LANES), F32),
-        ],
+        [wall, column, pltpu.VMEM((p.groups, p.table_rows, LANES), F32)],
         micros=0.01,
     )
     (sums,) = call(
@@ -710,31 +733,24 @@
         micros=0.1,
         unread=ring - 1,
     )
-    back += [sent[0]] + [
-        lax.ppermute(sent[d], "gx", rotation(ring, -d)) for d in range(1, ring)
-    ]
     sums = sum_over(sums, "gx")
-    (sums,) = call(
-        pass_body,
-        [shape(p.table_rows, LANES, kind=F32)],
-        (sums, *back[ring + 1 :]),
-        micros=0.1,
-        unread=ring - 1,
-    )
-    sums = sum_near(sums)
-    sums = sums / volume
     (grad_field,) = call(
         functools.partial(unpack_body, p),
-        [jax.ShapeDtypeStruct((chans, tall, cells_z), BF16)],
+        [shape(chans, tall, cells_z)],
         back,
         [pltpu.VMEM((ring, tall, LANES), F32)],
     )
-    return (
-        grad_field.reshape(features.shape),
-        sums[:ROW_WALL, :chans].T,
-        sums[ROW_WALL:ROW_CLASS, :chans].T,
-        sums[ROW_CLASS : ROW_CLASS + classes, :chans],
-    )
+    grad_tile, grad_wall, grad_class = call(
+        functools.partial(sums_body, p, volume),
+        [
+            shape(chans, ROW_WALL, kind=F32),
+            shape(WALL, chans, kind=F32),
+            shape(classes, chans, kind=F32),
+        ],
+        near_parts(sums),
+        micros=0.1,
+    )
+    return grad_field.reshape(features.shape), grad_tile, grad_wall.T, grad_class
 
 
 def with_halo(value, sides, width):

time: 76.6 us -> 71.2 us (0.930)
  starting transfers between devices: 34.2 us -> 25 us
  waiting for transfers between devices: 8.77 us -> 15.9 us
  local copies, waits for them, and re-layouts: 7.54 us -> 1.9 us
  Pallas kernels: 24.7 us -> 27.4 us
    ppermute x9 -> x6, starting transfers between devices: 17.4 us -> 8.63 us  [by_windows(): lax.ppermute(sent[d], 'gx', rotation(ring, d))]
    unnamed x20 -> x14, local copies, waits for them, and re-layouts: 5.02 us -> 1.9 us
    ppermute x9 -> x6, waiting for transfers between devices: 0.95 us -> 3.81 us  [by_windows(): lax.ppermute(sent[d], 'gx', rotation(ring, d))]
    pallas_call x10, Pallas kernels: 24.7 us -> 27.4 us  [call(): pl.pallas_call(body, out_shape=outs, in_specs=[*(scalars.get(i, spec) for...]
    ppermute x3, waiting for transfers between devices: 1.19 us -> 3.56 us  [sum_over(): lax.ppermute(value, axis, rotation(size, d))]
    ppermute x1, waiting for transfers between devices: 0.01 us -> 2.07 us  [by_windows(): left = lax.ppermute(edge, 'gz', rotation(gz, 1))]
    ppermute x6 -> x3, starting transfers between devices: 8.11 us -> 7.05 us  [by_windows(): lax.ppermute(sent[d], 'gx', rotation(ring, -d))]
    broadcast_in_dim x4 -> x0, local copies, waits for them, and re-layouts: 0.8 us -> none  [the longest x3 0.7 us: by_windows(): table = jnp.broadcast_to(params, params.shape[:3] + (p.block,))]
  transfers between devices with their start and end apart: 23 -> 17, of which waited for: 8 -> 11; matrix products, arithmetic and copies ran while one was open for 2% -> 0% of each run, Pallas kernels for 18% -> 20%
where the time goes in v3:
time: 71.2 us; the launch traced here: 71 us
  Pallas kernels  27.4 us (38%)
  starting transfers between devices  25 us (35%)
  waiting for transfers between devices  15.9 us (22%)
  local copies, waits for them, and re-layouts  1.9 us (3%)
  between operations  0.76 us (1%)
    pallas_call x10, Pallas kernels, call(): pl.pallas_call(body, out_shape=outs, in_specs=[*(scalars.get(i, spec) for...  27.4 us
    ppermute x6, starting transfers between devices, by_windows(): lax.ppermute(sent[d], 'gx', rotation(ring, d))  8.63 us
    ppermute x3, starting transfers between devices, by_windows(): lax.ppermute(sent[d], 'gx', rotation(ring, -d))  7.05 us
    ppermute x3, waiting for transfers between devices, by_windows(): lax.ppermute(sent[d], 'gx', rotation(ring, -d))  4.73 us
    ppermute x3, starting transfers between devices, sum_over(): lax.ppermute(value, axis, rotation(size, d))  4.35 us
    ppermute x6, waiting for transfers between devices, by_windows(): lax.ppermute(sent[d], 'gx', rotation(ring, d))  3.81 us
    ppermute x3, waiting for transfers between devices, sum_over(): lax.ppermute(value, axis, rotation(size, d))  3.56 us
    ppermute x1, starting transfers between devices, by_windows(): left = lax.ppermute(edge, 'gz', rotation(gz, 1))  2.95 us
  transfers between devices with their start and end apart: 17, of which 11 were waited for; matrix products, arithmetic and copies ran while one was open for 0% of the time, Pallas kernels for 20%

profile of v3, /device:TPU:0, one launch (start us, length us, event | category | flops | bytes accessed | tf_op | source)
XLA Modules:
  0.0 71.0 jit_solution(12054779637035358453)
XLA Ops:
  0.6 0.0 copy-start.5
  0.7 1.0 %copy-done = bf16[32,32,2,128]{3,2,1,0:T(2,128)(2,1)S(1)} copy-done((bf16[32,32,2,128]{3,2,1,0:T(2,128)(2,1)S(1)}, bf16[32,32,2,128]{3,2,1,0:T(2,128)(2,1)}, u32[]{:S(2)}) %copy-start) | copy-done | bytes 524312
  1.7 0.8 %copy-done.1 = s32[64,2,128]{2,1,0:T(2,128)S(1)} copy-done((s32[64,2,128]{2,1,0:T(2,128)S(1)}, s32[64,2,128]{2,1,0:T(2,128)}, u32[]{:S(2)}) %copy-start.1) | copy-done | bytes 65560
  2.6 0.3 shard_map.102
  2.9 3.0 %collective-permute-start = (bf16[3,64,128]{2,1,0:T(8,128)(2,1)S(1)}, bf16[3,64,128]{2,1,0:T(8,128)(2,1)S(1)}, u32[]{:S(2)}, u32[]{:S(2)}) collective-permute-start(bf16[3,64,128]{2,1,0:T(8,128)(2,1)S(1)} %shard_map.102), channel_id=1, source_target_pairs={{0,2},{2,0},{1,3},{3,1},{4,6},{6,4},{5,7},{7,5},{8,10},{10,8},{9,1... | collective-permute-start | bytes 147464 | tf_op jit(solution)/shard_map/ppermute | solution.py:638
  5.8 2.1 %collective-permute-done.left.right = bf16[3,64,128]{2,1,0:T(8,128)(2,1)S(1)} collective-permute-done((bf16[3,64,128]{2,1,0:T(8,128)(2,1)S(1)}, bf16[3,64,128]{2,1,0:T(8,128)(2,1)S(1)}, u32[]{:S(2)}, u32[]{:S(2)}) %collective-permute-start) | collective-permute-done | bytes 49184 | tf_op jit(solution)/shard_map/ppermute | solution.py:638
  7.9 2.3 %shard_map.103 = (bf16[8,2,32,128]{3,2,1,0:T(8,128)(2,1)S(1)}, bf16[8,2,32,128]{3,2,1,0:T(8,128)(2,1)S(1)}, bf16[8,2,32,128]{3,2,1,0:T(8,128)(2,1)S(1)}, bf16[8,...) custom-call(bf16[32,64,128]{2,1,0:T(8,128)(2,1)S(1)} %bitcast.6, ...), custom_call_target="tpu_custom_call" | custom-call | bytes 3000000 | tf_op jit(solution)/shard_map/pallas_call | solution.py:57
  10.3 2.2 %collective-permute-start.4 = (bf16[8,2,32,128]{3,2,1,0:T(8,128)(2,1)S(1)}, bf16[8,2,32,128]{3,2,1,0:T(8,128)(2,1)S(1)}, u32[]{:S(2)}, u32[]{:S(2)}) collective-permute-start(bf16[8,2,32,128]{3,2,1,0:T(8,128)(2,1)S(1)} %get-tuple-element.42), channel_id=1, source_target_pairs={{0,4},{4,8},{8,12},{12,0},{1,5},{5,9},{9,13},{13,1},{2,6},{6,10},{... | collective-permute-start | bytes 393224 | tf_op jit(solution)/shard_map/ppermute | solution.py:674
  12.4 2.6 %collective-permute-start.5 = (bf16[8,2,32,128]{3,2,1,0:T(8,128)(2,1)S(1)}, bf16[8,2,32,128]{3,2,1,0:T(8,128)(2,1)S(1)}, u32[]{:S(2)}, u32[]{:S(2)}) collective-permute-start(bf16[8,2,32,128]{3,2,1,0:T(8,128)(2,1)S(1)} %get-tuple-element.43), channel_id=1, source_target_pairs={{0,8},{4,12},{8,0},{12,4},{1,9},{5,13},{9,1},{13,5},{2,10},{6,14},... | collective-permute-start | bytes 393224 | tf_op jit(solution)/shard_map/ppermute | solution.py:674
  15.0 1.3 %collective-permute-start.6 = (bf16[8,2,32,128]{3,2,1,0:T(8,128)(2,1)S(1)}, bf16[8,2,32,128]{3,2,1,0:T(8,128)(2,1)S(1)}, u32[]{:S(2)}, u32[]{:S(2)}) collective-permute-start(bf16[8,2,32,128]{3,2,1,0:T(8,128)(2,1)S(1)} %get-tuple-element.44), channel_id=1, source_target_pairs={{0,12},{4,0},{8,4},{12,8},{1,13},{5,1},{9,5},{13,9},{2,14},{6,2},{... | collective-permute-start | bytes 393224 | tf_op jit(solution)/shard_map/ppermute | solution.py:674
  16.4 0.7 collective-permute-start.1
  17.0 0.3 collective-permute-start.2
  17.4 1.6 %collective-permute-done.4.refs_1_.refs_5_ = bf16[8,2,32,128]{3,2,1,0:T(8,128)(2,1)S(1)} collective-permute-done((bf16[8,2,32,128]{3,2,1,0:T(8,128)(2,1)S(1)}, bf16[8,2,32,128]{3,2,1,0:T(8,128)(2,1)S(1)}, u32[]{:S(2)}, u32[]{:S(2)}) %collective-permute-start.4) | collective-permute-done | bytes 131104 | tf_op jit(solution)/shard_map/ppermute | solution.py:674
  18.9 1.5 %collective-permute-start.3 = (bf16[3,2,32,128]{3,2,1,0:T(8,128)(2,1)S(1)}, bf16[3,2,32,128]{3,2,1,0:T(8,128)(2,1)S(1)}, u32[]{:S(2)}, u32[]{:S(2)}) collective-permute-start(bf16[3,2,32,128]{3,2,1,0:T(8,128)(2,1)S(1)} %get-tuple-element.41), channel_id=1, source_target_pairs={{0,12},{4,0},{8,4},{12,8},{1,13},{5,1},{9,5},{13,9},{2,14},{6,2},{... | collective-permute-start | bytes 147464 | tf_op jit(solution)/shard_map/ppermute | solution.py:674
  20.5 0.0 copy-done.5
  20.5 0.0 copy-done.4
  20.5 2.1 %shard_map.104 = (f32[11,40,128]{2,1,0:T(8,128)S(1)}, f32[9,40,128]{2,1,0:T(8,128)S(1)}) custom-call(f32[32,25]{1,0:T(8,128)S(1)} %copy-done.2, f32[9,32]{1,0:T(8,128)S(1)} %bitcast.9, f32[4,32]{1,0:T(4,128)S(1)} %copy-done.5, s32[64]{0:T(128)S(1)} %copy-done.6, f32[16,9]{1,0:T(8,128)S(1)} %copy-done.4, ...), custom_call_target="tpu_custom_call" | custom-call | bytes 300000 | tf_op jit(solution)/shard_map/pallas_call | solution.py:57
  22.6 1.0 %collective-permute-done.5.refs_2_.refs_6_ = bf16[8,2,32,128]{3,2,1,0:T(8,128)(2,1)S(1)} collective-permute-done((bf16[8,2,32,128]{3,2,1,0:T(8,128)(2,1)S(1)}, bf16[8,2,32,128]{3,2,1,0:T(8,128)(2,1)S(1)}, u32[]{:S(2)}, u32[]{:S(2)}) %collective-permute-start.5) | collective-permute-done | bytes 131104 | tf_op jit(solution)/shard_map/ppermute | solution.py:674
  23.6 0.1 collective-permute-done.6.refs_3_.refs_7_
  23.7 3.7 %shard_map.105 = (bf16[8,8,32,128]{3,2,1,0:T(8,128)(2,1)S(1)}, f32[8,8,40,128]{3,2,1,0:T(8,128)S(1)}, f32[8,8,40,128]{3,2,1,0:T(8,128)S(1)}, f32[4,8,40,128]{3,2,1,0:T(8,128)S(1)}, bf16[8,4,16,128]{3,2,1,0:T(8,128)(2,1)S(1)}) custom-call(f32[11,40,128]{2,1,0:T(8,128)S(1)} %get-tuple-element.36.table, f32[9,40,128]{2,1,0:T(8,128)S(1)} %get-tuple-element.37.bands, ...), custom_call_target="tpu_custom_call" | custom-call | bytes 3000 | tf_op jit(solution)/shard_map/pallas_call | solution.py:57
  27.4 0.0 collective-permute-done.1.refs_1_.refs_9_
  27.4 1.1 %collective-permute-done.2.refs_2_.refs_10_ = bf16[3,2,32,128]{3,2,1,0:T(8,128)(2,1)S(1)} collective-permute-done((bf16[3,2,32,128]{3,2,1,0:T(8,128)(2,1)S(1)}, bf16[3,2,32,128]{3,2,1,0:T(8,128)(2,1)S(1)}, u32[]{:S(2)}, u32[]{:S(2)}) %collective-permute-start.2) | collective-permute-done | bytes 49184 | tf_op jit(solution)/shard_map/ppermute | solution.py:674
  28.5 0.1 collective-permute-done.3.refs_3_.refs_11_
  28.6 1.4 %shard_map.106 = (bf16[3,8,32,128]{3,2,1,0:T(8,128)(2,1)S(1)}, f32[3,8,40,128]{3,2,1,0:T(8,128)S(1)}, f32[3,8,40,128]{3,2,1,0:T(8,128)S(1)}, f32[4,8,40,128]{3,2,1,0:T(8,128)S(1)}, bf16[11,4,16,128]{3,2,1,0:T(8,128)(2,1)S(1)}) custom-call(f32[11,40,128]{2,1,0:T(8,128)S(1)} %get-tuple-element.36.table, f32[9,40,128]{2,1,0:T(8,128)S(1)} %get-tuple-element.37.bands, ...), custom_call_target="tpu_custom_call" | custom-call | bytes 3000 | tf_op jit(solution)/shard_map/pallas_call | solution.py:57
  30.1 0.1 collective-permute-start.7
  30.1 1.4 %collective-permute-done.7.rim = bf16[11,4,16,128]{3,2,1,0:T(8,128)(2,1)S(1)} collective-permute-done((bf16[11,4,16,128]{3,2,1,0:T(8,128)(2,1)S(1)}, bf16[11,4,16,128]{3,2,1,0:T(8,128)(2,1)S(1)}, u32[]{:S(2)}, u32[]{:S(2)}) %collective-permute-start.7) | collective-permute-done | bytes 180256 | tf_op jit(solution)/shard_map/ppermute | solution.py:694
  31.5 8.7 %shard_map.107 = (bf16[8,2,32,128]{3,2,1,0:T(8,128)(2,1)S(1)}, bf16[8,2,32,128]{3,2,1,0:T(8,128)(2,1)S(1)}, bf16[8,2,32,128]{3,2,1,0:T(8,128)(2,1)S(1)}, bf16[8,...) custom-call(f32[11,40,128]{2,1,0:T(8,128)S(1)} %get-tuple-element.36, ...), custom_call_target="tpu_custom_call" | custom-call | bytes 15000000 | tf_op jit(solution)/shard_map/pallas_call | solution.py:57
  40.3 6.4 %collective-permute-start.8 = (bf16[8,2,32,128]{3,2,1,0:T(8,128)(2,1)S(1)}, bf16[8,2,32,128]{3,2,1,0:T(8,128)(2,1)S(1)}, u32[]{:S(2)}, u32[]{:S(2)}) collective-permute-start(bf16[8,2,32,128]{3,2,1,0:T(8,128)(2,1)S(1)} %get-tuple-element.54), channel_id=1, source_target_pairs={{0,12},{4,0},{8,4},{12,8},{1,13},{5,1},{9,5},{13,9},{2,14},{6,2},{... | collective-permute-start | bytes 393224 | tf_op jit(solution)/shard_map/ppermute | solution.py:717
  46.7 0.0 collective-permute-start.9
  46.7 0.6 collective-permute-start.10
  47.3 6.4 %shard_map.109.value = f32[40,128]{1,0:T(8,128)S(1)} custom-call(f32[9,40,128]{2,1,0:T(8,128)S(1)} %get-tuple-element.37.bands, f32[4,8,32,128]{3,2,1,0:T(8,128)S(1)} %get-tuple-element.57.errors, f32[11,8,8,128]{3,2,1,0:T(8,128)S(1)} %get-tuple-element.58.hidden_near, bf16[11,4,16,128]{3,2,1,0:T(8,128)(2,1)S(1)} %collective-permute-done.7.rim, ...), custom_call_target="tpu_custom_call" | custom-call | bytes 30000 | tf_op jit(solution)/shard_map/pallas_call | solution.py:57
  53.7 0.0 collective-permute-done.8.refs_1_.refs_0_
  53.7 4.7 %collective-permute-done.9.refs_2_.refs_1_ = bf16[8,2,32,128]{3,2,1,0:T(8,128)(2,1)S(1)} collective-permute-done((bf16[8,2,32,128]{3,2,1,0:T(8,128)(2,1)S(1)}, bf16[8,2,32,128]{3,2,1,0:T(8,128)(2,1)S(1)}, u32[]{:S(2)}, u32[]{:S(2)}) %collective-permute-start.9) | collective-permute-done | bytes 131104 | tf_op jit(solution)/shard_map/ppermute | solution.py:717
  58.5 0.0 collective-permute-done.10.refs_3_.refs_2_
  58.5 1.2 %collective-permute-start.13 = (f32[40,128]{1,0:T(8,128)S(1)}, f32[40,128]{1,0:T(8,128)S(1)}, u32[]{:S(2)}, u32[]{:S(2)}) collective-permute-start(f32[40,128]{1,0:T(8,128)S(1)} %shard_map.110), channel_id=1, source_target_pairs={{0,12},{4,0},{8,4},{12,8},{1,13},{5,1},{9,5},{13,9},{2,14},{6,2},{... | collective-permute-start | bytes 61448 | tf_op jit(solution)/shard_map/ppermute | solution.py:554
  59.7 1.1 %collective-permute-start.12 = (f32[40,128]{1,0:T(8,128)S(1)}, f32[40,128]{1,0:T(8,128)S(1)}, u32[]{:S(2)}, u32[]{:S(2)}) collective-permute-start(f32[40,128]{1,0:T(8,128)S(1)} %shard_map.110), channel_id=1, source_target_pairs={{0,8},{4,12},{8,0},{12,4},{1,9},{5,13},{9,1},{13,5},{2,10},{6,14},... | collective-permute-start | bytes 61448 | tf_op jit(solution)/shard_map/ppermute | solution.py:554
  60.8 2.0 %collective-permute-start.11 = (f32[40,128]{1,0:T(8,128)S(1)}, f32[40,128]{1,0:T(8,128)S(1)}, u32[]{:S(2)}, u32[]{:S(2)}) collective-permute-start(f32[40,128]{1,0:T(8,128)S(1)} %shard_map.110), channel_id=1, source_target_pairs={{0,4},{4,8},{8,12},{12,0},{1,5},{5,9},{9,13},{13,1},{2,6},{6,10},{... | collective-permute-start | bytes 61448 | tf_op jit(solution)/shard_map/ppermute | solution.py:554
  62.8 0.0 collective-permute-done.13
  62.8 2.0 %collective-permute-done.12 = f32[40,128]{1,0:T(8,128)S(1)} collective-permute-done((f32[40,128]{1,0:T(8,128)S(1)}, f32[40,128]{1,0:T(8,128)S(1)}, u32[]{:S(2)}, u32[]{:S(2)}) %collective-permute-start.12) | collective-permute-done | bytes 20512 | tf_op jit(solution)/shard_map/ppermute | solution.py:554
  64.8 1.6 %collective-permute-done.11 = f32[40,128]{1,0:T(8,128)S(1)} collective-permute-done((f32[40,128]{1,0:T(8,128)S(1)}, f32[40,128]{1,0:T(8,128)S(1)}, u32[]{:S(2)}, u32[]{:S(2)}) %collective-permute-start.11) | collective-permute-done | bytes 20512 | tf_op jit(solution)/shard_map/ppermute | solution.py:554
  66.4 0.1 collective-permute-start.16
  66.5 1.6 %collective-permute-start.15 = (f32[40,128]{1,0:T(8,128)S(1)}, f32[40,128]{1,0:T(8,128)S(1)}, u32[]{:S(2)}, u32[]{:S(2)}) collective-permute-start(f32[40,128]{1,0:T(8,128)S(1)} %add_add_fusion.refs_0_), channel_id=1, source_target_pairs={{0,2},{1,3},{2,0},{3,1},{4,6},{5,7},{6,4},{7,5},{8,10},{9,11},{10,... | collective-permute-start | bytes 61448 | tf_op jit(solution)/shard_map/ppermute | solution.py:566
  68.0 0.3 collective-permute-start.14
  68.3 1.6 %shard_map.108 = bf16[32,64,128]{2,1,0:T(8,128)(2,1)} custom-call(bf16[8,2,32,128]{3,2,1,0:T(8,128)(2,1)S(1)} %get-tuple-element.53.refs_0_, bf16[8,2,32,128]{3,2,1,0:T(8,128)(2,1)S(1)} %collective-permute-done.8.refs_1_.refs_0_, bf16[8,2,32,128]{3,2,1,0:T(8,128)(2,1)S(1)} %collective-permute-done.9.refs_2_.refs_1_, ...), custom_call_target="tpu_custom_call" | custom-call | bytes 3000000 | tf_op jit(solution)/shard_map/pallas_call | solution.py:57
  70.0 0.0 collective-permute-done.16.refs_3_
  70.0 0.4 collective-permute-done.15.refs_2_
  70.3 0.0 collective-permute-done.14.refs_1_
  70.3 0.7 shard_map.111
  (11 shorter events, 0.0 us)
Async XLA Ops:
  0.6 19.8 %copy-start.5 = (f32[4,32]{1,0:T(4,128)S(1)}, f32[4,32]{1,0:T(4,128)}, u32[]{:S(2)}) copy-start(f32[4,32]{1,0:T(4,128)} %classes.1) | copy-start | bytes 1540
  0.6 19.8 %copy-start.6 = (s32[64]{0:T(128)S(1)}, s32[64]{0:T(128)}, u32[]{:S(2)}) copy-start(s32[64]{0:T(128)} %levels.1) | copy-start | bytes 772
  0.7 1.1 %copy-start = (bf16[32,32,2,128]{3,2,1,0:T(2,128)(2,1)S(1)}, bf16[32,32,2,128]{3,2,1,0:T(2,128)(2,1)}, u32[]{:S(2)}) copy-start(bf16[32,32,2,128]{3,2,1,0:T(2,128)(2,1)} %param.7) | copy-start | bytes 1572868
  1.7 0.8 %copy-start.1 = (s32[64,2,128]{2,1,0:T(2,128)S(1)}, s32[64,2,128]{2,1,0:T(2,128)}, u32[]{:S(2)}) copy-start(s32[64,2,128]{2,1,0:T(2,128)} %param.8) | copy-start | bytes 196612
  2.5 17.9 %copy-start.2 = (f32[32,25]{1,0:T(8,128)S(1)}, f32[32,25]{1,0:T(8,128)}, u32[]{:S(2)}) copy-start(f32[32,25]{1,0:T(8,128)} %tile.1) | copy-start | bytes 9604
  2.5 17.9 %copy-start.3 = (f32[32,9]{0,1:T(8,128)S(1)}, f32[32,9]{0,1:T(8,128)}, u32[]{:S(2)}) copy-start(f32[32,9]{0,1:T(8,128)} %param.12) | copy-start | bytes 3460
  2.6 17.9 %copy-start.4 = (f32[16,9]{1,0:T(8,128)S(1)}, f32[16,9]{1,0:T(8,128)}, u32[]{:S(2)}) copy-start(f32[16,9]{1,0:T(8,128)} %stretch.1) | copy-start | bytes 1732
  2.9 5.0 %collective-permute-start = (bf16[3,64,128]{2,1,0:T(8,128)(2,1)S(1)}, bf16[3,64,128]{2,1,0:T(8,128)(2,1)S(1)}, u32[]{:S(2)}, u32[]{:S(2)}) collective-permute-start(bf16[3,64,128]{2,1,0:T(8,128)(2,1)S(1)} %shard_map.102), channel_id=1, source_target_pairs={{0,2},{2,0},{1,3},{3,1},{4,6},{6,4},{5,7},{7,5},{8,10},{10,8},{9,1... | collective-permute-start | bytes 147464 | tf_op jit(solution)/shard_map/ppermute | solution.py:638
  10.3 8.7 %collective-permute-start.4 = (bf16[8,2,32,128]{3,2,1,0:T(8,128)(2,1)S(1)}, bf16[8,2,32,128]{3,2,1,0:T(8,128)(2,1)S(1)}, u32[]{:S(2)}, u32[]{:S(2)}) collective-permute-start(bf16[8,2,32,128]{3,2,1,0:T(8,128)(2,1)S(1)} %get-tuple-element.42), channel_id=1, source_target_pairs={{0,4},{4,8},{8,12},{12,0},{1,5},{5,9},{9,13},{13,1},{2,6},{6,10},{... | collective-permute-start | bytes 393224 | tf_op jit(solution)/shard_map/ppermute | solution.py:674
  12.4 11.2 %collective-permute-start.5 = (bf16[8,2,32,128]{3,2,1,0:T(8,128)(2,1)S(1)}, bf16[8,2,32,128]{3,2,1,0:T(8,128)(2,1)S(1)}, u32[]{:S(2)}, u32[]{:S(2)}) collective-permute-start(bf16[8,2,32,128]{3,2,1,0:T(8,128)(2,1)S(1)} %get-tuple-element.43), channel_id=1, source_target_pairs={{0,8},{4,12},{8,0},{12,4},{1,9},{5,13},{9,1},{13,5},{2,10},{6,14},... | collective-permute-start | bytes 393224 | tf_op jit(solution)/shard_map/ppermute | solution.py:674
  15.0 8.7 %collective-permute-start.6 = (bf16[8,2,32,128]{3,2,1,0:T(8,128)(2,1)S(1)}, bf16[8,2,32,128]{3,2,1,0:T(8,128)(2,1)S(1)}, u32[]{:S(2)}, u32[]{:S(2)}) collective-permute-start(bf16[8,2,32,128]{3,2,1,0:T(8,128)(2,1)S(1)} %get-tuple-element.44), channel_id=1, source_target_pairs={{0,12},{4,0},{8,4},{12,8},{1,13},{5,1},{9,5},{13,9},{2,14},{6,2},{... | collective-permute-start | bytes 393224 | tf_op jit(solution)/shard_map/ppermute | solution.py:674
  16.4 11.1 %collective-permute-start.1 = (bf16[3,2,32,128]{3,2,1,0:T(8,128)(2,1)S(1)}, bf16[3,2,32,128]{3,2,1,0:T(8,128)(2,1)S(1)}, u32[]{:S(2)}, u32[]{:S(2)}) collective-permute-start(bf16[3,2,32,128]{3,2,1,0:T(8,128)(2,1)S(1)} %get-tuple-element.39), channel_id=1, source_target_pairs={{0,4},{4,8},{8,12},{12,0},{1,5},{5,9},{9,13},{13,1},{2,6},{6,10},{... | collective-permute-start | bytes 147464 | tf_op jit(solution)/shard_map/ppermute | solution.py:674
  17.0 11.5 %collective-permute-start.2 = (bf16[3,2,32,128]{3,2,1,0:T(8,128)(2,1)S(1)}, bf16[3,2,32,128]{3,2,1,0:T(8,128)(2,1)S(1)}, u32[]{:S(2)}, u32[]{:S(2)}) collective-permute-start(bf16[3,2,32,128]{3,2,1,0:T(8,128)(2,1)S(1)} %get-tuple-element.40), channel_id=1, source_target_pairs={{0,8},{4,12},{8,0},{12,4},{1,9},{5,13},{9,1},{13,5},{2,10},{6,14},... | collective-permute-start | bytes 147464 | tf_op jit(solution)/shard_map/ppermute | solution.py:674
  18.9 9.7 %collective-permute-start.3 = (bf16[3,2,32,128]{3,2,1,0:T(8,128)(2,1)S(1)}, bf16[3,2,32,128]{3,2,1,0:T(8,128)(2,1)S(1)}, u32[]{:S(2)}, u32[]{:S(2)}) collective-permute-start(bf16[3,2,32,128]{3,2,1,0:T(8,128)(2,1)S(1)} %get-tuple-element.41), channel_id=1, source_target_pairs={{0,12},{4,0},{8,4},{12,8},{1,13},{5,1},{9,5},{13,9},{2,14},{6,2},{... | collective-permute-start | bytes 147464 | tf_op jit(solution)/shard_map/ppermute | solution.py:674
  30.1 1.5 %collective-permute-start.7 = (bf16[11,4,16,128]{3,2,1,0:T(8,128)(2,1)S(1)}, bf16[11,4,16,128]{3,2,1,0:T(8,128)(2,1)S(1)}, u32[]{:S(2)}, u32[]{:S(2)}) collective-permute-start(bf16[11,4,16,128]{3,2,1,0:T(8,128)(2,1)S(1)} %get-tuple-element.48), channel_id=1, source_target_pairs={{0,1},{1,0},{2,3},{3,2},{4,5},{5,4},{6,7},{7,6},{8,9},{9,8},{10,11... | collective-permute-start | bytes 540680 | tf_op jit(solution)/shard_map/ppermute | solution.py:694
  40.3 13.4 %collective-permute-start.8 = (bf16[8,2,32,128]{3,2,1,0:T(8,128)(2,1)S(1)}, bf16[8,2,32,128]{3,2,1,0:T(8,128)(2,1)S(1)}, u32[]{:S(2)}, u32[]{:S(2)}) collective-permute-start(bf16[8,2,32,128]{3,2,1,0:T(8,128)(2,1)S(1)} %get-tuple-element.54), channel_id=1, source_target_pairs={{0,12},{4,0},{8,4},{12,8},{1,13},{5,1},{9,5},{13,9},{2,14},{6,2},{... | collective-permute-start | bytes 393224 | tf_op jit(solution)/shard_map/ppermute | solution.py:717
  46.7 11.8 %collective-permute-start.9 = (bf16[8,2,32,128]{3,2,1,0:T(8,128)(2,1)S(1)}, bf16[8,2,32,128]{3,2,1,0:T(8,128)(2,1)S(1)}, u32[]{:S(2)}, u32[]{:S(2)}) collective-permute-start(bf16[8,2,32,128]{3,2,1,0:T(8,128)(2,1)S(1)} %get-tuple-element.55), channel_id=1, source_target_pairs={{0,8},{4,12},{8,0},{12,4},{1,9},{5,13},{9,1},{13,5},{2,10},{6,14},... | collective-permute-start | bytes 393224 | tf_op jit(solution)/shard_map/ppermute | solution.py:717
  46.7 11.8 %collective-permute-start.10 = (bf16[8,2,32,128]{3,2,1,0:T(8,128)(2,1)S(1)}, bf16[8,2,32,128]{3,2,1,0:T(8,128)(2,1)S(1)}, u32[]{:S(2)}, u32[]{:S(2)}) collective-permute-start(bf16[8,2,32,128]{3,2,1,0:T(8,128)(2,1)S(1)} %get-tuple-element.56), channel_id=1, source_target_pairs={{0,4},{4,8},{8,12},{12,0},{1,5},{5,9},{9,13},{13,1},{2,6},{6,10},{... | collective-permute-start | bytes 393224 | tf_op jit(solution)/shard_map/ppermute | solution.py:717
  58.5 4.4 %collective-permute-start.13 = (f32[40,128]{1,0:T(8,128)S(1)}, f32[40,128]{1,0:T(8,128)S(1)}, u32[]{:S(2)}, u32[]{:S(2)}) collective-permute-start(f32[40,128]{1,0:T(8,128)S(1)} %shard_map.110), channel_id=1, source_target_pairs={{0,12},{4,0},{8,4},{12,8},{1,13},{5,1},{9,5},{13,9},{2,14},{6,2},{... | collective-permute-start | bytes 61448 | tf_op jit(solution)/shard_map/ppermute | solution.py:554
  59.7 5.1 %collective-permute-start.12 = (f32[40,128]{1,0:T(8,128)S(1)}, f32[40,128]{1,0:T(8,128)S(1)}, u32[]{:S(2)}, u32[]{:S(2)}) collective-permute-start(f32[40,128]{1,0:T(8,128)S(1)} %shard_map.110), channel_id=1, source_target_pairs={{0,8},{4,12},{8,0},{12,4},{1,9},{5,13},{9,1},{13,5},{2,10},{6,14},... | collective-permute-start | bytes 61448 | tf_op jit(solution)/shard_map/ppermute | solution.py:554
  60.8 5.6 %collective-permute-start.11 = (f32[40,128]{1,0:T(8,128)S(1)}, f32[40,128]{1,0:T(8,128)S(1)}, u32[]{:S(2)}, u32[]{:S(2)}) collective-permute-start(f32[40,128]{1,0:T(8,128)S(1)} %shard_map.110), channel_id=1, source_target_pairs={{0,4},{4,8},{8,12},{12,0},{1,5},{5,9},{9,13},{13,1},{2,6},{6,10},{... | collective-permute-start | bytes 61448 | tf_op jit(solution)/shard_map/ppermute | solution.py:554
  66.4 3.6 %collective-permute-start.16 = (f32[40,128]{1,0:T(8,128)S(1)}, f32[40,128]{1,0:T(8,128)S(1)}, u32[]{:S(2)}, u32[]{:S(2)}) collective-permute-start(f32[40,128]{1,0:T(8,128)S(1)} %add_add_fusion.refs_0_), channel_id=1, source_target_pairs={{0,3},{1,2},{2,1},{3,0},{4,7},{5,6},{6,5},{7,4},{8,11},{9,10},{10,... | collective-permute-start | bytes 61448 | tf_op jit(solution)/shard_map/ppermute | solution.py:566
  66.5 3.8 %collective-permute-start.15 = (f32[40,128]{1,0:T(8,128)S(1)}, f32[40,128]{1,0:T(8,128)S(1)}, u32[]{:S(2)}, u32[]{:S(2)}) collective-permute-start(f32[40,128]{1,0:T(8,128)S(1)} %add_add_fusion.refs_0_), channel_id=1, source_target_pairs={{0,2},{1,3},{2,0},{3,1},{4,6},{5,7},{6,4},{7,5},{8,10},{9,11},{10,... | collective-permute-start | bytes 61448 | tf_op jit(solution)/shard_map/ppermute | solution.py:566
  68.0 2.3 %collective-permute-start.14 = (f32[40,128]{1,0:T(8,128)S(1)}, f32[40,128]{1,0:T(8,128)S(1)}, u32[]{:S(2)}, u32[]{:S(2)}) collective-permute-start(f32[40,128]{1,0:T(8,128)S(1)} %add_add_fusion.refs_0_), channel_id=1, source_target_pairs={{0,1},{1,0},{2,3},{3,2},{4,5},{5,4},{6,7},{7,6},{8,9},{9,8},{10,11... | collective-permute-start | bytes 61448 | tf_op jit(solution)/shard_map/ppermute | solution.py:566

commit v4 on v3

--- a/solution.py
+++ b/solution.py
@@ -110,35 +110,35 @@
 
     def edges(c):
         g, e = c // p.edge_slots, c % p.edge_slots
-        both = jnp.where(older, left[g].astype(F32), right[g].astype(F32))
+        both = jnp.where(older, left[g], right[g])
         return pltpu.roll(both, LANES - EDGE - 2 * EDGE * e, 1)
 
     def group(cg, fetch, chunk, first):
         values = [fetch(cg * p.per + b) for b in range(p.per)]
         rims = [edges(cg * p.per + b) for b in range(p.per)]
         for d in range(ring):
-            total = jnp.zeros((tall, LANES), F32)
+            total = jnp.zeros((tall, LANES), BF16)
             for b in range(p.per):
                 shift = lax.rem(2 * LANES + p.block * b + EDGE - p.window * takes[d], LANES)
                 moved = pltpu.roll(jnp.where(fixes[d], rims[b], values[b]), shift, 1)
                 total = jnp.where(lane // p.block == b, moved, total)
-            stage[d] = total
+            stage[d] = total.astype(F32)
             for xp in range(p.cells_x):
                 outs[chunk * ring + d][cg - first, xp] = stage[
                     d, pl.ds(xp, p.rows, stride=p.cells_x), :
                 ].astype(BF16)
 
-    own = labels[pl.ds(pl.multiple_of(core * tall, 8), tall), :].astype(F32)
+    own = labels[pl.ds(pl.multiple_of(core * tall, 8), tall), :].astype(F32).astype(BF16)
     for chunk, (first, last) in enumerate(cuts):
         tail = last == p.groups
 
         def step(cg, carry, chunk=chunk, first=first):
-            group(cg, lambda c: field[c].astype(F32), chunk, first)
+            group(cg, lambda c: field[c], chunk, first)
             return carry
 
         lax.fori_loop(first, last - 1 if tail else last, step, 0)
         if tail:
-            group(last - 1, lambda c: field[c].astype(F32) if c < p.chans else own, chunk, first)
+            group(last - 1, lambda c: field[c] if c < p.chans else own, chunk, first)
 
 
 def cell_of(p, d, xp):
@@ -376,7 +376,7 @@
                     if j != REACH:
                         line = pltpu.roll(line, (j - REACH) % LANES, 1)
                     total = line if total is None else total + line
-                field[g, x, rows, :] = total
+                field[g, x, rows, :] = total.astype(BF16)
         return carry
 
     lax.fori_loop(0, count, step, 0)
@@ -387,7 +387,7 @@
     wide = lane_of(p.rows) // p.window
 
     def step(pack, carry):
-        totals = [jnp.zeros((p.rows, LANES), F32)] * p.xs
+        totals = [jnp.zeros((p.rows, LANES), BF16)] * p.xs
         for b in range(p.ring):
             c = pack * p.ring + b
             spot = lax.rem(b + me, p.ring)
@@ -397,7 +397,7 @@
                 totals[x] = jnp.where(wide == spot, moved, totals[x])
         for d in range(p.ring):
             for xp in range(p.cells_x):
-                results[d][pack, xp] = totals[cell_of(p, d, xp)].astype(BF16)
+                results[d][pack, xp] = totals[cell_of(p, d, xp)]
         return carry
 
     lax.fori_loop(0, packs, step, 0)
@@ -526,13 +526,13 @@
 
     def step(pack, carry, pieces, base):
         for xp in range(p.cells_x):
-            values = [pieces[d][pack, xp].astype(F32) for d in range(p.ring)]
+            values = [pieces[d][pack, xp] for d in range(p.ring)]
             for b in range(p.ring):
                 total = values[0]
                 for d in range(1, p.ring):
                     total = jnp.where(spot == lax.rem(b + me + d, p.ring), values[d], total)
                 total = pltpu.roll(total, (LANES - p.window * b) % LANES, 1) if b else total
-                stage[b, pl.ds(xp, p.rows, stride=p.cells_x), :] = total
+                stage[b, pl.ds(xp, p.rows, stride=p.cells_x), :] = total.astype(F32)
         for b in range(p.ring):
             out[(base + pack) * p.ring + b] = stage[b].astype(BF16)
         return carry
@@ -708,7 +708,7 @@
             pltpu.VMEM((classes, p.xs, p.reach_rows, LANES), F32),
             pltpu.VMEM(near_shape, F32),
             wall,
-            pltpu.VMEM((p.groups, p.xs, rows, LANES), F32),
+            pltpu.VMEM((p.groups, p.xs, rows, LANES), BF16),
             column,
         ],
         micros=5,

time: 71.2 us -> 71.1 us (level)
  no operation moved by 1% of the time
where the time goes in v4:
time: 71.1 us; the launch traced here: 70.9 us
  Pallas kernels  27.3 us (38%)
  starting transfers between devices  25 us (35%)
  waiting for transfers between devices  15.9 us (22%)
  local copies, waits for them, and re-layouts  1.9 us (3%)
  between operations  0.76 us (1%)
    pallas_call x10, Pallas kernels, call(): pl.pallas_call(body, out_shape=outs, in_specs=[*(scalars.get(i, spec) for...  27.3 us
    ppermute x6, starting transfers between devices, by_windows(): lax.ppermute(sent[d], 'gx', rotation(ring, d))  8.63 us
    ppermute x3, starting transfers between devices, by_windows(): lax.ppermute(sent[d], 'gx', rotation(ring, -d))  7.05 us
    ppermute x3, waiting for transfers between devices, by_windows(): lax.ppermute(sent[d], 'gx', rotation(ring, -d))  4.73 us
    ppermute x3, starting transfers between devices, sum_over(): lax.ppermute(value, axis, rotation(size, d))  4.35 us
    ppermute x6, waiting for transfers between devices, by_windows(): lax.ppermute(sent[d], 'gx', rotation(ring, d))  3.81 us
    ppermute x3, waiting for transfers between devices, sum_over(): lax.ppermute(value, axis, rotation(size, d))  3.56 us
    ppermute x1, starting transfers between devices, by_windows(): left = lax.ppermute(edge, 'gz', rotation(gz, 1))  2.95 us
  transfers between devices with their start and end apart: 17, of which 11 were waited for; matrix products, arithmetic and copies ran while one was open for 0% of the time, Pallas kernels for 20%

profile of v4, /device:TPU:0, one launch (start us, length us, event | category | flops | bytes accessed | tf_op | source)
XLA Modules:
  0.0 70.9 jit_solution(11919031957902322878)
XLA Ops:
  0.6 0.0 copy-start.5
  0.6 0.0 copy-start.6
  0.7 1.0 %copy-done = bf16[32,32,2,128]{3,2,1,0:T(2,128)(2,1)S(1)} copy-done((bf16[32,32,2,128]{3,2,1,0:T(2,128)(2,1)S(1)}, bf16[32,32,2,128]{3,2,1,0:T(2,128)(2,1)}, u32[]{:S(2)}) %copy-start) | copy-done | bytes 524312
  1.7 0.8 %copy-done.1 = s32[64,2,128]{2,1,0:T(2,128)S(1)} copy-done((s32[64,2,128]{2,1,0:T(2,128)S(1)}, s32[64,2,128]{2,1,0:T(2,128)}, u32[]{:S(2)}) %copy-start.1) | copy-done | bytes 65560
  2.6 0.3 shard_map.102
  2.9 3.0 %collective-permute-start = (bf16[3,64,128]{2,1,0:T(8,128)(2,1)S(1)}, bf16[3,64,128]{2,1,0:T(8,128)(2,1)S(1)}, u32[]{:S(2)}, u32[]{:S(2)}) collective-permute-start(bf16[3,64,128]{2,1,0:T(8,128)(2,1)S(1)} %shard_map.102), channel_id=1, source_target_pairs={{0,2},{2,0},{1,3},{3,1},{4,6},{6,4},{5,7},{7,5},{8,10},{10,8},{9,1... | collective-permute-start | bytes 147464 | tf_op jit(solution)/shard_map/ppermute | solution.py:638
  5.8 2.1 %collective-permute-done.left.right = bf16[3,64,128]{2,1,0:T(8,128)(2,1)S(1)} collective-permute-done((bf16[3,64,128]{2,1,0:T(8,128)(2,1)S(1)}, bf16[3,64,128]{2,1,0:T(8,128)(2,1)S(1)}, u32[]{:S(2)}, u32[]{:S(2)}) %collective-permute-start) | collective-permute-done | bytes 49184 | tf_op jit(solution)/shard_map/ppermute | solution.py:638
  7.9 2.3 %shard_map.103 = (bf16[8,2,32,128]{3,2,1,0:T(8,128)(2,1)S(1)}, bf16[8,2,32,128]{3,2,1,0:T(8,128)(2,1)S(1)}, bf16[8,2,32,128]{3,2,1,0:T(8,128)(2,1)S(1)}, bf16[8,...) custom-call(bf16[32,64,128]{2,1,0:T(8,128)(2,1)S(1)} %bitcast.6, ...), custom_call_target="tpu_custom_call" | custom-call | bytes 3000000 | tf_op jit(solution)/shard_map/pallas_call | solution.py:57
  10.2 2.2 %collective-permute-start.4 = (bf16[8,2,32,128]{3,2,1,0:T(8,128)(2,1)S(1)}, bf16[8,2,32,128]{3,2,1,0:T(8,128)(2,1)S(1)}, u32[]{:S(2)}, u32[]{:S(2)}) collective-permute-start(bf16[8,2,32,128]{3,2,1,0:T(8,128)(2,1)S(1)} %get-tuple-element.42), channel_id=1, source_target_pairs={{0,4},{4,8},{8,12},{12,0},{1,5},{5,9},{9,13},{13,1},{2,6},{6,10},{... | collective-permute-start | bytes 393224 | tf_op jit(solution)/shard_map/ppermute | solution.py:674
  12.4 2.6 %collective-permute-start.5 = (bf16[8,2,32,128]{3,2,1,0:T(8,128)(2,1)S(1)}, bf16[8,2,32,128]{3,2,1,0:T(8,128)(2,1)S(1)}, u32[]{:S(2)}, u32[]{:S(2)}) collective-permute-start(bf16[8,2,32,128]{3,2,1,0:T(8,128)(2,1)S(1)} %get-tuple-element.43), channel_id=1, source_target_pairs={{0,8},{4,12},{8,0},{12,4},{1,9},{5,13},{9,1},{13,5},{2,10},{6,14},... | collective-permute-start | bytes 393224 | tf_op jit(solution)/shard_map/ppermute | solution.py:674
  14.9 1.3 %collective-permute-start.6 = (bf16[8,2,32,128]{3,2,1,0:T(8,128)(2,1)S(1)}, bf16[8,2,32,128]{3,2,1,0:T(8,128)(2,1)S(1)}, u32[]{:S(2)}, u32[]{:S(2)}) collective-permute-start(bf16[8,2,32,128]{3,2,1,0:T(8,128)(2,1)S(1)} %get-tuple-element.44), channel_id=1, source_target_pairs={{0,12},{4,0},{8,4},{12,8},{1,13},{5,1},{9,5},{13,9},{2,14},{6,2},{... | collective-permute-start | bytes 393224 | tf_op jit(solution)/shard_map/ppermute | solution.py:674
  16.3 0.7 collective-permute-start.1
  17.0 0.3 collective-permute-start.2
  17.3 1.6 %collective-permute-done.4.refs_1_.refs_5_ = bf16[8,2,32,128]{3,2,1,0:T(8,128)(2,1)S(1)} collective-permute-done((bf16[8,2,32,128]{3,2,1,0:T(8,128)(2,1)S(1)}, bf16[8,2,32,128]{3,2,1,0:T(8,128)(2,1)S(1)}, u32[]{:S(2)}, u32[]{:S(2)}) %collective-permute-start.4) | collective-permute-done | bytes 131104 | tf_op jit(solution)/shard_map/ppermute | solution.py:674
  18.9 1.5 %collective-permute-start.3 = (bf16[3,2,32,128]{3,2,1,0:T(8,128)(2,1)S(1)}, bf16[3,2,32,128]{3,2,1,0:T(8,128)(2,1)S(1)}, u32[]{:S(2)}, u32[]{:S(2)}) collective-permute-start(bf16[3,2,32,128]{3,2,1,0:T(8,128)(2,1)S(1)} %get-tuple-element.41), channel_id=1, source_target_pairs={{0,12},{4,0},{8,4},{12,8},{1,13},{5,1},{9,5},{13,9},{2,14},{6,2},{... | collective-permute-start | bytes 147464 | tf_op jit(solution)/shard_map/ppermute | solution.py:674
  20.4 0.0 copy-done.2
  20.4 2.1 %shard_map.104 = (f32[11,40,128]{2,1,0:T(8,128)S(1)}, f32[9,40,128]{2,1,0:T(8,128)S(1)}) custom-call(f32[32,25]{1,0:T(8,128)S(1)} %copy-done.2, f32[9,32]{1,0:T(8,128)S(1)} %bitcast.9, f32[4,32]{1,0:T(4,128)S(1)} %copy-done.5, s32[64]{0:T(128)S(1)} %copy-done.6, f32[16,9]{1,0:T(8,128)S(1)} %copy-done.4, ...), custom_call_target="tpu_custom_call" | custom-call | bytes 300000 | tf_op jit(solution)/shard_map/pallas_call | solution.py:57
  22.5 1.0 %collective-permute-done.5.refs_2_.refs_6_ = bf16[8,2,32,128]{3,2,1,0:T(8,128)(2,1)S(1)} collective-permute-done((bf16[8,2,32,128]{3,2,1,0:T(8,128)(2,1)S(1)}, bf16[8,2,32,128]{3,2,1,0:T(8,128)(2,1)S(1)}, u32[]{:S(2)}, u32[]{:S(2)}) %collective-permute-start.5) | collective-permute-done | bytes 131104 | tf_op jit(solution)/shard_map/ppermute | solution.py:674
  23.5 0.1 collective-permute-done.6.refs_3_.refs_7_
  23.6 3.7 %shard_map.105 = (bf16[8,8,32,128]{3,2,1,0:T(8,128)(2,1)S(1)}, f32[8,8,40,128]{3,2,1,0:T(8,128)S(1)}, f32[8,8,40,128]{3,2,1,0:T(8,128)S(1)}, f32[4,8,40,128]{3,2,1,0:T(8,128)S(1)}, bf16[8,4,16,128]{3,2,1,0:T(8,128)(2,1)S(1)}) custom-call(f32[11,40,128]{2,1,0:T(8,128)S(1)} %get-tuple-element.36.table, f32[9,40,128]{2,1,0:T(8,128)S(1)} %get-tuple-element.37.bands, ...), custom_call_target="tpu_custom_call" | custom-call | bytes 3000 | tf_op jit(solution)/shard_map/pallas_call | solution.py:57
  27.4 0.0 collective-permute-done.1.refs_1_.refs_9_
  27.4 1.1 %collective-permute-done.2.refs_2_.refs_10_ = bf16[3,2,32,128]{3,2,1,0:T(8,128)(2,1)S(1)} collective-permute-done((bf16[3,2,32,128]{3,2,1,0:T(8,128)(2,1)S(1)}, bf16[3,2,32,128]{3,2,1,0:T(8,128)(2,1)S(1)}, u32[]{:S(2)}, u32[]{:S(2)}) %collective-permute-start.2) | collective-permute-done | bytes 49184 | tf_op jit(solution)/shard_map/ppermute | solution.py:674
  28.5 0.1 collective-permute-done.3.refs_3_.refs_11_
  28.5 1.4 %shard_map.106 = (bf16[3,8,32,128]{3,2,1,0:T(8,128)(2,1)S(1)}, f32[3,8,40,128]{3,2,1,0:T(8,128)S(1)}, f32[3,8,40,128]{3,2,1,0:T(8,128)S(1)}, f32[4,8,40,128]{3,2,1,0:T(8,128)S(1)}, bf16[11,4,16,128]{3,2,1,0:T(8,128)(2,1)S(1)}) custom-call(f32[11,40,128]{2,1,0:T(8,128)S(1)} %get-tuple-element.36.table, f32[9,40,128]{2,1,0:T(8,128)S(1)} %get-tuple-element.37.bands, ...), custom_call_target="tpu_custom_call" | custom-call | bytes 3000 | tf_op jit(solution)/shard_map/pallas_call | solution.py:57
  30.0 0.1 collective-permute-start.7
  30.1 1.4 %collective-permute-done.7.rim = bf16[11,4,16,128]{3,2,1,0:T(8,128)(2,1)S(1)} collective-permute-done((bf16[11,4,16,128]{3,2,1,0:T(8,128)(2,1)S(1)}, bf16[11,4,16,128]{3,2,1,0:T(8,128)(2,1)S(1)}, u32[]{:S(2)}, u32[]{:S(2)}) %collective-permute-start.7) | collective-permute-done | bytes 180256 | tf_op jit(solution)/shard_map/ppermute | solution.py:694
  31.5 8.7 %shard_map.107 = (bf16[8,2,32,128]{3,2,1,0:T(8,128)(2,1)S(1)}, bf16[8,2,32,128]{3,2,1,0:T(8,128)(2,1)S(1)}, bf16[8,2,32,128]{3,2,1,0:T(8,128)(2,1)S(1)}, bf16[8,...) custom-call(f32[11,40,128]{2,1,0:T(8,128)S(1)} %get-tuple-element.36, ...), custom_call_target="tpu_custom_call" | custom-call | bytes 15000000 | tf_op jit(solution)/shard_map/pallas_call | solution.py:57
  40.2 6.4 %collective-permute-start.8 = (bf16[8,2,32,128]{3,2,1,0:T(8,128)(2,1)S(1)}, bf16[8,2,32,128]{3,2,1,0:T(8,128)(2,1)S(1)}, u32[]{:S(2)}, u32[]{:S(2)}) collective-permute-start(bf16[8,2,32,128]{3,2,1,0:T(8,128)(2,1)S(1)} %get-tuple-element.54), channel_id=1, source_target_pairs={{0,12},{4,0},{8,4},{12,8},{1,13},{5,1},{9,5},{13,9},{2,14},{6,2},{... | collective-permute-start | bytes 393224 | tf_op jit(solution)/shard_map/ppermute | solution.py:717
  46.6 0.0 collective-permute-start.9
  46.6 0.6 collective-permute-start.10
  47.2 6.4 %shard_map.109.value = f32[40,128]{1,0:T(8,128)S(1)} custom-call(f32[9,40,128]{2,1,0:T(8,128)S(1)} %get-tuple-element.37.bands, f32[4,8,32,128]{3,2,1,0:T(8,128)S(1)} %get-tuple-element.57.errors, f32[11,8,8,128]{3,2,1,0:T(8,128)S(1)} %get-tuple-element.58.hidden_near, bf16[11,4,16,128]{3,2,1,0:T(8,128)(2,1)S(1)} %collective-permute-done.7.rim, ...), custom_call_target="tpu_custom_call" | custom-call | bytes 30000 | tf_op jit(solution)/shard_map/pallas_call | solution.py:57
  53.6 0.0 collective-permute-done.8.refs_1_.refs_0_
  53.6 4.7 %collective-permute-done.9.refs_2_.refs_1_ = bf16[8,2,32,128]{3,2,1,0:T(8,128)(2,1)S(1)} collective-permute-done((bf16[8,2,32,128]{3,2,1,0:T(8,128)(2,1)S(1)}, bf16[8,2,32,128]{3,2,1,0:T(8,128)(2,1)S(1)}, u32[]{:S(2)}, u32[]{:S(2)}) %collective-permute-start.9) | collective-permute-done | bytes 131104 | tf_op jit(solution)/shard_map/ppermute | solution.py:717
  58.3 0.0 collective-permute-done.10.refs_3_.refs_2_
  58.3 1.2 %collective-permute-start.13 = (f32[40,128]{1,0:T(8,128)S(1)}, f32[40,128]{1,0:T(8,128)S(1)}, u32[]{:S(2)}, u32[]{:S(2)}) collective-permute-start(f32[40,128]{1,0:T(8,128)S(1)} %shard_map.110), channel_id=1, source_target_pairs={{0,12},{4,0},{8,4},{12,8},{1,13},{5,1},{9,5},{13,9},{2,14},{6,2},{... | collective-permute-start | bytes 61448 | tf_op jit(solution)/shard_map/ppermute | solution.py:554
  59.6 1.1 %collective-permute-start.12 = (f32[40,128]{1,0:T(8,128)S(1)}, f32[40,128]{1,0:T(8,128)S(1)}, u32[]{:S(2)}, u32[]{:S(2)}) collective-permute-start(f32[40,128]{1,0:T(8,128)S(1)} %shard_map.110), channel_id=1, source_target_pairs={{0,8},{4,12},{8,0},{12,4},{1,9},{5,13},{9,1},{13,5},{2,10},{6,14},... | collective-permute-start | bytes 61448 | tf_op jit(solution)/shard_map/ppermute | solution.py:554
  60.7 2.0 %collective-permute-start.11 = (f32[40,128]{1,0:T(8,128)S(1)}, f32[40,128]{1,0:T(8,128)S(1)}, u32[]{:S(2)}, u32[]{:S(2)}) collective-permute-start(f32[40,128]{1,0:T(8,128)S(1)} %shard_map.110), channel_id=1, source_target_pairs={{0,4},{4,8},{8,12},{12,0},{1,5},{5,9},{9,13},{13,1},{2,6},{6,10},{... | collective-permute-start | bytes 61448 | tf_op jit(solution)/shard_map/ppermute | solution.py:554
  62.7 0.0 collective-permute-done.13
  62.7 2.0 %collective-permute-done.12 = f32[40,128]{1,0:T(8,128)S(1)} collective-permute-done((f32[40,128]{1,0:T(8,128)S(1)}, f32[40,128]{1,0:T(8,128)S(1)}, u32[]{:S(2)}, u32[]{:S(2)}) %collective-permute-start.12) | collective-permute-done | bytes 20512 | tf_op jit(solution)/shard_map/ppermute | solution.py:554
  64.7 1.6 %collective-permute-done.11 = f32[40,128]{1,0:T(8,128)S(1)} collective-permute-done((f32[40,128]{1,0:T(8,128)S(1)}, f32[40,128]{1,0:T(8,128)S(1)}, u32[]{:S(2)}, u32[]{:S(2)}) %collective-permute-start.11) | collective-permute-done | bytes 20512 | tf_op jit(solution)/shard_map/ppermute | solution.py:554
  66.3 0.1 collective-permute-start.16
  66.3 1.6 %collective-permute-start.15 = (f32[40,128]{1,0:T(8,128)S(1)}, f32[40,128]{1,0:T(8,128)S(1)}, u32[]{:S(2)}, u32[]{:S(2)}) collective-permute-start(f32[40,128]{1,0:T(8,128)S(1)} %add_add_fusion.refs_0_), channel_id=1, source_target_pairs={{0,2},{1,3},{2,0},{3,1},{4,6},{5,7},{6,4},{7,5},{8,10},{9,11},{10,... | collective-permute-start | bytes 61448 | tf_op jit(solution)/shard_map/ppermute | solution.py:566
  67.9 0.3 collective-permute-start.14
  68.2 1.6 %shard_map.108 = bf16[32,64,128]{2,1,0:T(8,128)(2,1)} custom-call(bf16[8,2,32,128]{3,2,1,0:T(8,128)(2,1)S(1)} %get-tuple-element.53.refs_0_, bf16[8,2,32,128]{3,2,1,0:T(8,128)(2,1)S(1)} %collective-permute-done.8.refs_1_.refs_0_, bf16[8,2,32,128]{3,2,1,0:T(8,128)(2,1)S(1)} %collective-permute-done.9.refs_2_.refs_1_, ...), custom_call_target="tpu_custom_call" | custom-call | bytes 3000000 | tf_op jit(solution)/shard_map/pallas_call | solution.py:57
  69.8 0.0 collective-permute-done.16.refs_3_
  69.8 0.4 collective-permute-done.15.refs_2_
  70.2 0.0 collective-permute-done.14.refs_1_
  70.2 0.7 shard_map.111
  (11 shorter events, 0.0 us)
Async XLA Ops:
  0.6 19.8 %copy-start.5 = (f32[4,32]{1,0:T(4,128)S(1)}, f32[4,32]{1,0:T(4,128)}, u32[]{:S(2)}) copy-start(f32[4,32]{1,0:T(4,128)} %classes.1) | copy-start | bytes 1540
  0.6 19.8 %copy-start.6 = (s32[64]{0:T(128)S(1)}, s32[64]{0:T(128)}, u32[]{:S(2)}) copy-start(s32[64]{0:T(128)} %levels.1) | copy-start | bytes 772
  0.7 1.1 %copy-start = (bf16[32,32,2,128]{3,2,1,0:T(2,128)(2,1)S(1)}, bf16[32,32,2,128]{3,2,1,0:T(2,128)(2,1)}, u32[]{:S(2)}) copy-start(bf16[32,32,2,128]{3,2,1,0:T(2,128)(2,1)} %param.7) | copy-start | bytes 1572868
  1.7 0.8 %copy-start.1 = (s32[64,2,128]{2,1,0:T(2,128)S(1)}, s32[64,2,128]{2,1,0:T(2,128)}, u32[]{:S(2)}) copy-start(s32[64,2,128]{2,1,0:T(2,128)} %param.8) | copy-start | bytes 196612
  2.5 17.9 %copy-start.2 = (f32[32,25]{1,0:T(8,128)S(1)}, f32[32,25]{1,0:T(8,128)}, u32[]{:S(2)}) copy-start(f32[32,25]{1,0:T(8,128)} %tile.1) | copy-start | bytes 9604
  2.5 17.9 %copy-start.3 = (f32[32,9]{0,1:T(8,128)S(1)}, f32[32,9]{0,1:T(8,128)}, u32[]{:S(2)}) copy-start(f32[32,9]{0,1:T(8,128)} %param.12) | copy-start | bytes 3460
  2.6 17.9 %copy-start.4 = (f32[16,9]{1,0:T(8,128)S(1)}, f32[16,9]{1,0:T(8,128)}, u32[]{:S(2)}) copy-start(f32[16,9]{1,0:T(8,128)} %stretch.1) | copy-start | bytes 1732
  2.9 5.0 %collective-permute-start = (bf16[3,64,128]{2,1,0:T(8,128)(2,1)S(1)}, bf16[3,64,128]{2,1,0:T(8,128)(2,1)S(1)}, u32[]{:S(2)}, u32[]{:S(2)}) collective-permute-start(bf16[3,64,128]{2,1,0:T(8,128)(2,1)S(1)} %shard_map.102), channel_id=1, source_target_pairs={{0,2},{2,0},{1,3},{3,1},{4,6},{6,4},{5,7},{7,5},{8,10},{10,8},{9,1... | collective-permute-start | bytes 147464 | tf_op jit(solution)/shard_map/ppermute | solution.py:638
  10.2 8.7 %collective-permute-start.4 = (bf16[8,2,32,128]{3,2,1,0:T(8,128)(2,1)S(1)}, bf16[8,2,32,128]{3,2,1,0:T(8,128)(2,1)S(1)}, u32[]{:S(2)}, u32[]{:S(2)}) collective-permute-start(bf16[8,2,32,128]{3,2,1,0:T(8,128)(2,1)S(1)} %get-tuple-element.42), channel_id=1, source_target_pairs={{0,4},{4,8},{8,12},{12,0},{1,5},{5,9},{9,13},{13,1},{2,6},{6,10},{... | collective-permute-start | bytes 393224 | tf_op jit(solution)/shard_map/ppermute | solution.py:674
  12.4 11.2 %collective-permute-start.5 = (bf16[8,2,32,128]{3,2,1,0:T(8,128)(2,1)S(1)}, bf16[8,2,32,128]{3,2,1,0:T(8,128)(2,1)S(1)}, u32[]{:S(2)}, u32[]{:S(2)}) collective-permute-start(bf16[8,2,32,128]{3,2,1,0:T(8,128)(2,1)S(1)} %get-tuple-element.43), channel_id=1, source_target_pairs={{0,8},{4,12},{8,0},{12,4},{1,9},{5,13},{9,1},{13,5},{2,10},{6,14},... | collective-permute-start | bytes 393224 | tf_op jit(solution)/shard_map/ppermute | solution.py:674
  14.9 8.7 %collective-permute-start.6 = (bf16[8,2,32,128]{3,2,1,0:T(8,128)(2,1)S(1)}, bf16[8,2,32,128]{3,2,1,0:T(8,128)(2,1)S(1)}, u32[]{:S(2)}, u32[]{:S(2)}) collective-permute-start(bf16[8,2,32,128]{3,2,1,0:T(8,128)(2,1)S(1)} %get-tuple-element.44), channel_id=1, source_target_pairs={{0,12},{4,0},{8,4},{12,8},{1,13},{5,1},{9,5},{13,9},{2,14},{6,2},{... | collective-permute-start | bytes 393224 | tf_op jit(solution)/shard_map/ppermute | solution.py:674
  16.3 11.1 %collective-permute-start.1 = (bf16[3,2,32,128]{3,2,1,0:T(8,128)(2,1)S(1)}, bf16[3,2,32,128]{3,2,1,0:T(8,128)(2,1)S(1)}, u32[]{:S(2)}, u32[]{:S(2)}) collective-permute-start(bf16[3,2,32,128]{3,2,1,0:T(8,128)(2,1)S(1)} %get-tuple-element.39), channel_id=1, source_target_pairs={{0,4},{4,8},{8,12},{12,0},{1,5},{5,9},{9,13},{13,1},{2,6},{6,10},{... | collective-permute-start | bytes 147464 | tf_op jit(solution)/shard_map/ppermute | solution.py:674
  17.0 11.5 %collective-permute-start.2 = (bf16[3,2,32,128]{3,2,1,0:T(8,128)(2,1)S(1)}, bf16[3,2,32,128]{3,2,1,0:T(8,128)(2,1)S(1)}, u32[]{:S(2)}, u32[]{:S(2)}) collective-permute-start(bf16[3,2,32,128]{3,2,1,0:T(8,128)(2,1)S(1)} %get-tuple-element.40), channel_id=1, source_target_pairs={{0,8},{4,12},{8,0},{12,4},{1,9},{5,13},{9,1},{13,5},{2,10},{6,14},... | collective-permute-start | bytes 147464 | tf_op jit(solution)/shard_map/ppermute | solution.py:674
  18.9 9.7 %collective-permute-start.3 = (bf16[3,2,32,128]{3,2,1,0:T(8,128)(2,1)S(1)}, bf16[3,2,32,128]{3,2,1,0:T(8,128)(2,1)S(1)}, u32[]{:S(2)}, u32[]{:S(2)}) collective-permute-start(bf16[3,2,32,128]{3,2,1,0:T(8,128)(2,1)S(1)} %get-tuple-element.41), channel_id=1, source_target_pairs={{0,12},{4,0},{8,4},{12,8},{1,13},{5,1},{9,5},{13,9},{2,14},{6,2},{... | collective-permute-start | bytes 147464 | tf_op jit(solution)/shard_map/ppermute | solution.py:674
  30.0 1.5 %collective-permute-start.7 = (bf16[11,4,16,128]{3,2,1,0:T(8,128)(2,1)S(1)}, bf16[11,4,16,128]{3,2,1,0:T(8,128)(2,1)S(1)}, u32[]{:S(2)}, u32[]{:S(2)}) collective-permute-start(bf16[11,4,16,128]{3,2,1,0:T(8,128)(2,1)S(1)} %get-tuple-element.48), channel_id=1, source_target_pairs={{0,1},{1,0},{2,3},{3,2},{4,5},{5,4},{6,7},{7,6},{8,9},{9,8},{10,11... | collective-permute-start | bytes 540680 | tf_op jit(solution)/shard_map/ppermute | solution.py:694
  40.2 13.4 %collective-permute-start.8 = (bf16[8,2,32,128]{3,2,1,0:T(8,128)(2,1)S(1)}, bf16[8,2,32,128]{3,2,1,0:T(8,128)(2,1)S(1)}, u32[]{:S(2)}, u32[]{:S(2)}) collective-permute-start(bf16[8,2,32,128]{3,2,1,0:T(8,128)(2,1)S(1)} %get-tuple-element.54), channel_id=1, source_target_pairs={{0,12},{4,0},{8,4},{12,8},{1,13},{5,1},{9,5},{13,9},{2,14},{6,2},{... | collective-permute-start | bytes 393224 | tf_op jit(solution)/shard_map/ppermute | solution.py:717
  46.6 11.8 %collective-permute-start.9 = (bf16[8,2,32,128]{3,2,1,0:T(8,128)(2,1)S(1)}, bf16[8,2,32,128]{3,2,1,0:T(8,128)(2,1)S(1)}, u32[]{:S(2)}, u32[]{:S(2)}) collective-permute-start(bf16[8,2,32,128]{3,2,1,0:T(8,128)(2,1)S(1)} %get-tuple-element.55), channel_id=1, source_target_pairs={{0,8},{4,12},{8,0},{12,4},{1,9},{5,13},{9,1},{13,5},{2,10},{6,14},... | collective-permute-start | bytes 393224 | tf_op jit(solution)/shard_map/ppermute | solution.py:717
  46.6 11.8 %collective-permute-start.10 = (bf16[8,2,32,128]{3,2,1,0:T(8,128)(2,1)S(1)}, bf16[8,2,32,128]{3,2,1,0:T(8,128)(2,1)S(1)}, u32[]{:S(2)}, u32[]{:S(2)}) collective-permute-start(bf16[8,2,32,128]{3,2,1,0:T(8,128)(2,1)S(1)} %get-tuple-element.56), channel_id=1, source_target_pairs={{0,4},{4,8},{8,12},{12,0},{1,5},{5,9},{9,13},{13,1},{2,6},{6,10},{... | collective-permute-start | bytes 393224 | tf_op jit(solution)/shard_map/ppermute | solution.py:717
  58.3 4.4 %collective-permute-start.13 = (f32[40,128]{1,0:T(8,128)S(1)}, f32[40,128]{1,0:T(8,128)S(1)}, u32[]{:S(2)}, u32[]{:S(2)}) collective-permute-start(f32[40,128]{1,0:T(8,128)S(1)} %shard_map.110), channel_id=1, source_target_pairs={{0,12},{4,0},{8,4},{12,8},{1,13},{5,1},{9,5},{13,9},{2,14},{6,2},{... | collective-permute-start | bytes 61448 | tf_op jit(solution)/shard_map/ppermute | solution.py:554
  59.6 5.1 %collective-permute-start.12 = (f32[40,128]{1,0:T(8,128)S(1)}, f32[40,128]{1,0:T(8,128)S(1)}, u32[]{:S(2)}, u32[]{:S(2)}) collective-permute-start(f32[40,128]{1,0:T(8,128)S(1)} %shard_map.110), channel_id=1, source_target_pairs={{0,8},{4,12},{8,0},{12,4},{1,9},{5,13},{9,1},{13,5},{2,10},{6,14},... | collective-permute-start | bytes 61448 | tf_op jit(solution)/shard_map/ppermute | solution.py:554
  60.7 5.6 %collective-permute-start.11 = (f32[40,128]{1,0:T(8,128)S(1)}, f32[40,128]{1,0:T(8,128)S(1)}, u32[]{:S(2)}, u32[]{:S(2)}) collective-permute-start(f32[40,128]{1,0:T(8,128)S(1)} %shard_map.110), channel_id=1, source_target_pairs={{0,4},{4,8},{8,12},{12,0},{1,5},{5,9},{9,13},{13,1},{2,6},{6,10},{... | collective-permute-start | bytes 61448 | tf_op jit(solution)/shard_map/ppermute | solution.py:554
  66.3 3.6 %collective-permute-start.16 = (f32[40,128]{1,0:T(8,128)S(1)}, f32[40,128]{1,0:T(8,128)S(1)}, u32[]{:S(2)}, u32[]{:S(2)}) collective-permute-start(f32[40,128]{1,0:T(8,128)S(1)} %add_add_fusion.refs_0_), channel_id=1, source_target_pairs={{0,3},{1,2},{2,1},{3,0},{4,7},{5,6},{6,5},{7,4},{8,11},{9,10},{10,... | collective-permute-start | bytes 61448 | tf_op jit(solution)/shard_map/ppermute | solution.py:566
  66.3 3.8 %collective-permute-start.15 = (f32[40,128]{1,0:T(8,128)S(1)}, f32[40,128]{1,0:T(8,128)S(1)}, u32[]{:S(2)}, u32[]{:S(2)}) collective-permute-start(f32[40,128]{1,0:T(8,128)S(1)} %add_add_fusion.refs_0_), channel_id=1, source_target_pairs={{0,2},{1,3},{2,0},{3,1},{4,6},{5,7},{6,4},{7,5},{8,10},{9,11},{10,... | collective-permute-start | bytes 61448 | tf_op jit(solution)/shard_map/ppermute | solution.py:566
  67.9 2.3 %collective-permute-start.14 = (f32[40,128]{1,0:T(8,128)S(1)}, f32[40,128]{1,0:T(8,128)S(1)}, u32[]{:S(2)}, u32[]{:S(2)}) collective-permute-start(f32[40,128]{1,0:T(8,128)S(1)} %add_add_fusion.refs_0_), channel_id=1, source_target_pairs={{0,1},{1,0},{2,3},{3,2},{4,5},{5,4},{6,7},{7,6},{8,9},{9,8},{10,11... | collective-permute-start | bytes 61448 | tf_op jit(solution)/shard_map/ppermute | solution.py:566

commit v5 on v3

--- a/solution.py
+++ b/solution.py
@@ -551,7 +551,13 @@
 
 def sum_over(value, axis):
     size = lax.axis_size(axis)
-    return sum((lax.ppermute(value, axis, rotation(size, d)) for d in range(1, size)), value)
+    if size & (size - 1):
+        return sum((lax.ppermute(value, axis, rotation(size, d)) for d in range(1, size)), value)
+    step = 1
+    while step < size:
+        value = value + lax.ppermute(value, axis, [(i, i ^ step) for i in range(size)])
+        step *= 2
+    return value
 
 
 def near_parts(value):

time: 71.2 us -> 71.7 us (level)
  waiting for transfers between devices: 15.9 us -> 18 us
  starting transfers between devices: 25 us -> 23.5 us
    ppermute x3 -> x2, waiting for transfers between devices: 3.56 us -> 5.64 us  [sum_over(): lax.ppermute(value, axis, [(i, i ^ step) for i in range(size)])]
    ppermute x3 -> x2, starting transfers between devices: 4.35 us -> 2.89 us  [sum_over(): lax.ppermute(value, axis, [(i, i ^ step) for i in range(size)])]
  transfers between devices with their start and end apart: 17 -> 16, of which waited for: 11 -> 11; matrix products, arithmetic and copies ran while one was open for 0% -> 0% of each run, Pallas kernels for 20% -> 19%
where the time goes in v5:
time: 71.7 us; the launch traced here: 71.5 us
  Pallas kernels  27.4 us (38%)
  starting transfers between devices  23.5 us (33%)
  waiting for transfers between devices  18 us (25%)
  local copies, waits for them, and re-layouts  1.9 us (3%)
  between operations  0.75 us (1%)
    pallas_call x10, Pallas kernels, call(): pl.pallas_call(body, out_shape=outs, in_specs=[*(scalars.get(i, spec) for...  27.4 us
    ppermute x6, starting transfers between devices, by_windows(): lax.ppermute(sent[d], 'gx', rotation(ring, d))  8.63 us
    ppermute x3, starting transfers between devices, by_windows(): lax.ppermute(sent[d], 'gx', rotation(ring, -d))  7.05 us
    ppermute x2, waiting for transfers between devices, sum_over(): lax.ppermute(value, axis, [(i, i ^ step) for i in range(size)])  5.64 us
    ppermute x3, waiting for transfers between devices, by_windows(): lax.ppermute(sent[d], 'gx', rotation(ring, -d))  4.73 us
    ppermute x6, waiting for transfers between devices, by_windows(): lax.ppermute(sent[d], 'gx', rotation(ring, d))  3.81 us
    ppermute x1, starting transfers between devices, by_windows(): left = lax.ppermute(edge, 'gz', rotation(gz, 1))  2.95 us
    ppermute x2, starting transfers between devices, sum_over(): lax.ppermute(value, axis, [(i, i ^ step) for i in range(size)])  2.89 us
  transfers between devices with their start and end apart: 16, of which 11 were waited for; matrix products, arithmetic and copies ran while one was open for 0% of the time, Pallas kernels for 19%

profile of v5, /device:TPU:0, one launch (start us, length us, event | category | flops | bytes accessed | tf_op | source)
XLA Modules:
  0.0 71.5 jit_solution(13897436905569527562)
XLA Ops:
  0.6 0.0 copy-start.5
  0.6 0.0 copy-start.6
  0.7 0.0 copy-start
  0.7 1.0 %copy-done = bf16[32,32,2,128]{3,2,1,0:T(2,128)(2,1)S(1)} copy-done((bf16[32,32,2,128]{3,2,1,0:T(2,128)(2,1)S(1)}, bf16[32,32,2,128]{3,2,1,0:T(2,128)(2,1)}, u32[]{:S(2)}) %copy-start) | copy-done | bytes 524312
  1.7 0.8 %copy-done.1 = s32[64,2,128]{2,1,0:T(2,128)S(1)} copy-done((s32[64,2,128]{2,1,0:T(2,128)S(1)}, s32[64,2,128]{2,1,0:T(2,128)}, u32[]{:S(2)}) %copy-start.1) | copy-done | bytes 65560
  2.6 0.3 shard_map.102
  2.9 3.0 %collective-permute-start = (bf16[3,64,128]{2,1,0:T(8,128)(2,1)S(1)}, bf16[3,64,128]{2,1,0:T(8,128)(2,1)S(1)}, u32[]{:S(2)}, u32[]{:S(2)}) collective-permute-start(bf16[3,64,128]{2,1,0:T(8,128)(2,1)S(1)} %shard_map.102), channel_id=1, source_target_pairs={{0,2},{2,0},{1,3},{3,1},{4,6},{6,4},{5,7},{7,5},{8,10},{10,8},{9,1... | collective-permute-start | bytes 147464 | tf_op jit(solution)/shard_map/ppermute | solution.py:644
  5.8 2.1 %collective-permute-done.left.right = bf16[3,64,128]{2,1,0:T(8,128)(2,1)S(1)} collective-permute-done((bf16[3,64,128]{2,1,0:T(8,128)(2,1)S(1)}, bf16[3,64,128]{2,1,0:T(8,128)(2,1)S(1)}, u32[]{:S(2)}, u32[]{:S(2)}) %collective-permute-start) | collective-permute-done | bytes 49184 | tf_op jit(solution)/shard_map/ppermute | solution.py:644
  7.9 2.3 %shard_map.103 = (bf16[8,2,32,128]{3,2,1,0:T(8,128)(2,1)S(1)}, bf16[8,2,32,128]{3,2,1,0:T(8,128)(2,1)S(1)}, bf16[8,2,32,128]{3,2,1,0:T(8,128)(2,1)S(1)}, bf16[8,...) custom-call(bf16[32,64,128]{2,1,0:T(8,128)(2,1)S(1)} %bitcast.6, ...), custom_call_target="tpu_custom_call" | custom-call | bytes 3000000 | tf_op jit(solution)/shard_map/pallas_call | solution.py:57
  10.3 2.2 %collective-permute-start.4 = (bf16[8,2,32,128]{3,2,1,0:T(8,128)(2,1)S(1)}, bf16[8,2,32,128]{3,2,1,0:T(8,128)(2,1)S(1)}, u32[]{:S(2)}, u32[]{:S(2)}) collective-permute-start(bf16[8,2,32,128]{3,2,1,0:T(8,128)(2,1)S(1)} %get-tuple-element.42), channel_id=1, source_target_pairs={{0,4},{4,8},{8,12},{12,0},{1,5},{5,9},{9,13},{13,1},{2,6},{6,10},{... | collective-permute-start | bytes 393224 | tf_op jit(solution)/shard_map/ppermute | solution.py:680
  12.4 2.6 %collective-permute-start.5 = (bf16[8,2,32,128]{3,2,1,0:T(8,128)(2,1)S(1)}, bf16[8,2,32,128]{3,2,1,0:T(8,128)(2,1)S(1)}, u32[]{:S(2)}, u32[]{:S(2)}) collective-permute-start(bf16[8,2,32,128]{3,2,1,0:T(8,128)(2,1)S(1)} %get-tuple-element.43), channel_id=1, source_target_pairs={{0,8},{4,12},{8,0},{12,4},{1,9},{5,13},{9,1},{13,5},{2,10},{6,14},... | collective-permute-start | bytes 393224 | tf_op jit(solution)/shard_map/ppermute | solution.py:680
  15.0 1.3 %collective-permute-start.6 = (bf16[8,2,32,128]{3,2,1,0:T(8,128)(2,1)S(1)}, bf16[8,2,32,128]{3,2,1,0:T(8,128)(2,1)S(1)}, u32[]{:S(2)}, u32[]{:S(2)}) collective-permute-start(bf16[8,2,32,128]{3,2,1,0:T(8,128)(2,1)S(1)} %get-tuple-element.44), channel_id=1, source_target_pairs={{0,12},{4,0},{8,4},{12,8},{1,13},{5,1},{9,5},{13,9},{2,14},{6,2},{... | collective-permute-start | bytes 393224 | tf_op jit(solution)/shard_map/ppermute | solution.py:680
  16.4 0.7 collective-permute-start.1
  17.0 0.3 collective-permute-start.2
  17.4 1.6 %collective-permute-done.4.refs_1_.refs_5_ = bf16[8,2,32,128]{3,2,1,0:T(8,128)(2,1)S(1)} collective-permute-done((bf16[8,2,32,128]{3,2,1,0:T(8,128)(2,1)S(1)}, bf16[8,2,32,128]{3,2,1,0:T(8,128)(2,1)S(1)}, u32[]{:S(2)}, u32[]{:S(2)}) %collective-permute-start.4) | collective-permute-done | bytes 131104 | tf_op jit(solution)/shard_map/ppermute | solution.py:680
  18.9 1.5 %collective-permute-start.3 = (bf16[3,2,32,128]{3,2,1,0:T(8,128)(2,1)S(1)}, bf16[3,2,32,128]{3,2,1,0:T(8,128)(2,1)S(1)}, u32[]{:S(2)}, u32[]{:S(2)}) collective-permute-start(bf16[3,2,32,128]{3,2,1,0:T(8,128)(2,1)S(1)} %get-tuple-element.41), channel_id=1, source_target_pairs={{0,12},{4,0},{8,4},{12,8},{1,13},{5,1},{9,5},{13,9},{2,14},{6,2},{... | collective-permute-start | bytes 147464 | tf_op jit(solution)/shard_map/ppermute | solution.py:680
  20.5 0.0 copy-done.5
  20.5 0.0 copy-done.4
  20.5 2.1 %shard_map.104 = (f32[11,40,128]{2,1,0:T(8,128)S(1)}, f32[9,40,128]{2,1,0:T(8,128)S(1)}) custom-call(f32[32,25]{1,0:T(8,128)S(1)} %copy-done.2, f32[9,32]{1,0:T(8,128)S(1)} %bitcast.9, f32[4,32]{1,0:T(4,128)S(1)} %copy-done.5, s32[64]{0:T(128)S(1)} %copy-done.6, f32[16,9]{1,0:T(8,128)S(1)} %copy-done.4, ...), custom_call_target="tpu_custom_call" | custom-call | bytes 300000 | tf_op jit(solution)/shard_map/pallas_call | solution.py:57
  22.6 1.0 %collective-permute-done.5.refs_2_.refs_6_ = bf16[8,2,32,128]{3,2,1,0:T(8,128)(2,1)S(1)} collective-permute-done((bf16[8,2,32,128]{3,2,1,0:T(8,128)(2,1)S(1)}, bf16[8,2,32,128]{3,2,1,0:T(8,128)(2,1)S(1)}, u32[]{:S(2)}, u32[]{:S(2)}) %collective-permute-start.5) | collective-permute-done | bytes 131104 | tf_op jit(solution)/shard_map/ppermute | solution.py:680
  23.6 0.1 collective-permute-done.6.refs_3_.refs_7_
  23.7 3.7 %shard_map.105 = (bf16[8,8,32,128]{3,2,1,0:T(8,128)(2,1)S(1)}, f32[8,8,40,128]{3,2,1,0:T(8,128)S(1)}, f32[8,8,40,128]{3,2,1,0:T(8,128)S(1)}, f32[4,8,40,128]{3,2,1,0:T(8,128)S(1)}, bf16[8,4,16,128]{3,2,1,0:T(8,128)(2,1)S(1)}) custom-call(f32[11,40,128]{2,1,0:T(8,128)S(1)} %get-tuple-element.36.table, f32[9,40,128]{2,1,0:T(8,128)S(1)} %get-tuple-element.37.bands, ...), custom_call_target="tpu_custom_call" | custom-call | bytes 3000 | tf_op jit(solution)/shard_map/pallas_call | solution.py:57
  27.4 0.0 collective-permute-done.1.refs_1_.refs_9_
  27.4 1.1 %collective-permute-done.2.refs_2_.refs_10_ = bf16[3,2,32,128]{3,2,1,0:T(8,128)(2,1)S(1)} collective-permute-done((bf16[3,2,32,128]{3,2,1,0:T(8,128)(2,1)S(1)}, bf16[3,2,32,128]{3,2,1,0:T(8,128)(2,1)S(1)}, u32[]{:S(2)}, u32[]{:S(2)}) %collective-permute-start.2) | collective-permute-done | bytes 49184 | tf_op jit(solution)/shard_map/ppermute | solution.py:680
  28.5 0.1 collective-permute-done.3.refs_3_.refs_11_
  28.6 1.4 %shard_map.106 = (bf16[3,8,32,128]{3,2,1,0:T(8,128)(2,1)S(1)}, f32[3,8,40,128]{3,2,1,0:T(8,128)S(1)}, f32[3,8,40,128]{3,2,1,0:T(8,128)S(1)}, f32[4,8,40,128]{3,2,1,0:T(8,128)S(1)}, bf16[11,4,16,128]{3,2,1,0:T(8,128)(2,1)S(1)}) custom-call(f32[11,40,128]{2,1,0:T(8,128)S(1)} %get-tuple-element.36.table, f32[9,40,128]{2,1,0:T(8,128)S(1)} %get-tuple-element.37.bands, ...), custom_call_target="tpu_custom_call" | custom-call | bytes 3000 | tf_op jit(solution)/shard_map/pallas_call | solution.py:57
  30.1 0.1 collective-permute-start.7
  30.1 1.4 %collective-permute-done.7.rim = bf16[11,4,16,128]{3,2,1,0:T(8,128)(2,1)S(1)} collective-permute-done((bf16[11,4,16,128]{3,2,1,0:T(8,128)(2,1)S(1)}, bf16[11,4,16,128]{3,2,1,0:T(8,128)(2,1)S(1)}, u32[]{:S(2)}, u32[]{:S(2)}) %collective-permute-start.7) | collective-permute-done | bytes 180256 | tf_op jit(solution)/shard_map/ppermute | solution.py:700
  31.5 8.7 %shard_map.107 = (bf16[8,2,32,128]{3,2,1,0:T(8,128)(2,1)S(1)}, bf16[8,2,32,128]{3,2,1,0:T(8,128)(2,1)S(1)}, bf16[8,2,32,128]{3,2,1,0:T(8,128)(2,1)S(1)}, bf16[8,...) custom-call(f32[11,40,128]{2,1,0:T(8,128)S(1)} %get-tuple-element.36, ...), custom_call_target="tpu_custom_call" | custom-call | bytes 15000000 | tf_op jit(solution)/shard_map/pallas_call | solution.py:57
  40.3 6.4 %collective-permute-start.8 = (bf16[8,2,32,128]{3,2,1,0:T(8,128)(2,1)S(1)}, bf16[8,2,32,128]{3,2,1,0:T(8,128)(2,1)S(1)}, u32[]{:S(2)}, u32[]{:S(2)}) collective-permute-start(bf16[8,2,32,128]{3,2,1,0:T(8,128)(2,1)S(1)} %get-tuple-element.54), channel_id=1, source_target_pairs={{0,12},{4,0},{8,4},{12,8},{1,13},{5,1},{9,5},{13,9},{2,14},{6,2},{... | collective-permute-start | bytes 393224 | tf_op jit(solution)/shard_map/ppermute | solution.py:723
  46.7 0.0 collective-permute-start.9
  46.7 0.6 collective-permute-start.10
  47.3 6.4 %shard_map.109.value = f32[40,128]{1,0:T(8,128)S(1)} custom-call(f32[9,40,128]{2,1,0:T(8,128)S(1)} %get-tuple-element.37.bands, f32[4,8,32,128]{3,2,1,0:T(8,128)S(1)} %get-tuple-element.57.errors, f32[11,8,8,128]{3,2,1,0:T(8,128)S(1)} %get-tuple-element.58.hidden_near, bf16[11,4,16,128]{3,2,1,0:T(8,128)(2,1)S(1)} %collective-permute-done.7.rim, ...), custom_call_target="tpu_custom_call" | custom-call | bytes 30000 | tf_op jit(solution)/shard_map/pallas_call | solution.py:57
  53.7 0.0 collective-permute-done.8.refs_1_.refs_0_
  53.7 4.7 %collective-permute-done.9.refs_2_.refs_1_ = bf16[8,2,32,128]{3,2,1,0:T(8,128)(2,1)S(1)} collective-permute-done((bf16[8,2,32,128]{3,2,1,0:T(8,128)(2,1)S(1)}, bf16[8,2,32,128]{3,2,1,0:T(8,128)(2,1)S(1)}, u32[]{:S(2)}, u32[]{:S(2)}) %collective-permute-start.9) | collective-permute-done | bytes 131104 | tf_op jit(solution)/shard_map/ppermute | solution.py:723
  58.5 0.0 collective-permute-done.10.refs_3_.refs_2_
  58.5 0.4 collective-permute-start.11
  58.9 3.4 %collective-permute-done.11 = f32[40,128]{1,0:T(8,128)S(1)} collective-permute-done((f32[40,128]{1,0:T(8,128)S(1)}, f32[40,128]{1,0:T(8,128)S(1)}, u32[]{:S(2)}, u32[]{:S(2)}) %collective-permute-start.11) | collective-permute-done | bytes 20512 | tf_op jit(solution)/shard_map/ppermute | solution.py:558
  62.2 2.5 %collective-permute-start.12 = (f32[40,128]{1,0:T(8,128)S(1)}, f32[40,128]{1,0:T(8,128)S(1)}, u32[]{:S(2)}, u32[]{:S(2)}) collective-permute-start(f32[40,128]{1,0:T(8,128)S(1)} %add.6), channel_id=1, source_target_pairs={{0,8},{4,12},{8,0},{12,4},{1,9},{5,13},{9,1},{13,5},{2,10},{6,14},... | collective-permute-start | bytes 61448 | tf_op jit(solution)/shard_map/ppermute | solution.py:558
  64.7 2.3 %collective-permute-done.12 = f32[40,128]{1,0:T(8,128)S(1)} collective-permute-done((f32[40,128]{1,0:T(8,128)S(1)}, f32[40,128]{1,0:T(8,128)S(1)}, u32[]{:S(2)}, u32[]{:S(2)}) %collective-permute-start.12) | collective-permute-done | bytes 20512 | tf_op jit(solution)/shard_map/ppermute | solution.py:558
  67.0 0.0 collective-permute-start.15
  67.0 1.6 %collective-permute-start.14 = (f32[40,128]{1,0:T(8,128)S(1)}, f32[40,128]{1,0:T(8,128)S(1)}, u32[]{:S(2)}, u32[]{:S(2)}) collective-permute-start(f32[40,128]{1,0:T(8,128)S(1)} %add.7.refs_0_), channel_id=1, source_target_pairs={{0,2},{1,3},{2,0},{3,1},{4,6},{5,7},{6,4},{7,5},{8,10},{9,11},{10,... | collective-permute-start | bytes 61448 | tf_op jit(solution)/shard_map/ppermute | solution.py:572
  68.6 0.3 collective-permute-start.13
  68.9 1.6 %shard_map.108 = bf16[32,64,128]{2,1,0:T(8,128)(2,1)} custom-call(bf16[8,2,32,128]{3,2,1,0:T(8,128)(2,1)S(1)} %get-tuple-element.53.refs_0_, bf16[8,2,32,128]{3,2,1,0:T(8,128)(2,1)S(1)} %collective-permute-done.8.refs_1_.refs_0_, bf16[8,2,32,128]{3,2,1,0:T(8,128)(2,1)S(1)} %collective-permute-done.9.refs_2_.refs_1_, ...), custom_call_target="tpu_custom_call" | custom-call | bytes 3000000 | tf_op jit(solution)/shard_map/pallas_call | solution.py:57
  70.5 0.0 collective-permute-done.15.refs_3_
  70.5 0.3 collective-permute-done.14.refs_2_
  70.9 0.0 collective-permute-done.13.refs_1_
  70.9 0.7 shard_map.111
  (10 shorter events, 0.0 us)
Async XLA Ops:
  0.6 19.8 %copy-start.5 = (f32[4,32]{1,0:T(4,128)S(1)}, f32[4,32]{1,0:T(4,128)}, u32[]{:S(2)}) copy-start(f32[4,32]{1,0:T(4,128)} %classes.1) | copy-start | bytes 1540
  0.6 19.8 %copy-start.6 = (s32[64]{0:T(128)S(1)}, s32[64]{0:T(128)}, u32[]{:S(2)}) copy-start(s32[64]{0:T(128)} %levels.1) | copy-start | bytes 772
  0.7 1.1 %copy-start = (bf16[32,32,2,128]{3,2,1,0:T(2,128)(2,1)S(1)}, bf16[32,32,2,128]{3,2,1,0:T(2,128)(2,1)}, u32[]{:S(2)}) copy-start(bf16[32,32,2,128]{3,2,1,0:T(2,128)(2,1)} %param.7) | copy-start | bytes 1572868
  1.7 0.8 %copy-start.1 = (s32[64,2,128]{2,1,0:T(2,128)S(1)}, s32[64,2,128]{2,1,0:T(2,128)}, u32[]{:S(2)}) copy-start(s32[64,2,128]{2,1,0:T(2,128)} %param.8) | copy-start | bytes 196612
  2.5 17.9 %copy-start.2 = (f32[32,25]{1,0:T(8,128)S(1)}, f32[32,25]{1,0:T(8,128)}, u32[]{:S(2)}) copy-start(f32[32,25]{1,0:T(8,128)} %tile.1) | copy-start | bytes 9604
  2.5 17.9 %copy-start.3 = (f32[32,9]{0,1:T(8,128)S(1)}, f32[32,9]{0,1:T(8,128)}, u32[]{:S(2)}) copy-start(f32[32,9]{0,1:T(8,128)} %param.12) | copy-start | bytes 3460
  2.6 17.9 %copy-start.4 = (f32[16,9]{1,0:T(8,128)S(1)}, f32[16,9]{1,0:T(8,128)}, u32[]{:S(2)}) copy-start(f32[16,9]{1,0:T(8,128)} %stretch.1) | copy-start | bytes 1732
  2.9 5.0 %collective-permute-start = (bf16[3,64,128]{2,1,0:T(8,128)(2,1)S(1)}, bf16[3,64,128]{2,1,0:T(8,128)(2,1)S(1)}, u32[]{:S(2)}, u32[]{:S(2)}) collective-permute-start(bf16[3,64,128]{2,1,0:T(8,128)(2,1)S(1)} %shard_map.102), channel_id=1, source_target_pairs={{0,2},{2,0},{1,3},{3,1},{4,6},{6,4},{5,7},{7,5},{8,10},{10,8},{9,1... | collective-permute-start | bytes 147464 | tf_op jit(solution)/shard_map/ppermute | solution.py:644
  10.3 8.7 %collective-permute-start.4 = (bf16[8,2,32,128]{3,2,1,0:T(8,128)(2,1)S(1)}, bf16[8,2,32,128]{3,2,1,0:T(8,128)(2,1)S(1)}, u32[]{:S(2)}, u32[]{:S(2)}) collective-permute-start(bf16[8,2,32,128]{3,2,1,0:T(8,128)(2,1)S(1)} %get-tuple-element.42), channel_id=1, source_target_pairs={{0,4},{4,8},{8,12},{12,0},{1,5},{5,9},{9,13},{13,1},{2,6},{6,10},{... | collective-permute-start | bytes 393224 | tf_op jit(solution)/shard_map/ppermute | solution.py:680
  12.4 11.2 %collective-permute-start.5 = (bf16[8,2,32,128]{3,2,1,0:T(8,128)(2,1)S(1)}, bf16[8,2,32,128]{3,2,1,0:T(8,128)(2,1)S(1)}, u32[]{:S(2)}, u32[]{:S(2)}) collective-permute-start(bf16[8,2,32,128]{3,2,1,0:T(8,128)(2,1)S(1)} %get-tuple-element.43), channel_id=1, source_target_pairs={{0,8},{4,12},{8,0},{12,4},{1,9},{5,13},{9,1},{13,5},{2,10},{6,14},... | collective-permute-start | bytes 393224 | tf_op jit(solution)/shard_map/ppermute | solution.py:680
  15.0 8.7 %collective-permute-start.6 = (bf16[8,2,32,128]{3,2,1,0:T(8,128)(2,1)S(1)}, bf16[8,2,32,128]{3,2,1,0:T(8,128)(2,1)S(1)}, u32[]{:S(2)}, u32[]{:S(2)}) collective-permute-start(bf16[8,2,32,128]{3,2,1,0:T(8,128)(2,1)S(1)} %get-tuple-element.44), channel_id=1, source_target_pairs={{0,12},{4,0},{8,4},{12,8},{1,13},{5,1},{9,5},{13,9},{2,14},{6,2},{... | collective-permute-start | bytes 393224 | tf_op jit(solution)/shard_map/ppermute | solution.py:680
  16.4 11.1 %collective-permute-start.1 = (bf16[3,2,32,128]{3,2,1,0:T(8,128)(2,1)S(1)}, bf16[3,2,32,128]{3,2,1,0:T(8,128)(2,1)S(1)}, u32[]{:S(2)}, u32[]{:S(2)}) collective-permute-start(bf16[3,2,32,128]{3,2,1,0:T(8,128)(2,1)S(1)} %get-tuple-element.39), channel_id=1, source_target_pairs={{0,4},{4,8},{8,12},{12,0},{1,5},{5,9},{9,13},{13,1},{2,6},{6,10},{... | collective-permute-start | bytes 147464 | tf_op jit(solution)/shard_map/ppermute | solution.py:680
  17.0 11.5 %collective-permute-start.2 = (bf16[3,2,32,128]{3,2,1,0:T(8,128)(2,1)S(1)}, bf16[3,2,32,128]{3,2,1,0:T(8,128)(2,1)S(1)}, u32[]{:S(2)}, u32[]{:S(2)}) collective-permute-start(bf16[3,2,32,128]{3,2,1,0:T(8,128)(2,1)S(1)} %get-tuple-element.40), channel_id=1, source_target_pairs={{0,8},{4,12},{8,0},{12,4},{1,9},{5,13},{9,1},{13,5},{2,10},{6,14},... | collective-permute-start | bytes 147464 | tf_op jit(solution)/shard_map/ppermute | solution.py:680
  18.9 9.7 %collective-permute-start.3 = (bf16[3,2,32,128]{3,2,1,0:T(8,128)(2,1)S(1)}, bf16[3,2,32,128]{3,2,1,0:T(8,128)(2,1)S(1)}, u32[]{:S(2)}, u32[]{:S(2)}) collective-permute-start(bf16[3,2,32,128]{3,2,1,0:T(8,128)(2,1)S(1)} %get-tuple-element.41), channel_id=1, source_target_pairs={{0,12},{4,0},{8,4},{12,8},{1,13},{5,1},{9,5},{13,9},{2,14},{6,2},{... | collective-permute-start | bytes 147464 | tf_op jit(solution)/shard_map/ppermute | solution.py:680
  30.1 1.5 %collective-permute-start.7 = (bf16[11,4,16,128]{3,2,1,0:T(8,128)(2,1)S(1)}, bf16[11,4,16,128]{3,2,1,0:T(8,128)(2,1)S(1)}, u32[]{:S(2)}, u32[]{:S(2)}) collective-permute-start(bf16[11,4,16,128]{3,2,1,0:T(8,128)(2,1)S(1)} %get-tuple-element.48), channel_id=1, source_target_pairs={{0,1},{1,0},{2,3},{3,2},{4,5},{5,4},{6,7},{7,6},{8,9},{9,8},{10,11... | collective-permute-start | bytes 540680 | tf_op jit(solution)/shard_map/ppermute | solution.py:700
  40.3 13.4 %collective-permute-start.8 = (bf16[8,2,32,128]{3,2,1,0:T(8,128)(2,1)S(1)}, bf16[8,2,32,128]{3,2,1,0:T(8,128)(2,1)S(1)}, u32[]{:S(2)}, u32[]{:S(2)}) collective-permute-start(bf16[8,2,32,128]{3,2,1,0:T(8,128)(2,1)S(1)} %get-tuple-element.54), channel_id=1, source_target_pairs={{0,12},{4,0},{8,4},{12,8},{1,13},{5,1},{9,5},{13,9},{2,14},{6,2},{... | collective-permute-start | bytes 393224 | tf_op jit(solution)/shard_map/ppermute | solution.py:723
  46.7 11.8 %collective-permute-start.9 = (bf16[8,2,32,128]{3,2,1,0:T(8,128)(2,1)S(1)}, bf16[8,2,32,128]{3,2,1,0:T(8,128)(2,1)S(1)}, u32[]{:S(2)}, u32[]{:S(2)}) collective-permute-start(bf16[8,2,32,128]{3,2,1,0:T(8,128)(2,1)S(1)} %get-tuple-element.55), channel_id=1, source_target_pairs={{0,8},{4,12},{8,0},{12,4},{1,9},{5,13},{9,1},{13,5},{2,10},{6,14},... | collective-permute-start | bytes 393224 | tf_op jit(solution)/shard_map/ppermute | solution.py:723
  46.7 11.8 %collective-permute-start.10 = (bf16[8,2,32,128]{3,2,1,0:T(8,128)(2,1)S(1)}, bf16[8,2,32,128]{3,2,1,0:T(8,128)(2,1)S(1)}, u32[]{:S(2)}, u32[]{:S(2)}) collective-permute-start(bf16[8,2,32,128]{3,2,1,0:T(8,128)(2,1)S(1)} %get-tuple-element.56), channel_id=1, source_target_pairs={{0,4},{4,8},{8,12},{12,0},{1,5},{5,9},{9,13},{13,1},{2,6},{6,10},{... | collective-permute-start | bytes 393224 | tf_op jit(solution)/shard_map/ppermute | solution.py:723
  58.5 3.8 %collective-permute-start.11 = (f32[40,128]{1,0:T(8,128)S(1)}, f32[40,128]{1,0:T(8,128)S(1)}, u32[]{:S(2)}, u32[]{:S(2)}) collective-permute-start(f32[40,128]{1,0:T(8,128)S(1)} %shard_map.110), channel_id=1, source_target_pairs={{0,4},{4,0},{8,12},{12,8},{1,5},{5,1},{9,13},{13,9},{2,6},{6,2},{1... | collective-permute-start | bytes 61448 | tf_op jit(solution)/shard_map/ppermute | solution.py:558
  62.2 4.7 %collective-permute-start.12 = (f32[40,128]{1,0:T(8,128)S(1)}, f32[40,128]{1,0:T(8,128)S(1)}, u32[]{:S(2)}, u32[]{:S(2)}) collective-permute-start(f32[40,128]{1,0:T(8,128)S(1)} %add.6), channel_id=1, source_target_pairs={{0,8},{4,12},{8,0},{12,4},{1,9},{5,13},{9,1},{13,5},{2,10},{6,14},... | collective-permute-start | bytes 61448 | tf_op jit(solution)/shard_map/ppermute | solution.py:558
  67.0 3.5 %collective-permute-start.15 = (f32[40,128]{1,0:T(8,128)S(1)}, f32[40,128]{1,0:T(8,128)S(1)}, u32[]{:S(2)}, u32[]{:S(2)}) collective-permute-start(f32[40,128]{1,0:T(8,128)S(1)} %add.7.refs_0_), channel_id=1, source_target_pairs={{0,3},{1,2},{2,1},{3,0},{4,7},{5,6},{6,5},{7,4},{8,11},{9,10},{10,... | collective-permute-start | bytes 61448 | tf_op jit(solution)/shard_map/ppermute | solution.py:572
  67.0 3.8 %collective-permute-start.14 = (f32[40,128]{1,0:T(8,128)S(1)}, f32[40,128]{1,0:T(8,128)S(1)}, u32[]{:S(2)}, u32[]{:S(2)}) collective-permute-start(f32[40,128]{1,0:T(8,128)S(1)} %add.7.refs_0_), channel_id=1, source_target_pairs={{0,2},{1,3},{2,0},{3,1},{4,6},{5,7},{6,4},{7,5},{8,10},{9,11},{10,... | collective-permute-start | bytes 61448 | tf_op jit(solution)/shard_map/ppermute | solution.py:572
  68.6 2.3 %collective-permute-start.13 = (f32[40,128]{1,0:T(8,128)S(1)}, f32[40,128]{1,0:T(8,128)S(1)}, u32[]{:S(2)}, u32[]{:S(2)}) collective-permute-start(f32[40,128]{1,0:T(8,128)S(1)} %add.7.refs_0_), channel_id=1, source_target_pairs={{0,1},{1,0},{2,3},{3,2},{4,5},{5,4},{6,7},{7,6},{8,9},{9,8},{10,11... | collective-permute-start | bytes 61448 | tf_op jit(solution)/shard_map/ppermute | solution.py:572

commit v6 on v3

--- a/solution.py
+++ b/solution.py
@@ -638,16 +638,15 @@
     left = lax.ppermute(edge, "gz", rotation(gz, 1))
     right = left if gz == 2 else lax.ppermute(edge, "gz", rotation(gz, -1))
 
-    windows = call(
-        functools.partial(pack_body, p, cuts),
-        [
-            jax.ShapeDtypeStruct((last - first, cells_x, rows, LANES), BF16)
-            for first, last in cuts
-            for d in range(ring)
-        ],
-        (field, marks, left, right),
-        [pltpu.VMEM((ring, tall, LANES), F32)],
-    )
+    windows = []
+    for first, last in cuts:
+        windows += call(
+            functools.partial(pack_body, p, ((first, last),)),
+            [jax.ShapeDtypeStruct((last - first, cells_x, rows, LANES), BF16)] * ring,
+            (field, marks, left, right),
+            [pltpu.VMEM((ring, tall, LANES), F32)],
+            micros=0.1,
+        )
 
     def shape(*sizes, kind=BF16):
         return jax.ShapeDtypeStruct(sizes, kind)

time: 71.2 us -> 70.5 us (level)
  waiting for transfers between devices: 15.9 us -> 14.8 us
    ppermute x6, waiting for transfers between devices: 3.81 us -> 2.67 us  [by_windows(): lax.ppermute(sent[d], 'gx', rotation(ring, d))]
    pallas_call x10 -> x11, Pallas kernels: 27.4 us -> 27.4 us  [call(): pl.pallas_call(body, out_shape=outs, in_specs=[*(scalars.get(i, spec) for...]
  transfers between devices with their start and end apart: 17 -> 17, of which waited for: 11 -> 11; matrix products, arithmetic and copies ran while one was open for 0% -> 0% of each run, Pallas kernels for 20% -> 21%
where the time goes in v6:
time: 70.5 us; the launch traced here: 70.4 us
  Pallas kernels  27.4 us (39%)
  starting transfers between devices  25.5 us (36%)
  waiting for transfers between devices  14.8 us (21%)
  local copies, waits for them, and re-layouts  1.9 us (3%)
  between operations  0.76 us (1%)
    pallas_call x11, Pallas kernels, call(): pl.pallas_call(body, out_shape=outs, in_specs=[*(scalars.get(i, spec) for...  27.4 us
    ppermute x6, starting transfers between devices, by_windows(): lax.ppermute(sent[d], 'gx', rotation(ring, d))  9.12 us
    ppermute x3, starting transfers between devices, by_windows(): lax.ppermute(sent[d], 'gx', rotation(ring, -d))  7.05 us
    ppermute x3, waiting for transfers between devices, by_windows(): lax.ppermute(sent[d], 'gx', rotation(ring, -d))  4.73 us
    ppermute x3, starting transfers between devices, sum_over(): lax.ppermute(value, axis, rotation(size, d))  4.35 us
    ppermute x3, waiting for transfers between devices, sum_over(): lax.ppermute(value, axis, rotation(size, d))  3.56 us
    ppermute x1, starting transfers between devices, by_windows(): left = lax.ppermute(edge, 'gz', rotation(gz, 1))  2.95 us
    ppermute x6, waiting for transfers between devices, by_windows(): lax.ppermute(sent[d], 'gx', rotation(ring, d))  2.67 us
  transfers between devices with their start and end apart: 17, of which 11 were waited for; matrix products, arithmetic and copies ran while one was open for 0% of the time, Pallas kernels for 21%

profile of v6, /device:TPU:0, one launch (start us, length us, event | category | flops | bytes accessed | tf_op | source)
XLA Modules:
  0.0 70.4 jit_solution(4833784687900541748)
XLA Ops:
  0.6 0.0 copy-start.5
  0.6 0.0 copy-start.6
  0.7 1.0 %copy-done = bf16[32,32,2,128]{3,2,1,0:T(2,128)(2,1)S(1)} copy-done((bf16[32,32,2,128]{3,2,1,0:T(2,128)(2,1)S(1)}, bf16[32,32,2,128]{3,2,1,0:T(2,128)(2,1)}, u32[]{:S(2)}) %copy-start) | copy-done | bytes 524312
  1.7 0.8 %copy-done.1 = s32[64,2,128]{2,1,0:T(2,128)S(1)} copy-done((s32[64,2,128]{2,1,0:T(2,128)S(1)}, s32[64,2,128]{2,1,0:T(2,128)}, u32[]{:S(2)}) %copy-start.1) | copy-done | bytes 65560
  2.6 0.3 shard_map.102
  2.9 3.0 %collective-permute-start = (bf16[3,64,128]{2,1,0:T(8,128)(2,1)S(1)}, bf16[3,64,128]{2,1,0:T(8,128)(2,1)S(1)}, u32[]{:S(2)}, u32[]{:S(2)}) collective-permute-start(bf16[3,64,128]{2,1,0:T(8,128)(2,1)S(1)} %shard_map.102), channel_id=1, source_target_pairs={{0,2},{2,0},{1,3},{3,1},{4,6},{6,4},{5,7},{7,5},{8,10},{10,8},{9,1... | collective-permute-start | bytes 147464 | tf_op jit(solution)/shard_map/ppermute | solution.py:638
  5.8 2.1 %collective-permute-done.left.right = bf16[3,64,128]{2,1,0:T(8,128)(2,1)S(1)} collective-permute-done((bf16[3,64,128]{2,1,0:T(8,128)(2,1)S(1)}, bf16[3,64,128]{2,1,0:T(8,128)(2,1)S(1)}, u32[]{:S(2)}, u32[]{:S(2)}) %collective-permute-start) | collective-permute-done | bytes 49184 | tf_op jit(solution)/shard_map/ppermute | solution.py:638
  7.9 1.7 %shard_map.103 = (bf16[8,2,32,128]{3,2,1,0:T(8,128)(2,1)S(1)}, bf16[8,2,32,128]{3,2,1,0:T(8,128)(2,1)S(1)}, bf16[8,2,32,128]{3,2,1,0:T(8,128)(2,1)S(1)}, bf16[8,2,32,128]{3,2,1,0:T(8,128)(2,1)S(1)}) custom-call(bf16[32,64,128]{2,1,0:T(8,128)(2,1)S(1)} %bitcast.6, s32[128,128]{1,0:T(8,128)S(1)} %bitcast.9, ...), custom_call_target="tpu_custom_call" | custom-call | bytes 300000 | tf_op jit(solution)/shard_map/pallas_call | solution.py:57
  9.6 2.2 %collective-permute-start.4 = (bf16[8,2,32,128]{3,2,1,0:T(8,128)(2,1)S(1)}, bf16[8,2,32,128]{3,2,1,0:T(8,128)(2,1)S(1)}, u32[]{:S(2)}, u32[]{:S(2)}) collective-permute-start(bf16[8,2,32,128]{3,2,1,0:T(8,128)(2,1)S(1)} %get-tuple-element.42), channel_id=1, source_target_pairs={{0,4},{4,8},{8,12},{12,0},{1,5},{5,9},{9,13},{13,1},{2,6},{6,10},{... | collective-permute-start | bytes 393224 | tf_op jit(solution)/shard_map/ppermute | solution.py:673
  11.8 2.6 %collective-permute-start.5 = (bf16[8,2,32,128]{3,2,1,0:T(8,128)(2,1)S(1)}, bf16[8,2,32,128]{3,2,1,0:T(8,128)(2,1)S(1)}, u32[]{:S(2)}, u32[]{:S(2)}) collective-permute-start(bf16[8,2,32,128]{3,2,1,0:T(8,128)(2,1)S(1)} %get-tuple-element.43), channel_id=1, source_target_pairs={{0,8},{4,12},{8,0},{12,4},{1,9},{5,13},{9,1},{13,5},{2,10},{6,14},... | collective-permute-start | bytes 393224 | tf_op jit(solution)/shard_map/ppermute | solution.py:673
  14.4 1.3 %collective-permute-start.6 = (bf16[8,2,32,128]{3,2,1,0:T(8,128)(2,1)S(1)}, bf16[8,2,32,128]{3,2,1,0:T(8,128)(2,1)S(1)}, u32[]{:S(2)}, u32[]{:S(2)}) collective-permute-start(bf16[8,2,32,128]{3,2,1,0:T(8,128)(2,1)S(1)} %get-tuple-element.44), channel_id=1, source_target_pairs={{0,12},{4,0},{8,4},{12,8},{1,13},{5,1},{9,5},{13,9},{2,14},{6,2},{... | collective-permute-start | bytes 393224 | tf_op jit(solution)/shard_map/ppermute | solution.py:673
  15.7 0.7 shard_map.105
  16.4 0.7 %collective-permute-start.1 = (bf16[3,2,32,128]{3,2,1,0:T(8,128)(2,1)S(1)}, bf16[3,2,32,128]{3,2,1,0:T(8,128)(2,1)S(1)}, u32[]{:S(2)}, u32[]{:S(2)}) collective-permute-start(bf16[3,2,32,128]{3,2,1,0:T(8,128)(2,1)S(1)} %get-tuple-element.39), channel_id=1, source_target_pairs={{0,4},{4,8},{8,12},{12,0},{1,5},{5,9},{9,13},{13,1},{2,6},{6,10},{... | collective-permute-start | bytes 147464 | tf_op jit(solution)/shard_map/ppermute | solution.py:673
  17.1 0.3 collective-permute-start.2
  17.4 0.9 %collective-permute-done.4.refs_1_.refs_5_ = bf16[8,2,32,128]{3,2,1,0:T(8,128)(2,1)S(1)} collective-permute-done((bf16[8,2,32,128]{3,2,1,0:T(8,128)(2,1)S(1)}, bf16[8,2,32,128]{3,2,1,0:T(8,128)(2,1)S(1)}, u32[]{:S(2)}, u32[]{:S(2)}) %collective-permute-start.4) | collective-permute-done | bytes 131104 | tf_op jit(solution)/shard_map/ppermute | solution.py:673
  18.3 2.0 %collective-permute-start.3 = (bf16[3,2,32,128]{3,2,1,0:T(8,128)(2,1)S(1)}, bf16[3,2,32,128]{3,2,1,0:T(8,128)(2,1)S(1)}, u32[]{:S(2)}, u32[]{:S(2)}) collective-permute-start(bf16[3,2,32,128]{3,2,1,0:T(8,128)(2,1)S(1)} %get-tuple-element.41), channel_id=1, source_target_pairs={{0,12},{4,0},{8,4},{12,8},{1,13},{5,1},{9,5},{13,9},{2,14},{6,2},{... | collective-permute-start | bytes 147464 | tf_op jit(solution)/shard_map/ppermute | solution.py:673
  20.3 2.1 %shard_map.104 = (f32[11,40,128]{2,1,0:T(8,128)S(1)}, f32[9,40,128]{2,1,0:T(8,128)S(1)}) custom-call(f32[32,25]{1,0:T(8,128)S(1)} %copy-done.2, f32[9,32]{1,0:T(8,128)S(1)} %bitcast.11, f32[4,32]{1,0:T(4,128)S(1)} %copy-done.5, s32[64]{0:T(128)S(1)} %copy-done.6, f32[16,9]{1,0:T(8,128)S(1)} %copy-done.4, ...), custom_call_target="tpu_custom_call" | custom-call | bytes 300000 | tf_op jit(solution)/shard_map/pallas_call | solution.py:57
  22.4 0.6 collective-permute-done.5.refs_2_.refs_6_
  23.0 0.1 collective-permute-done.6.refs_3_.refs_7_
  23.1 3.7 %shard_map.106 = (bf16[8,8,32,128]{3,2,1,0:T(8,128)(2,1)S(1)}, f32[8,8,40,128]{3,2,1,0:T(8,128)S(1)}, f32[8,8,40,128]{3,2,1,0:T(8,128)S(1)}, f32[4,8,40,128]{3,2,1,0:T(8,128)S(1)}, bf16[8,4,16,128]{3,2,1,0:T(8,128)(2,1)S(1)}) custom-call(f32[11,40,128]{2,1,0:T(8,128)S(1)} %get-tuple-element.36.table, f32[9,40,128]{2,1,0:T(8,128)S(1)} %get-tuple-element.37.bands, ...), custom_call_target="tpu_custom_call" | custom-call | bytes 3000 | tf_op jit(solution)/shard_map/pallas_call | solution.py:57
  26.8 0.0 collective-permute-done.1.refs_1_.refs_9_
  26.8 1.1 %collective-permute-done.2.refs_2_.refs_10_ = bf16[3,2,32,128]{3,2,1,0:T(8,128)(2,1)S(1)} collective-permute-done((bf16[3,2,32,128]{3,2,1,0:T(8,128)(2,1)S(1)}, bf16[3,2,32,128]{3,2,1,0:T(8,128)(2,1)S(1)}, u32[]{:S(2)}, u32[]{:S(2)}) %collective-permute-start.2) | collective-permute-done | bytes 49184 | tf_op jit(solution)/shard_map/ppermute | solution.py:673
  27.9 0.1 collective-permute-done.3.refs_3_.refs_11_
  28.0 1.4 %shard_map.107 = (bf16[3,8,32,128]{3,2,1,0:T(8,128)(2,1)S(1)}, f32[3,8,40,128]{3,2,1,0:T(8,128)S(1)}, f32[3,8,40,128]{3,2,1,0:T(8,128)S(1)}, f32[4,8,40,128]{3,2,1,0:T(8,128)S(1)}, bf16[11,4,16,128]{3,2,1,0:T(8,128)(2,1)S(1)}) custom-call(f32[11,40,128]{2,1,0:T(8,128)S(1)} %get-tuple-element.36.table, f32[9,40,128]{2,1,0:T(8,128)S(1)} %get-tuple-element.37.bands, ...), custom_call_target="tpu_custom_call" | custom-call | bytes 3000 | tf_op jit(solution)/shard_map/pallas_call | solution.py:57
  29.4 0.1 collective-permute-start.7
  29.5 1.4 %collective-permute-done.7.rim = bf16[11,4,16,128]{3,2,1,0:T(8,128)(2,1)S(1)} collective-permute-done((bf16[11,4,16,128]{3,2,1,0:T(8,128)(2,1)S(1)}, bf16[11,4,16,128]{3,2,1,0:T(8,128)(2,1)S(1)}, u32[]{:S(2)}, u32[]{:S(2)}) %collective-permute-start.7) | collective-permute-done | bytes 180256 | tf_op jit(solution)/shard_map/ppermute | solution.py:693
  30.9 8.7 %shard_map.108 = (bf16[8,2,32,128]{3,2,1,0:T(8,128)(2,1)S(1)}, bf16[8,2,32,128]{3,2,1,0:T(8,128)(2,1)S(1)}, bf16[8,2,32,128]{3,2,1,0:T(8,128)(2,1)S(1)}, bf16[8,...) custom-call(f32[11,40,128]{2,1,0:T(8,128)S(1)} %get-tuple-element.36, ...), custom_call_target="tpu_custom_call" | custom-call | bytes 15000000 | tf_op jit(solution)/shard_map/pallas_call | solution.py:57
  39.6 6.4 %collective-permute-start.8 = (bf16[8,2,32,128]{3,2,1,0:T(8,128)(2,1)S(1)}, bf16[8,2,32,128]{3,2,1,0:T(8,128)(2,1)S(1)}, u32[]{:S(2)}, u32[]{:S(2)}) collective-permute-start(bf16[8,2,32,128]{3,2,1,0:T(8,128)(2,1)S(1)} %get-tuple-element.54), channel_id=1, source_target_pairs={{0,12},{4,0},{8,4},{12,8},{1,13},{5,1},{9,5},{13,9},{2,14},{6,2},{... | collective-permute-start | bytes 393224 | tf_op jit(solution)/shard_map/ppermute | solution.py:716
  46.1 0.0 collective-permute-start.9
  46.1 0.6 collective-permute-start.10
  46.7 6.4 %shard_map.110.value = f32[40,128]{1,0:T(8,128)S(1)} custom-call(f32[9,40,128]{2,1,0:T(8,128)S(1)} %get-tuple-element.37.bands, f32[4,8,32,128]{3,2,1,0:T(8,128)S(1)} %get-tuple-element.57.errors, f32[11,8,8,128]{3,2,1,0:T(8,128)S(1)} %get-tuple-element.58.hidden_near, bf16[11,4,16,128]{3,2,1,0:T(8,128)(2,1)S(1)} %collective-permute-done.7.rim, ...), custom_call_target="tpu_custom_call" | custom-call | bytes 30000 | tf_op jit(solution)/shard_map/pallas_call | solution.py:57
  53.1 0.0 collective-permute-done.8.refs_1_.refs_0_
  53.1 4.7 %collective-permute-done.9.refs_2_.refs_1_ = bf16[8,2,32,128]{3,2,1,0:T(8,128)(2,1)S(1)} collective-permute-done((bf16[8,2,32,128]{3,2,1,0:T(8,128)(2,1)S(1)}, bf16[8,2,32,128]{3,2,1,0:T(8,128)(2,1)S(1)}, u32[]{:S(2)}, u32[]{:S(2)}) %collective-permute-start.9) | collective-permute-done | bytes 131104 | tf_op jit(solution)/shard_map/ppermute | solution.py:716
  57.8 0.0 collective-permute-done.10.refs_3_.refs_2_
  57.8 1.2 %collective-permute-start.13 = (f32[40,128]{1,0:T(8,128)S(1)}, f32[40,128]{1,0:T(8,128)S(1)}, u32[]{:S(2)}, u32[]{:S(2)}) collective-permute-start(f32[40,128]{1,0:T(8,128)S(1)} %shard_map.111), channel_id=1, source_target_pairs={{0,12},{4,0},{8,4},{12,8},{1,13},{5,1},{9,5},{13,9},{2,14},{6,2},{... | collective-permute-start | bytes 61448 | tf_op jit(solution)/shard_map/ppermute | solution.py:554
  59.0 1.1 %collective-permute-start.12 = (f32[40,128]{1,0:T(8,128)S(1)}, f32[40,128]{1,0:T(8,128)S(1)}, u32[]{:S(2)}, u32[]{:S(2)}) collective-permute-start(f32[40,128]{1,0:T(8,128)S(1)} %shard_map.111), channel_id=1, source_target_pairs={{0,8},{4,12},{8,0},{12,4},{1,9},{5,13},{9,1},{13,5},{2,10},{6,14},... | collective-permute-start | bytes 61448 | tf_op jit(solution)/shard_map/ppermute | solution.py:554
  60.1 2.0 %collective-permute-start.11 = (f32[40,128]{1,0:T(8,128)S(1)}, f32[40,128]{1,0:T(8,128)S(1)}, u32[]{:S(2)}, u32[]{:S(2)}) collective-permute-start(f32[40,128]{1,0:T(8,128)S(1)} %shard_map.111), channel_id=1, source_target_pairs={{0,4},{4,8},{8,12},{12,0},{1,5},{5,9},{9,13},{13,1},{2,6},{6,10},{... | collective-permute-start | bytes 61448 | tf_op jit(solution)/shard_map/ppermute | solution.py:554
  62.2 0.0 collective-permute-done.13
  62.2 2.0 %collective-permute-done.12 = f32[40,128]{1,0:T(8,128)S(1)} collective-permute-done((f32[40,128]{1,0:T(8,128)S(1)}, f32[40,128]{1,0:T(8,128)S(1)}, u32[]{:S(2)}, u32[]{:S(2)}) %collective-permute-start.12) | collective-permute-done | bytes 20512 | tf_op jit(solution)/shard_map/ppermute | solution.py:554
  64.1 1.6 %collective-permute-done.11 = f32[40,128]{1,0:T(8,128)S(1)} collective-permute-done((f32[40,128]{1,0:T(8,128)S(1)}, f32[40,128]{1,0:T(8,128)S(1)}, u32[]{:S(2)}, u32[]{:S(2)}) %collective-permute-start.11) | collective-permute-done | bytes 20512 | tf_op jit(solution)/shard_map/ppermute | solution.py:554
  65.7 0.1 collective-permute-start.16
  65.8 1.6 %collective-permute-start.15 = (f32[40,128]{1,0:T(8,128)S(1)}, f32[40,128]{1,0:T(8,128)S(1)}, u32[]{:S(2)}, u32[]{:S(2)}) collective-permute-start(f32[40,128]{1,0:T(8,128)S(1)} %add_add_fusion.refs_0_), channel_id=1, source_target_pairs={{0,2},{1,3},{2,0},{3,1},{4,6},{5,7},{6,4},{7,5},{8,10},{9,11},{10,... | collective-permute-start | bytes 61448 | tf_op jit(solution)/shard_map/ppermute | solution.py:566
  67.4 0.3 collective-permute-start.14
  67.7 1.6 %shard_map.109 = bf16[32,64,128]{2,1,0:T(8,128)(2,1)} custom-call(bf16[8,2,32,128]{3,2,1,0:T(8,128)(2,1)S(1)} %get-tuple-element.53.refs_0_, bf16[8,2,32,128]{3,2,1,0:T(8,128)(2,1)S(1)} %collective-permute-done.8.refs_1_.refs_0_, bf16[8,2,32,128]{3,2,1,0:T(8,128)(2,1)S(1)} %collective-permute-done.9.refs_2_.refs_1_, ...), custom_call_target="tpu_custom_call" | custom-call | bytes 3000000 | tf_op jit(solution)/shard_map/pallas_call | solution.py:57
  69.3 0.0 collective-permute-done.16.refs_3_
  69.3 0.4 collective-permute-done.15.refs_2_
  69.7 0.0 collective-permute-done.14.refs_1_
  69.7 0.7 shard_map.112
  (12 shorter events, 0.0 us)
Async XLA Ops:
  0.6 19.6 %copy-start.5 = (f32[4,32]{1,0:T(4,128)S(1)}, f32[4,32]{1,0:T(4,128)}, u32[]{:S(2)}) copy-start(f32[4,32]{1,0:T(4,128)} %classes.1) | copy-start | bytes 1540
  0.6 19.6 %copy-start.6 = (s32[64]{0:T(128)S(1)}, s32[64]{0:T(128)}, u32[]{:S(2)}) copy-start(s32[64]{0:T(128)} %levels.1) | copy-start | bytes 772
  0.7 1.1 %copy-start = (bf16[32,32,2,128]{3,2,1,0:T(2,128)(2,1)S(1)}, bf16[32,32,2,128]{3,2,1,0:T(2,128)(2,1)}, u32[]{:S(2)}) copy-start(bf16[32,32,2,128]{3,2,1,0:T(2,128)(2,1)} %param.7) | copy-start | bytes 1572868
  1.7 0.8 %copy-start.1 = (s32[64,2,128]{2,1,0:T(2,128)S(1)}, s32[64,2,128]{2,1,0:T(2,128)}, u32[]{:S(2)}) copy-start(s32[64,2,128]{2,1,0:T(2,128)} %param.8) | copy-start | bytes 196612
  2.5 17.7 %copy-start.2 = (f32[32,25]{1,0:T(8,128)S(1)}, f32[32,25]{1,0:T(8,128)}, u32[]{:S(2)}) copy-start(f32[32,25]{1,0:T(8,128)} %tile.1) | copy-start | bytes 9604
  2.5 17.7 %copy-start.3 = (f32[32,9]{0,1:T(8,128)S(1)}, f32[32,9]{0,1:T(8,128)}, u32[]{:S(2)}) copy-start(f32[32,9]{0,1:T(8,128)} %param.12) | copy-start | bytes 3460
  2.6 17.7 %copy-start.4 = (f32[16,9]{1,0:T(8,128)S(1)}, f32[16,9]{1,0:T(8,128)}, u32[]{:S(2)}) copy-start(f32[16,9]{1,0:T(8,128)} %stretch.1) | copy-start | bytes 1732
  2.9 5.0 %collective-permute-start = (bf16[3,64,128]{2,1,0:T(8,128)(2,1)S(1)}, bf16[3,64,128]{2,1,0:T(8,128)(2,1)S(1)}, u32[]{:S(2)}, u32[]{:S(2)}) collective-permute-start(bf16[3,64,128]{2,1,0:T(8,128)(2,1)S(1)} %shard_map.102), channel_id=1, source_target_pairs={{0,2},{2,0},{1,3},{3,1},{4,6},{6,4},{5,7},{7,5},{8,10},{10,8},{9,1... | collective-permute-start | bytes 147464 | tf_op jit(solution)/shard_map/ppermute | solution.py:638
  9.6 8.7 %collective-permute-start.4 = (bf16[8,2,32,128]{3,2,1,0:T(8,128)(2,1)S(1)}, bf16[8,2,32,128]{3,2,1,0:T(8,128)(2,1)S(1)}, u32[]{:S(2)}, u32[]{:S(2)}) collective-permute-start(bf16[8,2,32,128]{3,2,1,0:T(8,128)(2,1)S(1)} %get-tuple-element.42), channel_id=1, source_target_pairs={{0,4},{4,8},{8,12},{12,0},{1,5},{5,9},{9,13},{13,1},{2,6},{6,10},{... | collective-permute-start | bytes 393224 | tf_op jit(solution)/shard_map/ppermute | solution.py:673
  11.8 11.2 %collective-permute-start.5 = (bf16[8,2,32,128]{3,2,1,0:T(8,128)(2,1)S(1)}, bf16[8,2,32,128]{3,2,1,0:T(8,128)(2,1)S(1)}, u32[]{:S(2)}, u32[]{:S(2)}) collective-permute-start(bf16[8,2,32,128]{3,2,1,0:T(8,128)(2,1)S(1)} %get-tuple-element.43), channel_id=1, source_target_pairs={{0,8},{4,12},{8,0},{12,4},{1,9},{5,13},{9,1},{13,5},{2,10},{6,14},... | collective-permute-start | bytes 393224 | tf_op jit(solution)/shard_map/ppermute | solution.py:673
  14.4 8.7 %collective-permute-start.6 = (bf16[8,2,32,128]{3,2,1,0:T(8,128)(2,1)S(1)}, bf16[8,2,32,128]{3,2,1,0:T(8,128)(2,1)S(1)}, u32[]{:S(2)}, u32[]{:S(2)}) collective-permute-start(bf16[8,2,32,128]{3,2,1,0:T(8,128)(2,1)S(1)} %get-tuple-element.44), channel_id=1, source_target_pairs={{0,12},{4,0},{8,4},{12,8},{1,13},{5,1},{9,5},{13,9},{2,14},{6,2},{... | collective-permute-start | bytes 393224 | tf_op jit(solution)/shard_map/ppermute | solution.py:673
  16.4 10.4 %collective-permute-start.1 = (bf16[3,2,32,128]{3,2,1,0:T(8,128)(2,1)S(1)}, bf16[3,2,32,128]{3,2,1,0:T(8,128)(2,1)S(1)}, u32[]{:S(2)}, u32[]{:S(2)}) collective-permute-start(bf16[3,2,32,128]{3,2,1,0:T(8,128)(2,1)S(1)} %get-tuple-element.39), channel_id=1, source_target_pairs={{0,4},{4,8},{8,12},{12,0},{1,5},{5,9},{9,13},{13,1},{2,6},{6,10},{... | collective-permute-start | bytes 147464 | tf_op jit(solution)/shard_map/ppermute | solution.py:673
  17.1 10.8 %collective-permute-start.2 = (bf16[3,2,32,128]{3,2,1,0:T(8,128)(2,1)S(1)}, bf16[3,2,32,128]{3,2,1,0:T(8,128)(2,1)S(1)}, u32[]{:S(2)}, u32[]{:S(2)}) collective-permute-start(bf16[3,2,32,128]{3,2,1,0:T(8,128)(2,1)S(1)} %get-tuple-element.40), channel_id=1, source_target_pairs={{0,8},{4,12},{8,0},{12,4},{1,9},{5,13},{9,1},{13,5},{2,10},{6,14},... | collective-permute-start | bytes 147464 | tf_op jit(solution)/shard_map/ppermute | solution.py:673
  18.3 9.7 %collective-permute-start.3 = (bf16[3,2,32,128]{3,2,1,0:T(8,128)(2,1)S(1)}, bf16[3,2,32,128]{3,2,1,0:T(8,128)(2,1)S(1)}, u32[]{:S(2)}, u32[]{:S(2)}) collective-permute-start(bf16[3,2,32,128]{3,2,1,0:T(8,128)(2,1)S(1)} %get-tuple-element.41), channel_id=1, source_target_pairs={{0,12},{4,0},{8,4},{12,8},{1,13},{5,1},{9,5},{13,9},{2,14},{6,2},{... | collective-permute-start | bytes 147464 | tf_op jit(solution)/shard_map/ppermute | solution.py:673
  29.4 1.5 %collective-permute-start.7 = (bf16[11,4,16,128]{3,2,1,0:T(8,128)(2,1)S(1)}, bf16[11,4,16,128]{3,2,1,0:T(8,128)(2,1)S(1)}, u32[]{:S(2)}, u32[]{:S(2)}) collective-permute-start(bf16[11,4,16,128]{3,2,1,0:T(8,128)(2,1)S(1)} %get-tuple-element.48), channel_id=1, source_target_pairs={{0,1},{1,0},{2,3},{3,2},{4,5},{5,4},{6,7},{7,6},{8,9},{9,8},{10,11... | collective-permute-start | bytes 540680 | tf_op jit(solution)/shard_map/ppermute | solution.py:693
  39.6 13.4 %collective-permute-start.8 = (bf16[8,2,32,128]{3,2,1,0:T(8,128)(2,1)S(1)}, bf16[8,2,32,128]{3,2,1,0:T(8,128)(2,1)S(1)}, u32[]{:S(2)}, u32[]{:S(2)}) collective-permute-start(bf16[8,2,32,128]{3,2,1,0:T(8,128)(2,1)S(1)} %get-tuple-element.54), channel_id=1, source_target_pairs={{0,12},{4,0},{8,4},{12,8},{1,13},{5,1},{9,5},{13,9},{2,14},{6,2},{... | collective-permute-start | bytes 393224 | tf_op jit(solution)/shard_map/ppermute | solution.py:716
  46.1 11.8 %collective-permute-start.9 = (bf16[8,2,32,128]{3,2,1,0:T(8,128)(2,1)S(1)}, bf16[8,2,32,128]{3,2,1,0:T(8,128)(2,1)S(1)}, u32[]{:S(2)}, u32[]{:S(2)}) collective-permute-start(bf16[8,2,32,128]{3,2,1,0:T(8,128)(2,1)S(1)} %get-tuple-element.55), channel_id=1, source_target_pairs={{0,8},{4,12},{8,0},{12,4},{1,9},{5,13},{9,1},{13,5},{2,10},{6,14},... | collective-permute-start | bytes 393224 | tf_op jit(solution)/shard_map/ppermute | solution.py:716
  46.1 11.8 %collective-permute-start.10 = (bf16[8,2,32,128]{3,2,1,0:T(8,128)(2,1)S(1)}, bf16[8,2,32,128]{3,2,1,0:T(8,128)(2,1)S(1)}, u32[]{:S(2)}, u32[]{:S(2)}) collective-permute-start(bf16[8,2,32,128]{3,2,1,0:T(8,128)(2,1)S(1)} %get-tuple-element.56), channel_id=1, source_target_pairs={{0,4},{4,8},{8,12},{12,0},{1,5},{5,9},{9,13},{13,1},{2,6},{6,10},{... | collective-permute-start | bytes 393224 | tf_op jit(solution)/shard_map/ppermute | solution.py:716
  57.8 4.4 %collective-permute-start.13 = (f32[40,128]{1,0:T(8,128)S(1)}, f32[40,128]{1,0:T(8,128)S(1)}, u32[]{:S(2)}, u32[]{:S(2)}) collective-permute-start(f32[40,128]{1,0:T(8,128)S(1)} %shard_map.111), channel_id=1, source_target_pairs={{0,12},{4,0},{8,4},{12,8},{1,13},{5,1},{9,5},{13,9},{2,14},{6,2},{... | collective-permute-start | bytes 61448 | tf_op jit(solution)/shard_map/ppermute | solution.py:554
  59.0 5.1 %collective-permute-start.12 = (f32[40,128]{1,0:T(8,128)S(1)}, f32[40,128]{1,0:T(8,128)S(1)}, u32[]{:S(2)}, u32[]{:S(2)}) collective-permute-start(f32[40,128]{1,0:T(8,128)S(1)} %shard_map.111), channel_id=1, source_target_pairs={{0,8},{4,12},{8,0},{12,4},{1,9},{5,13},{9,1},{13,5},{2,10},{6,14},... | collective-permute-start | bytes 61448 | tf_op jit(solution)/shard_map/ppermute | solution.py:554
  60.1 5.6 %collective-permute-start.11 = (f32[40,128]{1,0:T(8,128)S(1)}, f32[40,128]{1,0:T(8,128)S(1)}, u32[]{:S(2)}, u32[]{:S(2)}) collective-permute-start(f32[40,128]{1,0:T(8,128)S(1)} %shard_map.111), channel_id=1, source_target_pairs={{0,4},{4,8},{8,12},{12,0},{1,5},{5,9},{9,13},{13,1},{2,6},{6,10},{... | collective-permute-start | bytes 61448 | tf_op jit(solution)/shard_map/ppermute | solution.py:554
  65.7 3.6 %collective-permute-start.16 = (f32[40,128]{1,0:T(8,128)S(1)}, f32[40,128]{1,0:T(8,128)S(1)}, u32[]{:S(2)}, u32[]{:S(2)}) collective-permute-start(f32[40,128]{1,0:T(8,128)S(1)} %add_add_fusion.refs_0_), channel_id=1, source_target_pairs={{0,3},{1,2},{2,1},{3,0},{4,7},{5,6},{6,5},{7,4},{8,11},{9,10},{10,... | collective-permute-start | bytes 61448 | tf_op jit(solution)/shard_map/ppermute | solution.py:566
  65.8 3.8 %collective-permute-start.15 = (f32[40,128]{1,0:T(8,128)S(1)}, f32[40,128]{1,0:T(8,128)S(1)}, u32[]{:S(2)}, u32[]{:S(2)}) collective-permute-start(f32[40,128]{1,0:T(8,128)S(1)} %add_add_fusion.refs_0_), channel_id=1, source_target_pairs={{0,2},{1,3},{2,0},{3,1},{4,6},{5,7},{6,4},{7,5},{8,10},{9,11},{10,... | collective-permute-start | bytes 61448 | tf_op jit(solution)/shard_map/ppermute | solution.py:566
  67.4 2.3 %collective-permute-start.14 = (f32[40,128]{1,0:T(8,128)S(1)}, f32[40,128]{1,0:T(8,128)S(1)}, u32[]{:S(2)}, u32[]{:S(2)}) collective-permute-start(f32[40,128]{1,0:T(8,128)S(1)} %add_add_fusion.refs_0_), channel_id=1, source_target_pairs={{0,1},{1,0},{2,3},{3,2},{4,5},{5,4},{6,7},{7,6},{8,9},{9,8},{10,11... | collective-permute-start | bytes 61448 | tf_op jit(solution)/shard_map/ppermute | solution.py:566
